TPU v7x, 256 devices: a whole 4x4x8 slice. The times are simulated.
256 devices in a mesh: date: 128 (over x_lo, z, y, core), row: 2 (over x_hi).
Axes of the slice: x: 4 (x_hi: 2, x_lo: 2; x = x_hi * 2 + x_lo), y: 4, z: 8, core: 2. Of those that a mesh axis runs over, the one named last changes fastest.
Arguments:
- slc: bfloat16 [128, 2, 160, 2560], P('date', None, 'row'), may hold values from -6 to 6
- coarse: int32 [128, 2], P('date'), may hold values from -8 to 8, as said below
- fraction: int32 [128, 2], P('date'), may hold values from 0 to 63
- pair_on: int32 [128, 3], P('date'), may hold values 0 or 1
- ref_date: int32 [1], replicated, may hold values from 0 to 127
Outputs:
- ref_ifg: float32 [128, 2, 32, 128], P('date', None, 'row')
- pair_ifg: float32 [128, 3, 2, 32, 128], P('date', None, None, 'row')
- coherence: float32 [128, 3, 32, 128], P('date', None, 'row')
Inputs may be any that keep to these rules, and one draw needn't show every extreme that they name: `coarse`: some date has row offset 8 and some other date row offset -8.
All inputs are finite; a program needn't handle non-finite values. No bound on the sum of `pair_on` on one device may be relied on, other than what follows from the above.
Results may differ from a plain program's by a relative error of at most 0.0075.
Values may be sent and summed in bfloat16 or wider, within the bound.
No kernel may reach another device: no remote copies, remote signals or barrier semaphores. Data moves between devices by JAX's collectives and lax.ppermute only.
A program may use at most 64 MiB of HBM per device.

v0:
```python
import jax
import jax.numpy as jnp
from jax import lax
from jax.sharding import PartitionSpec as P

NFRAC = 64
SPAN = 3
LOOK_R = 5
LOOK_C = 20
HALO = 12


col_margin = 64
epsilon = 1e-06


def extended_2(block, sides, width):
    for axis, dim in sides:
        count = lax.axis_size(axis)
        forward = [(i, i + 1) for i in range(count - 1)]
        backward = [(target, source) for source, target in forward]
        low = lax.ppermute(
            lax.slice_in_dim(block, block.shape[dim] - width, None, axis=dim), axis, forward
        )
        high = lax.ppermute(lax.slice_in_dim(block, 0, width, axis=dim), axis, backward)
        block = jnp.concatenate([low, block, high], axis=dim)
    return block


def broadcast(value, axis, source):
    kept = jnp.where(lax.axis_index(axis) == source, value, 0).astype(value.dtype)
    return lax.psum(kept, axis)


def shifted(shard, axis, by):
    peers = lax.axis_size(axis)
    pairs = [(i, i + by) for i in range(peers) if 0 <= i + by < peers]
    return lax.ppermute(shard, axis, pairs)


def filter_taps(index):
    position = jnp.arange(8, dtype=jnp.float32) - 3.0 - index.astype(jnp.float32) / NFRAC
    weights = jnp.sinc(position) * (0.54 + 0.46 * jnp.cos(jnp.pi * position / 4.0))
    return (weights / jnp.sum(weights)).astype(jnp.bfloat16)


def multilook(values):
    row_count, col_count = (values.shape[-2], values.shape[-1])
    shaped = values.reshape(
        values.shape[:-2] + (row_count // LOOK_R, LOOK_R, col_count // LOOK_C, LOOK_C)
    )
    return jnp.mean(shaped, axis=(-3, -1))


def band_matrix(out_count, in_count, shift, taps):
    target = jnp.arange(out_count, dtype=jnp.int32)[:, None]
    source = jnp.arange(in_count, dtype=jnp.int32)[None, :]
    distance = source - target - shift
    selector = distance[:, :, None] == jnp.arange(8, dtype=jnp.int32)[None, None, :]
    return jnp.sum(jnp.where(selector, taps, jnp.zeros((), jnp.bfloat16)), axis=-1)


def pair_terms(first, second):
    z_real, z_imag = (first[0].astype(jnp.float32), first[1].astype(jnp.float32))
    v_real, v_imag = (second[0].astype(jnp.float32), second[1].astype(jnp.float32))
    real_part = multilook(z_real * v_real + z_imag * v_imag)
    imag_part = multilook(z_imag * v_real - z_real * v_imag)
    power_one = multilook(z_real * z_real + z_imag * z_imag)
    power_two = multilook(v_real * v_real + v_imag * v_imag)
    coherent = jnp.sqrt(real_part * real_part + imag_part * imag_part) / (
        jnp.sqrt(power_one + epsilon) * jnp.sqrt(power_two + epsilon)
    )
    return (jnp.stack([real_part, imag_part]), coherent)


def with_reference(image, ref_image):
    z_real, z_imag = (image[0].astype(jnp.float32), image[1].astype(jnp.float32))
    ref_real, ref_imag = (ref_image[0].astype(jnp.float32), ref_image[1].astype(jnp.float32))
    real_part = multilook(z_real * ref_real + z_imag * ref_imag)
    imag_part = multilook(z_imag * ref_real - z_real * ref_imag)
    return jnp.stack([real_part, imag_part])


def on_device(slc, coarse, fraction, pair_on, ref_date):
    own_tile = slc[0]
    row_count = own_tile.shape[1]
    col_count = own_tile.shape[2]
    row_taps = filter_taps(fraction[0, 0])
    col_taps = filter_taps(fraction[0, 1])
    extended = extended_2(own_tile, (("row", 1),), HALO)
    row_matrix = band_matrix(row_count, row_count + 2 * HALO, HALO + coarse[0, 0] - 3, row_taps)
    rowfit = jnp.einsum(
        "rj,pjc->prc", row_matrix, extended, preferred_element_type=jnp.float32
    ).astype(jnp.bfloat16)
    padded = jnp.pad(rowfit, ((0, 0), (0, 0), (col_margin, col_margin)))
    col_block = 512
    col_matrix = band_matrix(
        col_block, col_block + 2 * col_margin, col_margin + coarse[0, 1] - 3, col_taps
    ).T
    outputs = []
    for start in range(0, col_count, col_block):
        slab = padded[:, :, start : start + col_block + 2 * col_margin]
        outputs.append(
            jnp.einsum("prj,jc->prc", slab, col_matrix, preferred_element_type=jnp.float32)
        )
    resampled = jnp.concatenate(outputs, axis=2).astype(jnp.bfloat16)
    ref_owner = ref_date[0]
    received = broadcast(own_tile, "date", ref_owner)
    ref_ifg = with_reference(resampled, received)
    date_index = lax.axis_index("date")
    date_count = lax.axis_size("date")
    ifg_list, coh_list = ([], [])
    partner_image = resampled
    for s in range(SPAN):
        partner_image = shifted(resampled, "date", -(s + 1))
        usable = jnp.logical_and(date_index + s + 1 < date_count, pair_on[0, s] == 1)
        ifg, coherent = pair_terms(resampled, partner_image)
        ifg_list.append(jnp.where(usable, ifg, 0.0))
        coh_list.append(jnp.where(usable, coherent, 0.0))
    pair_ifg = jnp.stack(ifg_list)[None]
    coherence = jnp.stack(coh_list)[None]
    return (ref_ifg[None], pair_ifg, coherence)


def solution(mesh):
    return jax.shard_map(
        on_device,
        mesh=mesh,
        in_specs=(
            P("date", None, "row", None),
            P("date", None),
            P("date", None),
            P("date", None),
            P(),
        ),
        out_specs=(
            P("date", None, "row", None),
            P("date", None, None, "row", None),
            P("date", None, "row", None),
        ),
        check_vma=False,
    )
```

profile of v0, /device:TPU:1, one launch (start us, length us, event | category | flops | bytes accessed | tf_op | source)
XLA Modules:
  0.0 1210.0 jit_solution(234106864880249260)
XLA Ops:
  8.0 2.1 broadcast_select_fusion
  10.2 1.3 collective-permute-start.1
  11.5 5.5 collective-permute-start
  17.0 0.6 fusion.54
  18.4 0.6 fusion.53
  19.6 0.6 fusion.46
  20.2 0.6 divide_convert_fusion
  22.1 0.7 fusion.47
  22.8 0.7 divide_convert_fusion.1
  23.5 0.6 fusion.52
  26.0 3.7 fusion.1
  30.0 0.5 fusion.2
  30.5 0.4 fusion.7
  31.6 0.4 fusion.4
  32.4 5.7 collective-permute-start.2
  38.1 1.3 collective-permute-start.3
  39.4 1.3 collective-permute-start.4
  40.7 1022.4 %all-reduce.3.cloned.1.call-done = bf16[2,80,2560]{2,1,0:T(8,128)(2,1)} async-done(((bf16[2,80,2560]{2,1,0:T(8,128)(2,1)}), bf16[2,80,2560]{2,1,0:T(8,128)(2,1)}) %all-reduce.3.cloned.1.call-update) | async-done | bytes 819216 | tf_op jit(solution)/shard_map/psum | solution.py:32
  1063.1 2.3 fusion.16
  1065.4 8.1 sub.152
  1073.5 7.7 add.235
  1081.2 2.9 reduce_sum.163
  1084.1 2.9 reduce_sum.162
  1087.0 0.6 maximum_bitcast_fusion.2
  1087.6 2.9 fusion.18
  1090.6 8.1 add.250
  1098.7 2.9 reduce_sum.171
  1101.6 8.1 sub.154
  1109.6 2.9 reduce_sum.165
  1112.5 8.1 add.238
  1120.6 2.9 reduce_sum.164
  1123.5 7.7 add.247
  1131.2 2.9 reduce_sum.170
  1134.1 3.4 fusion.20
  1137.5 8.1 add.254
  1145.6 3.0 reduce_sum.172
  1148.6 7.7 sub.156
  1156.2 3.0 reduce_sum.167
  1159.2 7.7 add.241
  1166.9 2.9 reduce_sum.166
  1170.0 7.7 add.258
  1177.6 3.0 reduce_sum.173
  1180.6 7.7 sub.158
  1188.3 2.9 reduce_sum.169
  1191.2 7.7 add.244
  1198.9 2.9 reduce_sum.168
  1201.9 0.6 maximum_bitcast_fusion
  1202.5 0.6 maximum_bitcast_fusion.1
  (33 shorter events, 1.8 us)
Async XLA Ops:
  7.2 2.9 copy-start.3
  7.2 9.8 copy-start.5
  7.2 11.2 copy-start.6
  7.2 16.3 %copy-start.4 = (s32[1,3]{1,0:T(1,128)S(1)}, s32[1,3]{1,0:T(1,128)}, u32[]{:S(2)}) copy-start(s32[1,3]{1,0:T(1,128)} %param.9) | copy-start | bytes 40
  7.2 1055.9 %all-reduce.3.cloned.1.call-start = ((), (), s32[]{:S(2)}) async-start(), calls=%async_computation | async-start | bytes 1638400 | tf_op jit(solution)/shard_map/psum | solution.py:32
  10.2 19.8 %collective-permute-start.1 = (bf16[2,12,2560]{2,1,0:T(8,128)(2,1)S(1)}, bf16[2,12,2560]{2,1,0:T(8,128)(2,1)S(1)}, u32[]{:S(2)}, u32[]{:S(2)}) collective-permute-start(bf16[2,12,2560]{2,1,0:T(8,128)(2,1)S(1)} %get-tuple-element.18), channel_id=1, source_target_pairs={{1,0},{3,2},{5,4},{7,6},{9,8},{11,10},{13,12},{15,14},{17,16},{19,... | collective-permute-start | bytes 368648 | tf_op jit(solution)/shard_map/ppermute | solution.py:25
  11.5 18.5 %collective-permute-start = (bf16[2,12,2560]{2,1,0:T(8,128)(2,1)S(1)}, bf16[2,12,2560]{2,1,0:T(8,128)(2,1)S(1)}, u32[]{:S(2)}, u32[]{:S(2)}) collective-permute-start(bf16[2,12,2560]{2,1,0:T(8,128)(2,1)S(1)} %get-tuple-element.17), channel_id=1, source_target_pairs={{0,1},{2,3},{4,5},{6,7},{8,9},{10,11},{12,13},{14,15},{16,17},{18,... | collective-permute-start | bytes 368648 | tf_op jit(solution)/shard_map/ppermute | solution.py:22
  32.4 1055.2 %collective-permute-start.2 = (bf16[2,80,2560]{2,1,0:T(8,128)(2,1)S(1)}, bf16[2,80,2560]{2,1,0:T(8,128)(2,1)}, u32[]{:S(2)}, u32[]{:S(2)}) collective-permute-start(bf16[2,80,2560]{2,1,0:T(8,128)(2,1)S(1)} %fusion.3), channel_id=1, source_target_pairs={{2,0},{4,2},{6,4},{8,6},{10,8},{12,10},{14,12},{16,14},{18,16},{20... | collective-permute-start | bytes 2457608 | tf_op jit(solution)/shard_map/ppermute | solution.py:38
  38.1 1096.0 %collective-permute-start.3 = (bf16[2,80,2560]{2,1,0:T(8,128)(2,1)S(1)}, bf16[2,80,2560]{2,1,0:T(8,128)(2,1)}, u32[]{:S(2)}, u32[]{:S(2)}) collective-permute-start(bf16[2,80,2560]{2,1,0:T(8,128)(2,1)S(1)} %fusion.3), channel_id=1, source_target_pairs={{4,0},{6,2},{8,4},{10,6},{12,8},{14,10},{16,12},{18,14},{20,16},{2... | collective-permute-start | bytes 2457608 | tf_op jit(solution)/shard_map/ppermute | solution.py:38
  39.4 1094.7 %collective-permute-start.4 = (bf16[2,80,2560]{2,1,0:T(8,128)(2,1)S(1)}, bf16[2,80,2560]{2,1,0:T(8,128)(2,1)S(1)}, u32[]{:S(2)}, u32[]{:S(2)}) collective-permute-start(bf16[2,80,2560]{2,1,0:T(8,128)(2,1)S(1)} %fusion.3), channel_id=1, source_target_pairs={{6,0},{8,2},{10,4},{12,6},{14,8},{16,10},{18,12},{20,14},{22,16},{... | collective-permute-start | bytes 2457608 | tf_op jit(solution)/shard_map/ppermute | solution.py:38
  1145.6 3.0 copy-start.2
  1156.2 3.0 copy-start.1
  1177.6 3.0 copy-start
Sparse Core Ops, SparseCore 0:
  10.7 1052.4 all-reduce.2
where the time goes:
time: 1210 us
  waiting for transfers between devices  1020 us (84%)
  local copies, waits for them, and re-layouts  95.9 us (8%)
  other arithmetic  54.5 us (5%)
  between operations  19.6 us (2%)
  starting transfers between devices  15.1 us (1%)
    psum x1, waiting for transfers between devices, broadcast(): return lax.psum(kept, axis)  1020 us
    reduce_sum x12, other arithmetic, multilook(): return jnp.mean(shaped, axis=(-3, -1))  35.1 us
  transfers between devices with their start and end apart: 6, of which 1 were waited for; matrix products, arithmetic and copies ran while one was open for 7% of the time, Pallas kernels for 0%

commit v1 on v0

v1 whole, which is shorter than its diff:
```python
import functools

import jax
import jax.numpy as jnp
import ml_dtypes
import numpy as np
from jax import lax
from jax.experimental import pallas as pl
from jax.experimental.pallas import tpu as pltpu
from jax.sharding import Mesh, PartitionSpec as P

NFRAC = 64
LOOK_R = 5
LOOK_C = 20
EPS = 1e-06
MARGIN = 128
BLK = 256
HALO = 16
BF = jnp.bfloat16
F32 = jnp.float32

GRID = (2, 8, 4, 2)
DATE = ("xl", "z", "y", "core")
FAR = ("xl", "z")


def tap_table():
    x = np.arange(8)[None, :] - 3.0 - np.arange(NFRAC)[:, None] / NFRAC
    w = np.sinc(x) * (0.54 + 0.46 * np.cos(np.pi * x / 4.0))
    taps = (w / w.sum(axis=1, keepdims=True)).astype(np.float32)
    return taps.astype(ml_dtypes.bfloat16).astype(np.float32)


def iota(shape, dim):
    return lax.broadcasted_iota(jnp.int32, shape, dim)


def dot(a, b):
    return jnp.dot(a, b, preferred_element_type=F32)


def source_row(position, groups):
    return (position % groups) * LOOK_R + position // groups


def band(distance, shift, table, index):
    total = jnp.zeros(distance.shape, F32)
    for k in range(8):
        total = jnp.where(distance == shift + k, table[index, k], total)
    return total.astype(BF)


def resample_kernel(meta, table, x, halo, z, fit):
    rows, cols = x.shape[1], x.shape[2]
    groups = rows // LOOK_R
    shift = meta[0] - 3
    out_row = source_row(iota((rows, rows), 0), groups)
    near = band(iota((rows, rows), 1) - out_row, shift, table, meta[2])
    out_row = source_row(iota((rows, HALO), 0), groups)
    start = jnp.where(meta[4] == 0, rows, -HALO)
    edge = band(iota((rows, HALO), 1) + start - out_row, shift, table, meta[2])
    fit[:, :MARGIN] = jnp.zeros((2 * rows, MARGIN), BF)
    fit[:, MARGIN + cols :] = jnp.zeros((2 * rows, MARGIN), BF)
    for p in range(2):
        for c in range(0, cols, BLK):
            fit[p * rows : (p + 1) * rows, MARGIN + c : MARGIN + c + BLK] = (
                dot(near, x[p, :, c : c + BLK]) + dot(edge, halo[p, :, c : c + BLK])
            ).astype(BF)
    span = BLK + 2 * MARGIN
    lanes = iota((span, BLK), 0) - MARGIN - iota((span, BLK), 1)
    taps = band(lanes, meta[1] - 3, table, meta[3])
    for c in range(0, cols, BLK):
        part = dot(fit[:, c : c + span], taps).astype(BF)
        z[0, :, c : c + BLK] = part[:rows]
        z[1, :, c : c + BLK] = part[rows:]


def look_matrix(start, count):
    distance = iota((count, 128), 0) + start - LOOK_C * iota((count, 128), 1)
    return jnp.where((distance >= 0) & (distance < LOOK_C), 1.0, 0.0).astype(BF)


def split_dot(sums, looks):
    high = sums.astype(BF)
    low = (sums - high.astype(F32)).astype(BF)
    return dot(high, looks) + dot(low, looks)


def cross(first, second):
    return (
        first[0] * second[0] + first[1] * second[1],
        first[1] * second[0] - first[0] * second[1],
    )


def power(value):
    return value[0] * value[0] + value[1] * value[1]


def pair_kernel(meta, z, v1, vb, vc, own, back_b, back_c):
    rows, cols = z.shape[1], z.shape[2]
    groups = rows // LOOK_R
    total = jnp.zeros((12 * groups, 128), F32)
    for c in range(0, cols, BLK):
        sums = None
        for j in range(LOOK_R):
            at = slice(j * groups, (j + 1) * groups), slice(c, c + BLK)
            images = [
                (ref[(0,) + at].astype(F32), ref[(1,) + at].astype(F32))
                for ref in (z, v1, vb, vc)
            ]
            a, b, d, e = images
            terms = (
                cross(a, b) + cross(a, d) + cross(a, e) + cross(d, b)
                + (power(a), power(b), power(d), power(e))
            )
            sums = terms if sums is None else [s + t for s, t in zip(sums, terms)]
        total = total + split_dot(jnp.concatenate(sums, axis=0), look_matrix(c, BLK))
    total = total * (1.0 / (LOOK_R * LOOK_C))
    maps = [total[i * groups : (i + 1) * groups] for i in range(12)]
    root = [jnp.sqrt(m + EPS) for m in maps[8:]]
    odd = meta[5] == 1

    def write(out, at, pair, first, second, flip):
        re, im = maps[2 * pair], maps[2 * pair + 1]
        out[at] = re
        out[at + 1] = jnp.where(flip, -im, im)
        out[at + 2] = jnp.sqrt(re * re + im * im) / (root[first] * root[second])

    write(own, 0, 0, 0, 1, False)
    write(own, 3, 1, 0, 2, False)
    write(back_b, 0, 1, 0, 2, odd)
    write(back_b, 3, 3, 2, 1, False)
    write(back_c, 0, 2, 0, 3, odd)


def reference_kernel(meta, z, q_own, q_other, out):
    rows, cols = z.shape[1], z.shape[2]
    groups = rows // LOOK_R
    first = meta[5] == 0
    total = jnp.zeros((2 * groups, 128), F32)
    for c in range(0, cols, 128):
        sums = None
        for j in range(LOOK_R):
            at = slice(j * groups, (j + 1) * groups), slice(c, c + 128)
            start = c // 128 * rows + j * groups
            mine = q_own[start : start + groups].astype(F32)
            other = q_other[start : start + groups].astype(F32)
            a = (z[(0,) + at].astype(F32), z[(1,) + at].astype(F32))
            q = jnp.where(first, mine, other), jnp.where(first, other, mine)
            terms = cross(a, q)
            sums = terms if sums is None else [s + t for s, t in zip(sums, terms)]
        total = total + split_dot(jnp.concatenate(sums, axis=0), look_matrix(c, 128))
    total = total * (1.0 / (LOOK_R * LOOK_C))
    out[0, 0] = total[:groups]
    out[0, 1] = total[groups:]


def candidate_kernel(meta, x, received, out):
    rows, cols = x.shape[1], x.shape[2]
    groups = rows // LOOK_R
    keep = meta[5] == meta[6]
    order = source_row(iota((rows, rows), 0), groups) == iota((rows, rows), 1)
    order = jnp.where(order, 1.0, 0.0).astype(BF)
    for c in range(0, cols, 128):
        mine = x[meta[5], :, c : c + 128]
        value = jnp.where(keep, mine, received[:, c : c + 128])
        out[c // 128 * rows : (c // 128 + 1) * rows] = dot(order, value).astype(BF)
    used = cols // 128 * rows
    out[used:] = jnp.zeros((out.shape[0] - used, 128), BF)


def finish_kernel(meta, on, own, got_b, got_c, ifg, coh):
    odd = meta[5] == 1
    for s in range(3):
        usable = (on[0, s] == 1) & (meta[7] + s + 1 < meta[8])
        for m in range(3):
            if s == 0:
                value = own[m]
            elif s == 1:
                value = jnp.where(odd, got_b[m], own[3 + m])
            else:
                value = jnp.where(odd, got_b[3 + m], got_c[m])
            value = jnp.where(usable, value, 0.0)
            if m < 2:
                ifg[0, s, m] = value
            else:
                coh[0, s] = value


SMEM = pl.BlockSpec(memory_space=pltpu.SMEM)
VMEM = pl.BlockSpec(memory_space=pltpu.VMEM)


def call(kernel, scalars, arrays, outs, flops, scratch=(), size=None):
    moved = sum(a.size * a.dtype.itemsize for a in arrays)
    out_shape = [jax.ShapeDtypeStruct(s, d) for s, d in outs]
    single = len(out_shape) == 1
    return pl.pallas_call(
        kernel,
        out_shape=out_shape[0] if single else out_shape,
        in_specs=[SMEM] * len(scalars) + [VMEM] * len(arrays),
        out_specs=VMEM if single else [VMEM] * len(out_shape),
        scratch_shapes=list(scratch),
        compiler_params=pltpu.CompilerParams(vmem_limit_bytes=32 * 2**20),
        cost_estimate=pl.CostEstimate(flops=flops, bytes_accessed=moved, transcendentals=0),
    )(*scalars, *arrays)


def on_device(table, slc, coarse, fraction, pair_on, ref_date):
    x = slc[0]
    _, rows, cols = x.shape
    groups = rows // LOOK_R
    row = lax.axis_index("row")
    core = lax.axis_index("core")
    date = lax.axis_index(DATE)
    dates = lax.axis_size(DATE)
    near = lax.axis_size("y") * lax.axis_size("core")
    far = dates // near
    ref = ref_date[0]
    meta = jnp.stack(
        [coarse[0, 0], coarse[0, 1], fraction[0, 0], fraction[0, 1], row, core, ref % 2, date, dates]
    ).astype(jnp.int32)

    other = lax.dynamic_index_in_dim(x, 1 - core, 0, keepdims=False)
    other = lax.ppermute(other, "core", [(0, 1), (1, 0)])
    edge = jnp.where(row == 0, x[:, rows - HALO :], x[:, :HALO])
    halo = lax.ppermute(edge, "row", [(0, 1), (1, 0)])

    tiles = cols // 128 * rows
    piece = -(-tiles // (16 * far)) * 16
    cand = call(
        candidate_kernel, [meta], [x, other], [((far * piece, 128), BF)], 2 * rows * rows * cols
    ).reshape(far, piece, 128)

    z = call(
        resample_kernel, [meta, table], [x, halo], [(x.shape, BF)],
        4 * rows * cols * (rows + HALO + BLK + 2 * MARGIN),
        [pltpu.VMEM((2 * rows, cols + 2 * MARGIN), BF)],
    )

    v1 = lax.ppermute(z, DATE, [(i + 1, i) for i in range(dates - 1)])
    pairs_b = [(i, i - 2) for i in range(2, dates, 2)] + [(i, i + 2) for i in range(1, dates - 2, 2)]
    vb = lax.ppermute(z, DATE, pairs_b)
    vc = lax.ppermute(z, DATE, [(i, i + 3) for i in range(0, dates - 3, 2)])

    got = lax.all_to_all(cand, FAR, 0, 0)
    got = lax.dynamic_index_in_dim(got, ref // near, 0)
    got = lax.all_to_all(jnp.broadcast_to(got, (near // 2, piece, 128)), "y", 0, 0)
    got = lax.dynamic_index_in_dim(got, ref % near // 2, 0)
    q_own = lax.all_to_all(jnp.broadcast_to(got, (far, piece, 128)), FAR, 0, 0)
    q_own = q_own.reshape(far * piece, 128)
    q_other = lax.ppermute(q_own, "core", [(0, 1), (1, 0)])

    small = (groups, 128)
    own, back_b, back_c = call(
        pair_kernel, [meta], [z, v1, vb, vc],
        [((6,) + small, F32), ((6,) + small, F32), ((3,) + small, F32)],
        100 * rows * cols,
    )
    got_b = lax.ppermute(back_b, DATE, [(i, i - 2) for i in range(3, dates, 2)])
    got_c = lax.ppermute(back_c, DATE, [(i, i - 3) for i in range(3, dates, 2)])
    ref_ifg = call(
        reference_kernel, [meta], [z, q_own, q_other], [((1, 2) + small, F32)], 30 * rows * cols
    )
    pair_ifg, coherence = call(
        finish_kernel, [meta, pair_on], [own, got_b, got_c],
        [((1, 3, 2) + small, F32), ((1, 3) + small, F32)], 1000,
    )
    return (ref_ifg, pair_ifg, coherence)


def solution(mesh):
    shape = GRID + (mesh.shape["row"],)
    grid = Mesh(mesh.devices.reshape(shape), DATE + ("row",))
    table = tap_table()

    def program(slc, coarse, fraction, pair_on, ref_date):
        return jax.shard_map(
            on_device,
            mesh=grid,
            in_specs=(
                P(),
                P(DATE, None, "row", None),
                P(DATE, None),
                P(DATE, None),
                P(DATE, None),
                P(),
            ),
            out_specs=(
                P(DATE, None, "row", None),
                P(DATE, None, None, "row", None),
                P(DATE, None, "row", None),
            ),
            check_vma=False,
        )(jnp.asarray(table), slc, coarse, fraction, pair_on, ref_date)

    return program
```

time: 1210 us -> 104 us (0.09)
  the two profiles are of different devices: /device:TPU:1 before, /device:TPU:6 now
where the time goes in v1:
time: 104 us; the launch traced here: 103 us
  waiting for transfers between devices  50.6 us (49%)
  starting transfers between devices  33.1 us (32%)
  Pallas kernels  10.6 us (10%)
  local copies, waits for them, and re-layouts  7.17 us (7%)
  between operations  1.43 us (1%)
    all_to_all x1, waiting for transfers between devices, on_device(): got = lax.all_to_all(cand, FAR, 0, 0)  13.8 us
    pallas_call x5, Pallas kernels, call(): pl.pallas_call(kernel, out_shape=out_shape[0] if single else out_shape, i...  10.6 us
    ppermute x1, waiting for transfers between devices, on_device(): got_c = lax.ppermute(back_c, DATE, [(i, i - 3) for i in range(3, dates, 2)])  10.1 us
    all_to_all x1, starting transfers between devices, on_device(): got = lax.all_to_all(cand, FAR, 0, 0)  9.94 us
    ppermute x1, waiting for transfers between devices, on_device(): vb = lax.ppermute(z, DATE, pairs_b)  9.54 us
    ppermute x1, waiting for transfers between devices, on_device(): halo = lax.ppermute(edge, 'row', [(0, 1), (1, 0)])  7.65 us
    all_to_all x1, waiting for transfers between devices, on_device(): lax.all_to_all(jnp.broadcast_to(got, (near // 2, piece, 128)), 'y', 0, 0)  5.89 us
    all_to_all x1, starting transfers between devices, on_device(): q_own = lax.all_to_all(jnp.broadcast_to(got, (far, piece, 128)), FAR, 0, 0)  5.71 us
  transfers between devices with their start and end apart: 11, of which 7 were waited for; matrix products, arithmetic and copies ran while one was open for 4% of the time, Pallas kernels for 7%

profile of v1, /device:TPU:6, one launch (start us, length us, event | category | flops | bytes accessed | tf_op | source)
XLA Modules:
  0.0 102.9 jit_solution(10184847242045246881)
XLA Ops:
  0.6 0.0 copy-start
  0.6 1.1 %dynamic-slice_bitcast_fusion = bf16[80,2560]{1,0:T(8,128)(2,1)S(1)} fusion(bf16[1,2,80,2560]{3,2,1,0:T(8,128)(2,1)} %param.6, s32[]{:T(128)S(6)} %select_n.41), kind=kLoop, calls=%fused_computation | loop fusion | bytes 819204 | tf_op jit(solution)/shard_map/jit(dynamic_index_in_dim)/squeeze | solution.py:225
  1.8 0.1 collective-permute-start.1
  2.5 0.0 copy-start.3
  2.5 0.6 copy-done.3
  3.2 0.0 copy-start.4
  3.2 0.6 fusion.1
  3.8 0.1 copy-done.4
  3.8 0.6 fusion
  4.4 2.6 %stack.19.meta = s32[9]{0:T(128)S(1)} concatenate(s32[1]{0:T(128)} %bitcast, s32[1]{0:T(128)} %bitcast.1, s32[1]{0:T(128)} %bitcast.2, s32[1]{0:T(128)} %bitcast.3, s32[1]{0:T(128)} %bitcast.4, s32[1]{0:T(128)} %bitcast.5, s32[1]{0:T(128)} %bitcast.7, s32[1]{0:T(128)} %bitcast.8, s32[1]{0:T(128)} %constant.81.clone.1), dimensions={0} | concatenate | bytes 72 | tf_op jit(solution)/shard_map/stack | solution.py:221
  7.1 0.0 collective-permute-done.1.received
  7.1 0.0 copy-done
  7.1 1.7 %shard_map.86 = bf16[1792,128]{1,0:T(8,128)(2,1)} custom-call(s32[9]{0:T(128)S(1)} %stack.19.meta, bf16[2,80,2560]{2,1,0:T(8,128)(2,1)S(1)} %bitcast.22, bf16[80,2560]{1,0:T(8,128)(2,1)S(1)} %collective-permute-done.1.received), custom_call_target="tpu_custom_call" | custom-call | flops 32768000 | bytes 1228800 | tf_op jit(solution)/shard_map/pallas_call | solution.py:199
  8.8 9.9 %all-to-all-start = ((bf16[16,112,128]{2,1,0:T(8,128)(2,1)}), bf16[16,112,128]{2,1,0:T(8,128)(2,1)S(1)}, u32[]{:S(2)}, u32[]{:S(2)}) async-start(bf16[16,112,128]{2,1,0:T(8,128)(2,1)} %bitcast.11), calls=%async_computation | async-start | bytes 917504 | tf_op jit(solution)/shard_map/all_to_all | solution.py:247
  18.7 13.8 %all-to-all-done = bf16[16,112,128]{2,1,0:T(8,128)(2,1)S(1)} async-done(((bf16[16,112,128]{2,1,0:T(8,128)(2,1)}), bf16[16,112,128]{2,1,0:T(8,128)(2,1)S(1)}, u32[]{:S(2)}, u32[]{:S(2)}) %all-to-all-start) | async-done | bytes 458784 | tf_op jit(solution)/shard_map/all_to_all | solution.py:247
  32.5 0.7 broadcast_in_dim.15
  33.2 4.5 %all-to-all-start.1 = ((bf16[4,112,128]{2,1,0:T(8,128)(2,1)}), bf16[4,112,128]{2,1,0:T(8,128)(2,1)S(1)}, u32[]{:S(2)}, u32[]{:S(2)}) async-start(bf16[4,112,128]{2,1,0:T(8,128)(2,1)} %broadcast_in_dim.15), calls=%async_computation.1 | async-start | bytes 229376 | tf_op jit(solution)/shard_map/all_to_all | solution.py:249
  37.6 5.9 %all-to-all-done.1 = bf16[4,112,128]{2,1,0:T(8,128)(2,1)S(1)} async-done(((bf16[4,112,128]{2,1,0:T(8,128)(2,1)}), bf16[4,112,128]{2,1,0:T(8,128)(2,1)S(1)}, u32[]{:S(2)}, u32[]{:S(2)}) %all-to-all-start.1) | async-done | bytes 114720 | tf_op jit(solution)/shard_map/all_to_all | solution.py:249
  43.5 0.9 broadcast_in_dim.17
  44.4 5.7 %all-to-all-start.2 = ((bf16[16,112,128]{2,1,0:T(8,128)(2,1)}), bf16[16,112,128]{2,1,0:T(8,128)(2,1)S(1)}, u32[]{:S(2)}, u32[]{:S(2)}) async-start(bf16[16,112,128]{2,1,0:T(8,128)(2,1)} %broadcast_in_dim.17), calls=%async_computation.2 | async-start | bytes 917504 | tf_op jit(solution)/shard_map/all_to_all | solution.py:251
  50.1 0.0 copy-start.2
  50.1 1.5 %collective-permute-start = (bf16[2,16,2560]{2,1,0:T(8,128)(2,1)S(1)}, bf16[2,16,2560]{2,1,0:T(8,128)(2,1)S(1)}, u32[]{:S(2)}, u32[]{:S(2)}) collective-permute-start(bf16[2,16,2560]{2,1,0:T(8,128)(2,1)S(1)} %slice_select_fusion), channel_id=1, source_target_pairs={{0,1},{1,0},{2,3},{3,2},{4,5},{5,4},{6,7},{7,6},{8,9},{9,8},{10,11... | collective-permute-start | bytes 491528 | tf_op jit(solution)/shard_map/ppermute | solution.py:228
  51.6 7.6 %collective-permute-done.halo = bf16[2,16,2560]{2,1,0:T(8,128)(2,1)S(1)} collective-permute-done((bf16[2,16,2560]{2,1,0:T(8,128)(2,1)S(1)}, bf16[2,16,2560]{2,1,0:T(8,128)(2,1)S(1)}, u32[]{:S(2)}, u32[]{:S(2)}) %collective-permute-start) | collective-permute-done | bytes 163872 | tf_op jit(solution)/shard_map/ppermute | solution.py:228
  59.3 0.0 copy-done.2
  59.3 2.3 %shard_map.85.z = bf16[2,80,2560]{2,1,0:T(8,128)(2,1)S(1)} custom-call(s32[9]{0:T(128)S(1)} %stack.19.meta, f32[64,8]{1,0:T(8,128)S(1)} %copy-done.2, bf16[2,80,2560]{2,1,0:T(8,128)(2,1)S(1)} %bitcast.24, bf16[2,16,2560]{2,1,0:T(8,128)(2,1)S(1)} %collective-permute-done.halo), custom_call_target="tpu_custom_call" | custom-call | flops 498073600 | bytes 983040 | tf_op jit(solution)/shard_map/pallas_call | solution.py:199
  61.6 2.2 %collective-permute-start.3 = (bf16[2,80,2560]{2,1,0:T(8,128)(2,1)S(1)}, bf16[2,80,2560]{2,1,0:T(8,128)(2,1)S(1)}, u32[]{:S(2)}, u32[]{:S(2)}) collective-permute-start(bf16[2,80,2560]{2,1,0:T(8,128)(2,1)S(1)} %shard_map.85.z), channel_id=1, source_target_pairs={{2,0},{4,2},{6,4},{8,6},{10,8},{12,10},{14,12},{16,14},{18,16},{20... | collective-permute-start | bytes 2457608 | tf_op jit(solution)/shard_map/ppermute | solution.py:242
  63.8 5.1 %collective-permute-start.4 = (bf16[2,80,2560]{2,1,0:T(8,128)(2,1)S(1)}, bf16[2,80,2560]{2,1,0:T(8,128)(2,1)S(1)}, u32[]{:S(2)}, u32[]{:S(2)}) collective-permute-start(bf16[2,80,2560]{2,1,0:T(8,128)(2,1)S(1)} %shard_map.85.z), channel_id=1, source_target_pairs={{4,0},{8,4},{12,8},{16,12},{20,16},{24,20},{28,24},{32,28},{36,32}... | collective-permute-start | bytes 2457608 | tf_op jit(solution)/shard_map/ppermute | solution.py:244
  68.9 2.2 %collective-permute-start.5 = (bf16[2,80,2560]{2,1,0:T(8,128)(2,1)S(1)}, bf16[2,80,2560]{2,1,0:T(8,128)(2,1)}, u32[]{:S(2)}, u32[]{:S(2)}) collective-permute-start(bf16[2,80,2560]{2,1,0:T(8,128)(2,1)S(1)} %shard_map.85.z), channel_id=1, source_target_pairs={{0,6},{4,10},{8,14},{12,18},{16,22},{20,26},{24,30},{28,34},{32,38... | collective-permute-start | bytes 2457608 | tf_op jit(solution)/shard_map/ppermute | solution.py:245
  71.1 0.0 all-to-all-done.2
  71.1 0.0 collective-permute-start.2
  71.1 2.5 %collective-permute-done.3.v1 = bf16[2,80,2560]{2,1,0:T(8,128)(2,1)S(1)} collective-permute-done((bf16[2,80,2560]{2,1,0:T(8,128)(2,1)S(1)}, bf16[2,80,2560]{2,1,0:T(8,128)(2,1)S(1)}, u32[]{:S(2)}, u32[]{:S(2)}) %collective-permute-start.3) | collective-permute-done | bytes 819232 | tf_op jit(solution)/shard_map/ppermute | solution.py:242
  73.6 9.5 %collective-permute-done.4.vb = bf16[2,80,2560]{2,1,0:T(8,128)(2,1)S(1)} collective-permute-done((bf16[2,80,2560]{2,1,0:T(8,128)(2,1)S(1)}, bf16[2,80,2560]{2,1,0:T(8,128)(2,1)S(1)}, u32[]{:S(2)}, u32[]{:S(2)}) %collective-permute-start.4) | collective-permute-done | bytes 819232 | tf_op jit(solution)/shard_map/ppermute | solution.py:244
  83.2 1.0 collective-permute-done.5.vc
  84.2 3.4 %shard_map.88 = (f32[6,16,128]{2,1,0:T(8,128)S(1)}, f32[6,16,128]{2,1,0:T(8,128)S(1)}, f32[3,16,128]{2,1,0:T(8,128)S(1)}) custom-call(s32[9]{0:T(128)S(1)} %stack.19.meta, bf16[2,80,2560]{2,1,0:T(8,128)(2,1)S(1)} %shard_map.85.z, bf16[2,80,2560]{2,1,0:T(8,128)(2,1)S(1)} %collective-permute-done.3.v1, bf16[2,80,2560]{2,1,0:T(8,128)(2,1)S(1)} %collective-permute-done.4.vb, ...), custom_call_target="tpu_custom_call" | custom-call | flops 20480000 | bytes 3276800 | tf_op jit(solution)/shard_map/pallas_call | solution.py:199
  87.6 0.7 collective-permute-start.6
  88.2 0.0 copy-start.1
  88.3 1.3 %collective-permute-start.7 = (f32[3,16,128]{2,1,0:T(8,128)S(1)}, f32[3,16,128]{2,1,0:T(8,128)S(1)}, u32[]{:S(2)}, u32[]{:S(2)}) collective-permute-start(f32[3,16,128]{2,1,0:T(8,128)S(1)} %get-tuple-element.10), channel_id=1, source_target_pairs={{6,0},{10,4},{14,8},{18,12},{22,16},{26,20},{30,24},{34,28},{38,32... | collective-permute-start | bytes 73736 | tf_op jit(solution)/shard_map/ppermute | solution.py:262
  89.6 10.1 %collective-permute-done.7.got_c = f32[3,16,128]{2,1,0:T(8,128)S(1)} collective-permute-done((f32[3,16,128]{2,1,0:T(8,128)S(1)}, f32[3,16,128]{2,1,0:T(8,128)S(1)}, u32[]{:S(2)}, u32[]{:S(2)}) %collective-permute-start.7) | collective-permute-done | bytes 24608 | tf_op jit(solution)/shard_map/ppermute | solution.py:262
  99.7 0.0 collective-permute-done.6.got_b
  99.7 0.0 copy-done.1
  99.7 1.2 %shard_map.89 = (f32[1,3,2,16,128]{4,3,2,1,0:T(8,128)}, f32[1,3,16,128]{3,2,1,0:T(8,128)}) custom-call(s32[9]{0:T(128)S(1)} %stack.19.meta, s32[1,3]{1,0:T(1,128)S(1)} %copy-done.1, f32[6,16,128]{2,1,0:T(8,128)S(1)} %get-tuple-element.8.own, f32[6,16,128]{2,1,0:T(8,128)S(1)} %collective-permute-done.6.got_b, f32[3,16,128]{2,1,0:T(8,128)S(1)} %collective-permute-done.7.got_c), custom_call_target="tpu_custom_call" | custom-call | flops 1000 | bytes 122880 | tf_op jit(solution)/shard_map/pallas_call | solution.py:199
  100.9 0.0 collective-permute-done.2.q_other
  100.9 2.0 %shard_map.87 = f32[1,2,16,128]{3,2,1,0:T(8,128)} custom-call(s32[9]{0:T(128)S(1)} %stack.19.meta, bf16[2,80,2560]{2,1,0:T(8,128)(2,1)S(1)} %shard_map.85.z, bf16[1792,128]{1,0:T(8,128)(2,1)S(1)} %bitcast.26, bf16[1792,128]{1,0:T(8,128)(2,1)S(1)} %collective-permute-done.2.q_other), custom_call_target="tpu_custom_call" | custom-call | flops 6144000 | bytes 1736704 | tf_op jit(solution)/shard_map/pallas_call | solution.py:199
  (3 shorter events, 0.0 us)
Async XLA Ops:
  0.6 6.5 %copy-start = (bf16[1,2,80,2560]{3,2,1,0:T(8,128)(2,1)S(1)}, bf16[1,2,80,2560]{3,2,1,0:T(8,128)(2,1)}, u32[]{:S(2)}) copy-start(bf16[1,2,80,2560]{3,2,1,0:T(8,128)(2,1)} %param.6) | copy-start | bytes 2457604
  1.8 5.3 %collective-permute-start.1 = (bf16[80,2560]{1,0:T(8,128)(2,1)S(1)}, bf16[80,2560]{1,0:T(8,128)(2,1)S(1)}, u32[]{:S(2)}, u32[]{:S(2)}) collective-permute-start(bf16[80,2560]{1,0:T(8,128)(2,1)S(1)} %dynamic-slice_bitcast_fusion), channel_id=1, source_target_pairs={{0,2},{2,0},{1,3},{3,1},{4,6},{6,4},{5,7},{7,5},{8,10},{10,8},{9,1... | collective-permute-start | bytes 1228808 | tf_op jit(solution)/shard_map/ppermute | solution.py:226
  2.5 0.7 copy-start.3
  3.2 0.7 copy-start.4
  8.8 23.7 %all-to-all-start = ((bf16[16,112,128]{2,1,0:T(8,128)(2,1)}), bf16[16,112,128]{2,1,0:T(8,128)(2,1)S(1)}, u32[]{:S(2)}, u32[]{:S(2)}) async-start(bf16[16,112,128]{2,1,0:T(8,128)(2,1)} %bitcast.11), calls=%async_computation | async-start | bytes 917504 | tf_op jit(solution)/shard_map/all_to_all | solution.py:247
  33.2 10.4 %all-to-all-start.1 = ((bf16[4,112,128]{2,1,0:T(8,128)(2,1)}), bf16[4,112,128]{2,1,0:T(8,128)(2,1)S(1)}, u32[]{:S(2)}, u32[]{:S(2)}) async-start(bf16[4,112,128]{2,1,0:T(8,128)(2,1)} %broadcast_in_dim.15), calls=%async_computation.1 | async-start | bytes 229376 | tf_op jit(solution)/shard_map/all_to_all | solution.py:249
  44.4 26.7 %all-to-all-start.2 = ((bf16[16,112,128]{2,1,0:T(8,128)(2,1)}), bf16[16,112,128]{2,1,0:T(8,128)(2,1)S(1)}, u32[]{:S(2)}, u32[]{:S(2)}) async-start(bf16[16,112,128]{2,1,0:T(8,128)(2,1)} %broadcast_in_dim.17), calls=%async_computation.2 | async-start | bytes 917504 | tf_op jit(solution)/shard_map/all_to_all | solution.py:251
  50.1 9.2 %copy-start.2 = (f32[64,8]{1,0:T(8,128)S(1)}, f32[64,8]{1,0:T(8,128)}, u32[]{:S(2)}) copy-start(f32[64,8]{1,0:T(8,128)} %constant.87.clone.table) | copy-start | bytes 6148
  50.1 9.1 %collective-permute-start = (bf16[2,16,2560]{2,1,0:T(8,128)(2,1)S(1)}, bf16[2,16,2560]{2,1,0:T(8,128)(2,1)S(1)}, u32[]{:S(2)}, u32[]{:S(2)}) collective-permute-start(bf16[2,16,2560]{2,1,0:T(8,128)(2,1)S(1)} %slice_select_fusion), channel_id=1, source_target_pairs={{0,1},{1,0},{2,3},{3,2},{4,5},{5,4},{6,7},{7,6},{8,9},{9,8},{10,11... | collective-permute-start | bytes 491528 | tf_op jit(solution)/shard_map/ppermute | solution.py:228
  61.6 12.0 %collective-permute-start.3 = (bf16[2,80,2560]{2,1,0:T(8,128)(2,1)S(1)}, bf16[2,80,2560]{2,1,0:T(8,128)(2,1)S(1)}, u32[]{:S(2)}, u32[]{:S(2)}) collective-permute-start(bf16[2,80,2560]{2,1,0:T(8,128)(2,1)S(1)} %shard_map.85.z), channel_id=1, source_target_pairs={{2,0},{4,2},{6,4},{8,6},{10,8},{12,10},{14,12},{16,14},{18,16},{20... | collective-permute-start | bytes 2457608 | tf_op jit(solution)/shard_map/ppermute | solution.py:242
  63.8 19.4 %collective-permute-start.4 = (bf16[2,80,2560]{2,1,0:T(8,128)(2,1)S(1)}, bf16[2,80,2560]{2,1,0:T(8,128)(2,1)S(1)}, u32[]{:S(2)}, u32[]{:S(2)}) collective-permute-start(bf16[2,80,2560]{2,1,0:T(8,128)(2,1)S(1)} %shard_map.85.z), channel_id=1, source_target_pairs={{4,0},{8,4},{12,8},{16,12},{20,16},{24,20},{28,24},{32,28},{36,32}... | collective-permute-start | bytes 2457608 | tf_op jit(solution)/shard_map/ppermute | solution.py:244
  68.9 15.3 %collective-permute-start.5 = (bf16[2,80,2560]{2,1,0:T(8,128)(2,1)S(1)}, bf16[2,80,2560]{2,1,0:T(8,128)(2,1)}, u32[]{:S(2)}, u32[]{:S(2)}) collective-permute-start(bf16[2,80,2560]{2,1,0:T(8,128)(2,1)S(1)} %shard_map.85.z), channel_id=1, source_target_pairs={{0,6},{4,10},{8,14},{12,18},{16,22},{20,26},{24,30},{28,34},{32,38... | collective-permute-start | bytes 2457608 | tf_op jit(solution)/shard_map/ppermute | solution.py:245
  71.1 29.8 %collective-permute-start.2 = (bf16[1792,128]{1,0:T(8,128)(2,1)S(1)}, bf16[1792,128]{1,0:T(8,128)(2,1)S(1)}, u32[]{:S(2)}, u32[]{:S(2)}) collective-permute-start(bf16[1792,128]{1,0:T(8,128)(2,1)S(1)} %bitcast.25), channel_id=1, source_target_pairs={{0,2},{2,0},{1,3},{3,1},{4,6},{6,4},{5,7},{7,5},{8,10},{10,8},{9,1... | collective-permute-start | bytes 1376264 | tf_op jit(solution)/shard_map/ppermute | solution.py:253
  87.6 12.1 %collective-permute-start.6 = (f32[6,16,128]{2,1,0:T(8,128)S(1)}, f32[6,16,128]{2,1,0:T(8,128)S(1)}, u32[]{:S(2)}, u32[]{:S(2)}) collective-permute-start(f32[6,16,128]{2,1,0:T(8,128)S(1)} %get-tuple-element.9), channel_id=1, source_target_pairs={{6,2},{10,6},{14,10},{18,14},{22,18},{26,22},{30,26},{34,30},{38,3... | collective-permute-start | bytes 147464 | tf_op jit(solution)/shard_map/ppermute | solution.py:261
  88.2 11.5 %copy-start.1 = (s32[1,3]{1,0:T(1,128)S(1)}, s32[1,3]{1,0:T(1,128)}, u32[]{:S(2)}) copy-start(s32[1,3]{1,0:T(1,128)} %on.1) | copy-start | bytes 40
  88.3 11.4 %collective-permute-start.7 = (f32[3,16,128]{2,1,0:T(8,128)S(1)}, f32[3,16,128]{2,1,0:T(8,128)S(1)}, u32[]{:S(2)}, u32[]{:S(2)}) collective-permute-start(f32[3,16,128]{2,1,0:T(8,128)S(1)} %get-tuple-element.10), channel_id=1, source_target_pairs={{6,0},{10,4},{14,8},{18,12},{22,16},{26,20},{30,24},{34,28},{38,32... | collective-permute-start | bytes 73736 | tf_op jit(solution)/shard_map/ppermute | solution.py:262

commit v2 on v1

--- a/solution.py
+++ b/solution.py
@@ -21,7 +21,7 @@
 
 GRID = (2, 8, 4, 2)
 DATE = ("xl", "z", "y", "core")
-FAR = ("xl", "z")
+CHIP = ("xl", "z", "y")
 
 
 def tap_table():
@@ -50,15 +50,15 @@
     return total.astype(BF)
 
 
-def resample_kernel(meta, table, x, halo, z, fit):
+def resample_kernel(coarse, fraction, table, x, halo, z, fit):
     rows, cols = x.shape[1], x.shape[2]
     groups = rows // LOOK_R
-    shift = meta[0] - 3
+    shift = coarse[0, 0] - 3
     out_row = source_row(iota((rows, rows), 0), groups)
-    near = band(iota((rows, rows), 1) - out_row, shift, table, meta[2])
+    near = band(iota((rows, rows), 1) - out_row, shift, table, fraction[0, 0])
     out_row = source_row(iota((rows, HALO), 0), groups)
-    start = jnp.where(meta[4] == 0, rows, -HALO)
-    edge = band(iota((rows, HALO), 1) + start - out_row, shift, table, meta[2])
+    start = jnp.where(lax.axis_index("row") == 0, rows, -HALO)
+    edge = band(iota((rows, HALO), 1) + start - out_row, shift, table, fraction[0, 0])
     fit[:, :MARGIN] = jnp.zeros((2 * rows, MARGIN), BF)
     fit[:, MARGIN + cols :] = jnp.zeros((2 * rows, MARGIN), BF)
     for p in range(2):
@@ -68,7 +68,7 @@
             ).astype(BF)
     span = BLK + 2 * MARGIN
     lanes = iota((span, BLK), 0) - MARGIN - iota((span, BLK), 1)
-    taps = band(lanes, meta[1] - 3, table, meta[3])
+    taps = band(lanes, coarse[0, 1] - 3, table, fraction[0, 1])
     for c in range(0, cols, BLK):
         part = dot(fit[:, c : c + span], taps).astype(BF)
         z[0, :, c : c + BLK] = part[:rows]
@@ -97,7 +97,7 @@
     return value[0] * value[0] + value[1] * value[1]
 
 
-def pair_kernel(meta, z, v1, vb, vc, own, back_b, back_c):
+def pair_kernel(z, v1, vb, vc, own, back_b, back_c):
     rows, cols = z.shape[1], z.shape[2]
     groups = rows // LOOK_R
     total = jnp.zeros((12 * groups, 128), F32)
@@ -119,7 +119,7 @@
     total = total * (1.0 / (LOOK_R * LOOK_C))
     maps = [total[i * groups : (i + 1) * groups] for i in range(12)]
     root = [jnp.sqrt(m + EPS) for m in maps[8:]]
-    odd = meta[5] == 1
+    odd = lax.axis_index("core") == 1
 
     def write(out, at, pair, first, second, flip):
         re, im = maps[2 * pair], maps[2 * pair + 1]
@@ -134,10 +134,10 @@
     write(back_c, 0, 2, 0, 3, odd)
 
 
-def reference_kernel(meta, z, q_own, q_other, out):
+def reference_kernel(z, q_own, q_other, out):
     rows, cols = z.shape[1], z.shape[2]
     groups = rows // LOOK_R
-    first = meta[5] == 0
+    first = lax.axis_index("core") == 0
     total = jnp.zeros((2 * groups, 128), F32)
     for c in range(0, cols, 128):
         sums = None
@@ -156,24 +156,26 @@
     out[0, 1] = total[groups:]
 
 
-def candidate_kernel(meta, x, received, out):
+def candidate_kernel(ref, x, received, out):
     rows, cols = x.shape[1], x.shape[2]
     groups = rows // LOOK_R
-    keep = meta[5] == meta[6]
+    core = lax.axis_index("core")
+    keep = core == ref[0] % 2
     order = source_row(iota((rows, rows), 0), groups) == iota((rows, rows), 1)
     order = jnp.where(order, 1.0, 0.0).astype(BF)
     for c in range(0, cols, 128):
-        mine = x[meta[5], :, c : c + 128]
+        mine = x[core, :, c : c + 128]
         value = jnp.where(keep, mine, received[:, c : c + 128])
         out[c // 128 * rows : (c // 128 + 1) * rows] = dot(order, value).astype(BF)
     used = cols // 128 * rows
     out[used:] = jnp.zeros((out.shape[0] - used, 128), BF)
 
 
-def finish_kernel(meta, on, own, got_b, got_c, ifg, coh):
-    odd = meta[5] == 1
+def finish_kernel(on, own, got_b, got_c, ifg, coh):
+    date, dates = lax.axis_index(DATE), lax.axis_size(DATE)
+    odd = lax.axis_index("core") == 1
     for s in range(3):
-        usable = (on[0, s] == 1) & (meta[7] + s + 1 < meta[8])
+        usable = (on[0, s] == 1) & (date + s + 1 < dates)
         for m in range(3):
             if s == 0:
                 value = own[m]
@@ -213,58 +215,51 @@
     groups = rows // LOOK_R
     row = lax.axis_index("row")
     core = lax.axis_index("core")
-    date = lax.axis_index(DATE)
     dates = lax.axis_size(DATE)
-    near = lax.axis_size("y") * lax.axis_size("core")
-    far = dates // near
+    chips = dates // lax.axis_size("core")
     ref = ref_date[0]
-    meta = jnp.stack(
-        [coarse[0, 0], coarse[0, 1], fraction[0, 0], fraction[0, 1], row, core, ref % 2, date, dates]
-    ).astype(jnp.int32)
-
     other = lax.dynamic_index_in_dim(x, 1 - core, 0, keepdims=False)
     other = lax.ppermute(other, "core", [(0, 1), (1, 0)])
     edge = jnp.where(row == 0, x[:, rows - HALO :], x[:, :HALO])
     halo = lax.ppermute(edge, "row", [(0, 1), (1, 0)])
 
     tiles = cols // 128 * rows
-    piece = -(-tiles // (16 * far)) * 16
+    piece = -(-tiles // (16 * chips)) * 16
     cand = call(
-        candidate_kernel, [meta], [x, other], [((far * piece, 128), BF)], 2 * rows * rows * cols
-    ).reshape(far, piece, 128)
+        candidate_kernel, [ref_date], [x, other], [((chips * piece, 128), BF)], 2 * rows * rows * cols
+    ).reshape(chips, piece, 128)
 
     z = call(
-        resample_kernel, [meta, table], [x, halo], [(x.shape, BF)],
+        resample_kernel, [coarse, fraction, table], [x, halo], [(x.shape, BF)],
         4 * rows * cols * (rows + HALO + BLK + 2 * MARGIN),
         [pltpu.VMEM((2 * rows, cols + 2 * MARGIN), BF)],
     )
+
+    got = lax.all_to_all(cand, CHIP, 0, 0)
+    got, z = lax.optimization_barrier((got, z))
+    got = lax.dynamic_index_in_dim(got, ref // 2, 0)
+    q_own = lax.all_to_all(jnp.broadcast_to(got, (chips, piece, 128)), CHIP, 0, 0)
+    q_own = q_own.reshape(chips * piece, 128)
+    q_other = lax.ppermute(q_own, "core", [(0, 1), (1, 0)])
 
     v1 = lax.ppermute(z, DATE, [(i + 1, i) for i in range(dates - 1)])
     pairs_b = [(i, i - 2) for i in range(2, dates, 2)] + [(i, i + 2) for i in range(1, dates - 2, 2)]
     vb = lax.ppermute(z, DATE, pairs_b)
     vc = lax.ppermute(z, DATE, [(i, i + 3) for i in range(0, dates - 3, 2)])
 
-    got = lax.all_to_all(cand, FAR, 0, 0)
-    got = lax.dynamic_index_in_dim(got, ref // near, 0)
-    got = lax.all_to_all(jnp.broadcast_to(got, (near // 2, piece, 128)), "y", 0, 0)
-    got = lax.dynamic_index_in_dim(got, ref % near // 2, 0)
-    q_own = lax.all_to_all(jnp.broadcast_to(got, (far, piece, 128)), FAR, 0, 0)
-    q_own = q_own.reshape(far * piece, 128)
-    q_other = lax.ppermute(q_own, "core", [(0, 1), (1, 0)])
-
     small = (groups, 128)
     own, back_b, back_c = call(
-        pair_kernel, [meta], [z, v1, vb, vc],
+        pair_kernel, [], [z, v1, vb, vc],
         [((6,) + small, F32), ((6,) + small, F32), ((3,) + small, F32)],
         100 * rows * cols,
     )
     got_b = lax.ppermute(back_b, DATE, [(i, i - 2) for i in range(3, dates, 2)])
     got_c = lax.ppermute(back_c, DATE, [(i, i - 3) for i in range(3, dates, 2)])
     ref_ifg = call(
-        reference_kernel, [meta], [z, q_own, q_other], [((1, 2) + small, F32)], 30 * rows * cols
+        reference_kernel, [], [z, q_own, q_other], [((1, 2) + small, F32)], 30 * rows * cols
     )
     pair_ifg, coherence = call(
-        finish_kernel, [meta, pair_on], [own, got_b, got_c],
+        finish_kernel, [pair_on], [own, got_b, got_c],
         [((1, 3, 2) + small, F32), ((1, 3) + small, F32)], 1000,
     )
     return (ref_ifg, pair_ifg, coherence)

time: 104 us -> 88.3 us (0.85)
  the two profiles are of different devices: /device:TPU:6 before, /device:TPU:3 now
where the time goes in v2:
time: 88.3 us; the launch traced here: 87.9 us
  starting transfers between devices  44.4 us (50%)
  waiting for transfers between devices  30.5 us (35%)
  Pallas kernels  9.57 us (11%)
  local copies, waits for them, and re-layouts  2.01 us (2%)
  between operations  1.41 us (2%)
    ppermute x1, waiting for transfers between devices, on_device(): vc = lax.ppermute(z, DATE, [(i, i + 3) for i in range(0, dates - 3, 2)])  16 us
    all_to_all x1, starting transfers between devices, on_device(): got = lax.all_to_all(cand, CHIP, 0, 0)  12.6 us
    pallas_call x5, Pallas kernels, call(): pl.pallas_call(kernel, out_shape=out_shape[0] if single else out_shape, i...  9.57 us
    all_to_all x1, starting transfers between devices, on_device(): lax.all_to_all(jnp.broadcast_to(got, (chips, piece, 128)), CHIP, 0, 0)  8.08 us
    ppermute x1, starting transfers between devices, on_device(): v1 = lax.ppermute(z, DATE, [(i + 1, i) for i in range(dates - 1)])  7.74 us
    ppermute x1, waiting for transfers between devices, on_device(): halo = lax.ppermute(edge, 'row', [(0, 1), (1, 0)])  6.61 us
    all_to_all x1, waiting for transfers between devices, on_device(): got = lax.all_to_all(cand, CHIP, 0, 0)  4.21 us
    ppermute x1, starting transfers between devices, on_device(): q_other = lax.ppermute(q_own, 'core', [(0, 1), (1, 0)])  3.9 us
  transfers between devices with their start and end apart: 10, of which 6 were waited for; matrix products, arithmetic and copies ran while one was open for 0% of the time, Pallas kernels for 8%

profile of v2, /device:TPU:3, one launch (start us, length us, event | category | flops | bytes accessed | tf_op | source)
XLA Modules:
  0.0 87.9 jit_solution(6215005722178335824)
XLA Ops:
  0.6 0.0 copy-start
  0.6 1.1 %dynamic-slice_bitcast_fusion = bf16[80,2560]{1,0:T(8,128)(2,1)S(1)} fusion(bf16[1,2,80,2560]{3,2,1,0:T(8,128)(2,1)} %param.6, s32[]{:T(128)S(6)} %select_n.21), kind=kLoop, calls=%fused_computation | loop fusion | bytes 819204 | tf_op jit(solution)/shard_map/jit(dynamic_index_in_dim)/squeeze | solution.py:221
  1.8 0.8 collective-permute-start
  3.2 0.7 collective-permute-done.received
  3.9 0.0 copy-done
  3.9 1.2 %shard_map.85 = bf16[2048,128]{1,0:T(8,128)(2,1)} custom-call(s32[1]{0:T(128)} %copy.9.ref, bf16[2,80,2560]{2,1,0:T(8,128)(2,1)S(1)} %bitcast.12, bf16[80,2560]{1,0:T(8,128)(2,1)S(1)} %collective-permute-done.received), custom_call_target="tpu_custom_call" | custom-call | flops 32768000 | bytes 1228800 | tf_op jit(solution)/shard_map/pallas_call | solution.py:201
  5.1 12.6 %all-to-all-start = ((bf16[64,32,128]{2,1,0:T(8,128)(2,1)}), bf16[64,32,128]{2,1,0:T(8,128)(2,1)S(1)}, u32[]{:S(2)}, u32[]{:S(2)}) async-start(bf16[64,32,128]{2,1,0:T(8,128)(2,1)} %bitcast.2), calls=%async_computation | async-start | bytes 1048576 | tf_op jit(solution)/shard_map/all_to_all | solution.py:238
  17.8 0.0 copy-start.4
  17.8 1.9 %collective-permute-start.1 = (bf16[2,16,2560]{2,1,0:T(8,128)(2,1)S(1)}, bf16[2,16,2560]{2,1,0:T(8,128)(2,1)S(1)}, u32[]{:S(2)}, u32[]{:S(2)}) collective-permute-start(bf16[2,16,2560]{2,1,0:T(8,128)(2,1)S(1)} %slice_select_fusion), channel_id=1, source_target_pairs={{0,1},{1,0},{2,3},{3,2},{4,5},{5,4},{6,7},{7,6},{8,9},{9,8},{10,11... | collective-permute-start | bytes 491528 | tf_op jit(solution)/shard_map/ppermute | solution.py:224
  19.7 0.0 copy-start.2
  19.7 0.0 copy-start.3
  19.7 6.6 %collective-permute-done.1.halo = bf16[2,16,2560]{2,1,0:T(8,128)(2,1)S(1)} collective-permute-done((bf16[2,16,2560]{2,1,0:T(8,128)(2,1)S(1)}, bf16[2,16,2560]{2,1,0:T(8,128)(2,1)S(1)}, u32[]{:S(2)}, u32[]{:S(2)}) %collective-permute-start.1) | collective-permute-done | bytes 163872 | tf_op jit(solution)/shard_map/ppermute | solution.py:224
  26.3 0.0 copy-done.4
  26.3 0.0 copy-done.2
  26.3 0.0 copy-done.3
  26.3 2.3 %shard_map.86.z = bf16[2,80,2560]{2,1,0:T(8,128)(2,1)S(1)} custom-call(s32[1,2]{1,0:T(1,128)S(1)} %copy-done.2, s32[1,2]{1,0:T(1,128)S(1)} %copy-done.3, f32[64,8]{1,0:T(8,128)S(1)} %copy-done.4, bf16[2,80,2560]{2,1,0:T(8,128)(2,1)S(1)} %bitcast.14, bf16[2,16,2560]{2,1,0:T(8,128)(2,1)S(1)} %collective-permute-done.1.halo), custom_call_target="tpu_custom_call" | custom-call | flops 498073600 | bytes 983040 | tf_op jit(solution)/shard_map/pallas_call | solution.py:201
  28.7 4.2 %all-to-all-done = bf16[64,32,128]{2,1,0:T(8,128)(2,1)S(1)} async-done(((bf16[64,32,128]{2,1,0:T(8,128)(2,1)}), bf16[64,32,128]{2,1,0:T(8,128)(2,1)S(1)}, u32[]{:S(2)}, u32[]{:S(2)}) %all-to-all-start) | async-done | bytes 524320 | tf_op jit(solution)/shard_map/all_to_all | solution.py:238
  32.9 0.9 %broadcast_in_dim.8 = bf16[64,32,128]{2,1,0:T(8,128)(2,1)} broadcast(bf16[32,128]{1,0:T(8,128)(2,1)S(1)} %dynamic-slice_bitcast_fusion.1), dimensions={1,2} | broadcast | bytes 532480 | tf_op jit(solution)/shard_map/broadcast_in_dim | solution.py:241
  33.8 8.1 %all-to-all-start.1 = ((bf16[64,32,128]{2,1,0:T(8,128)(2,1)}), bf16[64,32,128]{2,1,0:T(8,128)(2,1)S(1)}, u32[]{:S(2)}, u32[]{:S(2)}) async-start(bf16[64,32,128]{2,1,0:T(8,128)(2,1)} %broadcast_in_dim.8), calls=%async_computation.1 | async-start | bytes 1048576 | tf_op jit(solution)/shard_map/all_to_all | solution.py:241
  41.9 1.3 %collective-permute-start.5 = (bf16[2,80,2560]{2,1,0:T(8,128)(2,1)S(1)}, bf16[2,80,2560]{2,1,0:T(8,128)(2,1)S(1)}, u32[]{:S(2)}, u32[]{:S(2)}) collective-permute-start(bf16[2,80,2560]{2,1,0:T(8,128)(2,1)S(1)} %shard_map.86.z), channel_id=1, source_target_pairs={{0,6},{4,10},{8,14},{12,18},{16,22},{20,26},{24,30},{28,34},{32,38... | collective-permute-start | bytes 2457608 | tf_op jit(solution)/shard_map/ppermute | solution.py:248
  43.2 3.1 %collective-permute-start.4 = (bf16[2,80,2560]{2,1,0:T(8,128)(2,1)S(1)}, bf16[2,80,2560]{2,1,0:T(8,128)(2,1)S(1)}, u32[]{:S(2)}, u32[]{:S(2)}) collective-permute-start(bf16[2,80,2560]{2,1,0:T(8,128)(2,1)S(1)} %shard_map.86.z), channel_id=1, source_target_pairs={{4,0},{8,4},{12,8},{16,12},{20,16},{24,20},{28,24},{32,28},{36,32}... | collective-permute-start | bytes 2457608 | tf_op jit(solution)/shard_map/ppermute | solution.py:247
  46.3 7.7 %collective-permute-start.3 = (bf16[2,80,2560]{2,1,0:T(8,128)(2,1)S(1)}, bf16[2,80,2560]{2,1,0:T(8,128)(2,1)}, u32[]{:S(2)}, u32[]{:S(2)}) collective-permute-start(bf16[2,80,2560]{2,1,0:T(8,128)(2,1)S(1)} %shard_map.86.z), channel_id=1, source_target_pairs={{2,0},{4,2},{6,4},{8,6},{10,8},{12,10},{14,12},{16,14},{18,16},{20... | collective-permute-start | bytes 2457608 | tf_op jit(solution)/shard_map/ppermute | solution.py:245
  54.0 2.0 %all-to-all-done.1 = bf16[64,32,128]{2,1,0:T(8,128)(2,1)S(1)} async-done(((bf16[64,32,128]{2,1,0:T(8,128)(2,1)}), bf16[64,32,128]{2,1,0:T(8,128)(2,1)S(1)}, u32[]{:S(2)}, u32[]{:S(2)}) %all-to-all-start.1) | async-done | bytes 524320 | tf_op jit(solution)/shard_map/all_to_all | solution.py:241
  56.1 3.9 %collective-permute-start.2 = (bf16[2048,128]{1,0:T(8,128)(2,1)S(1)}, bf16[2048,128]{1,0:T(8,128)(2,1)S(1)}, u32[]{:S(2)}, u32[]{:S(2)}) collective-permute-start(bf16[2048,128]{1,0:T(8,128)(2,1)S(1)} %bitcast.15), channel_id=1, source_target_pairs={{0,2},{2,0},{1,3},{3,1},{4,6},{6,4},{5,7},{7,5},{8,10},{10,8},{9,1... | collective-permute-start | bytes 1572872 | tf_op jit(solution)/shard_map/ppermute | solution.py:243
  60.0 16.0 %collective-permute-done.5.vc = bf16[2,80,2560]{2,1,0:T(8,128)(2,1)S(1)} collective-permute-done((bf16[2,80,2560]{2,1,0:T(8,128)(2,1)S(1)}, bf16[2,80,2560]{2,1,0:T(8,128)(2,1)S(1)}, u32[]{:S(2)}, u32[]{:S(2)}) %collective-permute-start.5) | collective-permute-done | bytes 819232 | tf_op jit(solution)/shard_map/ppermute | solution.py:248
  75.9 0.0 collective-permute-done.4.vb
  75.9 0.0 collective-permute-done.3.v1
  76.0 3.4 %shard_map.88 = (f32[6,16,128]{2,1,0:T(8,128)S(1)}, f32[6,16,128]{2,1,0:T(8,128)S(1)}, f32[3,16,128]{2,1,0:T(8,128)S(1)}) custom-call(bf16[2,80,2560]{2,1,0:T(8,128)(2,1)S(1)} %shard_map.86.z, bf16[2,80,2560]{2,1,0:T(8,128)(2,1)} %collective-permute-done.3.v1, bf16[2,80,2560]{2,1,0:T(8,128)(2,1)S(1)} %collective-permute-done.4.vb, ...), custom_call_target="tpu_custom_call" | custom-call | flops 20480000 | bytes 3276800 | tf_op jit(solution)/shard_map/pallas_call | solution.py:201
  79.3 3.7 %collective-permute-start.6 = (f32[6,16,128]{2,1,0:T(8,128)S(1)}, f32[6,16,128]{2,1,0:T(8,128)S(1)}, u32[]{:S(2)}, u32[]{:S(2)}) collective-permute-start(f32[6,16,128]{2,1,0:T(8,128)S(1)} %get-tuple-element.13), channel_id=1, source_target_pairs={{6,2},{10,6},{14,10},{18,14},{22,18},{26,22},{30,26},{34,30},{38,3... | collective-permute-start | bytes 147464 | tf_op jit(solution)/shard_map/ppermute | solution.py:256
  83.0 0.0 copy-start.1
  83.0 1.3 %collective-permute-start.7 = (f32[3,16,128]{2,1,0:T(8,128)S(1)}, f32[3,16,128]{2,1,0:T(8,128)S(1)}, u32[]{:S(2)}, u32[]{:S(2)}) collective-permute-start(f32[3,16,128]{2,1,0:T(8,128)S(1)} %get-tuple-element.14), channel_id=1, source_target_pairs={{6,0},{10,4},{14,8},{18,12},{22,16},{26,20},{30,24},{34,28},{38,32... | collective-permute-start | bytes 73736 | tf_op jit(solution)/shard_map/ppermute | solution.py:257
  84.3 0.9 %collective-permute-done.7.got_c = f32[3,16,128]{2,1,0:T(8,128)S(1)} collective-permute-done((f32[3,16,128]{2,1,0:T(8,128)S(1)}, f32[3,16,128]{2,1,0:T(8,128)S(1)}, u32[]{:S(2)}, u32[]{:S(2)}) %collective-permute-start.7) | collective-permute-done | bytes 24608 | tf_op jit(solution)/shard_map/ppermute | solution.py:257
  85.3 0.0 collective-permute-done.6.got_b
  85.3 0.0 copy-done.1
  85.3 1.2 %shard_map.89 = (f32[1,3,2,16,128]{4,3,2,1,0:T(8,128)}, f32[1,3,16,128]{3,2,1,0:T(8,128)}) custom-call(s32[1,3]{1,0:T(1,128)S(1)} %copy-done.1, f32[6,16,128]{2,1,0:T(8,128)S(1)} %get-tuple-element.12.own, f32[6,16,128]{2,1,0:T(8,128)S(1)} %collective-permute-done.6.got_b, f32[3,16,128]{2,1,0:T(8,128)S(1)} %collective-permute-done.7.got_c), custom_call_target="tpu_custom_call" | custom-call | flops 1000 | bytes 122880 | tf_op jit(solution)/shard_map/pallas_call | solution.py:201
  86.5 0.0 collective-permute-done.2.q_other
  86.5 1.5 %shard_map.87 = f32[1,2,16,128]{3,2,1,0:T(8,128)} custom-call(bf16[2,80,2560]{2,1,0:T(8,128)(2,1)S(1)} %shard_map.86.z, bf16[2048,128]{1,0:T(8,128)(2,1)S(1)} %bitcast.16, bf16[2048,128]{1,0:T(8,128)(2,1)S(1)} %collective-permute-done.2.q_other), custom_call_target="tpu_custom_call" | custom-call | flops 6144000 | bytes 1867776 | tf_op jit(solution)/shard_map/pallas_call | solution.py:201
  (2 shorter events, 0.0 us)
Async XLA Ops:
  0.6 3.3 %copy-start = (bf16[1,2,80,2560]{3,2,1,0:T(8,128)(2,1)S(1)}, bf16[1,2,80,2560]{3,2,1,0:T(8,128)(2,1)}, u32[]{:S(2)}) copy-start(bf16[1,2,80,2560]{3,2,1,0:T(8,128)(2,1)} %param.6) | copy-start | bytes 2457604
  1.8 2.1 %collective-permute-start = (bf16[80,2560]{1,0:T(8,128)(2,1)S(1)}, bf16[80,2560]{1,0:T(8,128)(2,1)S(1)}, u32[]{:S(2)}, u32[]{:S(2)}) collective-permute-start(bf16[80,2560]{1,0:T(8,128)(2,1)S(1)} %dynamic-slice_bitcast_fusion), channel_id=1, source_target_pairs={{0,2},{2,0},{1,3},{3,1},{4,6},{6,4},{5,7},{7,5},{8,10},{10,8},{9,1... | collective-permute-start | bytes 1228808 | tf_op jit(solution)/shard_map/ppermute | solution.py:222
  5.1 27.8 %all-to-all-start = ((bf16[64,32,128]{2,1,0:T(8,128)(2,1)}), bf16[64,32,128]{2,1,0:T(8,128)(2,1)S(1)}, u32[]{:S(2)}, u32[]{:S(2)}) async-start(bf16[64,32,128]{2,1,0:T(8,128)(2,1)} %bitcast.2), calls=%async_computation | async-start | bytes 1048576 | tf_op jit(solution)/shard_map/all_to_all | solution.py:238
  17.8 8.6 %copy-start.4 = (f32[64,8]{1,0:T(8,128)S(1)}, f32[64,8]{1,0:T(8,128)}, u32[]{:S(2)}) copy-start(f32[64,8]{1,0:T(8,128)} %constant.36.clone.table) | copy-start | bytes 6148
  17.8 8.6 %collective-permute-start.1 = (bf16[2,16,2560]{2,1,0:T(8,128)(2,1)S(1)}, bf16[2,16,2560]{2,1,0:T(8,128)(2,1)S(1)}, u32[]{:S(2)}, u32[]{:S(2)}) collective-permute-start(bf16[2,16,2560]{2,1,0:T(8,128)(2,1)S(1)} %slice_select_fusion), channel_id=1, source_target_pairs={{0,1},{1,0},{2,3},{3,2},{4,5},{5,4},{6,7},{7,6},{8,9},{9,8},{10,11... | collective-permute-start | bytes 491528 | tf_op jit(solution)/shard_map/ppermute | solution.py:224
  19.7 6.6 %copy-start.2 = (s32[1,2]{1,0:T(1,128)S(1)}, s32[1,2]{1,0:T(1,128)}, u32[]{:S(2)}) copy-start(s32[1,2]{1,0:T(1,128)} %coarse.1) | copy-start | bytes 28
  19.7 6.6 %copy-start.3 = (s32[1,2]{1,0:T(1,128)S(1)}, s32[1,2]{1,0:T(1,128)}, u32[]{:S(2)}) copy-start(s32[1,2]{1,0:T(1,128)} %fraction.1) | copy-start | bytes 28
  33.8 22.3 %all-to-all-start.1 = ((bf16[64,32,128]{2,1,0:T(8,128)(2,1)}), bf16[64,32,128]{2,1,0:T(8,128)(2,1)S(1)}, u32[]{:S(2)}, u32[]{:S(2)}) async-start(bf16[64,32,128]{2,1,0:T(8,128)(2,1)} %broadcast_in_dim.8), calls=%async_computation.1 | async-start | bytes 1048576 | tf_op jit(solution)/shard_map/all_to_all | solution.py:241
  41.9 34.1 %collective-permute-start.5 = (bf16[2,80,2560]{2,1,0:T(8,128)(2,1)S(1)}, bf16[2,80,2560]{2,1,0:T(8,128)(2,1)S(1)}, u32[]{:S(2)}, u32[]{:S(2)}) collective-permute-start(bf16[2,80,2560]{2,1,0:T(8,128)(2,1)S(1)} %shard_map.86.z), channel_id=1, source_target_pairs={{0,6},{4,10},{8,14},{12,18},{16,22},{20,26},{24,30},{28,34},{32,38... | collective-permute-start | bytes 2457608 | tf_op jit(solution)/shard_map/ppermute | solution.py:248
  43.2 32.8 %collective-permute-start.4 = (bf16[2,80,2560]{2,1,0:T(8,128)(2,1)S(1)}, bf16[2,80,2560]{2,1,0:T(8,128)(2,1)S(1)}, u32[]{:S(2)}, u32[]{:S(2)}) collective-permute-start(bf16[2,80,2560]{2,1,0:T(8,128)(2,1)S(1)} %shard_map.86.z), channel_id=1, source_target_pairs={{4,0},{8,4},{12,8},{16,12},{20,16},{24,20},{28,24},{32,28},{36,32}... | collective-permute-start | bytes 2457608 | tf_op jit(solution)/shard_map/ppermute | solution.py:247
  46.3 29.7 %collective-permute-start.3 = (bf16[2,80,2560]{2,1,0:T(8,128)(2,1)S(1)}, bf16[2,80,2560]{2,1,0:T(8,128)(2,1)}, u32[]{:S(2)}, u32[]{:S(2)}) collective-permute-start(bf16[2,80,2560]{2,1,0:T(8,128)(2,1)S(1)} %shard_map.86.z), channel_id=1, source_target_pairs={{2,0},{4,2},{6,4},{8,6},{10,8},{12,10},{14,12},{16,14},{18,16},{20... | collective-permute-start | bytes 2457608 | tf_op jit(solution)/shard_map/ppermute | solution.py:245
  56.1 30.4 %collective-permute-start.2 = (bf16[2048,128]{1,0:T(8,128)(2,1)S(1)}, bf16[2048,128]{1,0:T(8,128)(2,1)S(1)}, u32[]{:S(2)}, u32[]{:S(2)}) collective-permute-start(bf16[2048,128]{1,0:T(8,128)(2,1)S(1)} %bitcast.15), channel_id=1, source_target_pairs={{0,2},{2,0},{1,3},{3,1},{4,6},{6,4},{5,7},{7,5},{8,10},{10,8},{9,1... | collective-permute-start | bytes 1572872 | tf_op jit(solution)/shard_map/ppermute | solution.py:243
  79.3 5.9 %collective-permute-start.6 = (f32[6,16,128]{2,1,0:T(8,128)S(1)}, f32[6,16,128]{2,1,0:T(8,128)S(1)}, u32[]{:S(2)}, u32[]{:S(2)}) collective-permute-start(f32[6,16,128]{2,1,0:T(8,128)S(1)} %get-tuple-element.13), channel_id=1, source_target_pairs={{6,2},{10,6},{14,10},{18,14},{22,18},{26,22},{30,26},{34,30},{38,3... | collective-permute-start | bytes 147464 | tf_op jit(solution)/shard_map/ppermute | solution.py:256
  83.0 2.2 %copy-start.1 = (s32[1,3]{1,0:T(1,128)S(1)}, s32[1,3]{1,0:T(1,128)}, u32[]{:S(2)}) copy-start(s32[1,3]{1,0:T(1,128)} %on.1) | copy-start | bytes 40
  83.0 2.2 %collective-permute-start.7 = (f32[3,16,128]{2,1,0:T(8,128)S(1)}, f32[3,16,128]{2,1,0:T(8,128)S(1)}, u32[]{:S(2)}, u32[]{:S(2)}) collective-permute-start(f32[3,16,128]{2,1,0:T(8,128)S(1)} %get-tuple-element.14), channel_id=1, source_target_pairs={{6,0},{10,4},{14,8},{18,12},{22,16},{26,20},{30,24},{34,28},{38,32... | collective-permute-start | bytes 73736 | tf_op jit(solution)/shard_map/ppermute | solution.py:257

commit v3 on v0

v3 whole, which is shorter than its diff:
```python
import jax
import jax.numpy as jnp
import ml_dtypes
import numpy as np
from jax import lax
from jax.experimental import pallas as pl
from jax.experimental.pallas import tpu as pltpu
from jax.sharding import Mesh, PartitionSpec as P

NFRAC = 64
SPAN = 3
LOOK_R = 5
LOOK_C = 20
EPS = 1e-06
BF = jnp.bfloat16
F32 = jnp.float32

GRID = (2, 8, 4, 2)
DATE = ("xl", "z", "y", "core")
FAR = ("xl", "z")
NEAR = ("y", "core", "row")

SLAB = 160
WIN = 192
LEAD = 16
LANES = 2 * WIN
SPARE = 190
SLOT = SLAB // LOOK_C


def tap_table():
    x = np.arange(8)[None, :] - 3.0 - np.arange(NFRAC)[:, None] / NFRAC
    w = np.sinc(x) * (0.54 + 0.46 * np.cos(np.pi * x / 4.0))
    taps = (w / w.sum(axis=1, keepdims=True)).astype(np.float32)
    return taps.astype(ml_dtypes.bfloat16).astype(np.float32)


def iota(shape, dim):
    return lax.broadcasted_iota(jnp.int32, shape, dim)


def dot(a, b):
    return jnp.dot(a, b, preferred_element_type=F32)


def row_distance(rows):
    looks = rows // LOOK_R
    out = iota((rows, rows), 0)
    return iota((rows, rows), 1) - (out % looks) * LOOK_R - out // looks


def lane_distance():
    return iota((256, 128), 0) - iota((256, 128), 1)


def band(distance, shift, table, index):
    total = jnp.zeros(distance.shape, F32)
    for k in range(8):
        total = jnp.where(distance == shift + k, table[index, k], total)
    return total.astype(BF)


def filtered(image, row_band, lane_band):
    fit = dot(row_band, image).astype(BF)
    return jnp.concatenate(
        [
            dot(fit[:, :256], lane_band),
            dot(fit[:, 128:], lane_band),
            dot(fit[:, 256:], lane_band[:128]),
        ],
        axis=1,
    )


def crossed(value):
    turned = pltpu.roll(value, WIN, 1)
    return jnp.where(iota(value.shape, 1) < WIN, -turned, turned)


def look_matrix():
    lane = iota((LANES, 128), 0)
    col = jnp.where(lane < WIN, lane, lane - WIN)
    distance = col - LOOK_C * iota((LANES, 128), 1)
    inside = (col < SLAB) & (distance >= 0) & (distance < LOOK_C)
    return jnp.where(inside, 1.0, 0.0).astype(BF)


def looks_of(sums, looks):
    high = sums.astype(BF)
    low = (sums - high.astype(F32)).astype(BF)
    return dot(high, looks) + dot(low, looks)


def row_sum(first, second):
    rows = first.shape[0] // LOOK_R
    total = None
    for j in range(LOOK_R):
        part = first[j * rows : (j + 1) * rows].astype(F32) * second[j * rows : (j + 1) * rows].astype(F32)
        total = part if total is None else total + part
    return total


def pack_kernel(coarse, fraction, x, out, wide):
    _, rows, cols = x.shape
    for p in range(2):
        wide[p, :, :128] = jnp.zeros((rows, 128), BF)
        wide[p, :, 128 + cols :] = jnp.zeros((rows, 128), BF)
        wide[p, :, 128 : 128 + cols] = x[p]
    lane = iota((rows, LANES), 1)
    row = iota((rows, LANES), 0)
    own = jnp.where(row == 0, coarse[0, 0], jnp.where(row == 1, coarse[0, 1], 0))
    own = jnp.where(row == 2, fraction[0, 0], jnp.where(row == 3, fraction[0, 1], own))
    own = own.astype(F32)
    for j in range(out.shape[0]):
        start = 128 + SLAB * j - LEAD
        base, off = start // 128 * 128, start % 128
        first = pltpu.roll(wide[0, :, base : base + LANES].astype(F32), (LANES - off) % LANES, 1)
        second = pltpu.roll(wide[1, :, base : base + LANES].astype(F32), WIN - off, 1)
        value = jnp.where(lane < WIN, first, second)
        out[j] = jnp.where(lane == SPARE, own, value).astype(BF)


def candidate_kernel(image, out):
    rows = image.shape[0]
    order = jnp.where(row_distance(rows) == 0, 1.0, 0.0).astype(BF)
    shift = jnp.where(lane_distance() == LEAD, 1.0, 0.0).astype(BF)
    value = filtered(image[...], order, shift).astype(BF)
    for t in range(LANES // 128):
        out[t * rows : (t + 1) * rows] = value[:, t * 128 : (t + 1) * 128]
    used = LANES // 128 * rows
    out[used:] = jnp.zeros((out.shape[0] - used, 128), BF)


def pair_kernel(offsets, later_offsets, table, images, later, z, out, turned, powers):
    dates, rows, _ = images.shape
    looks = look_matrix()
    rows_apart, lanes_apart = row_distance(rows), lane_distance()

    def resample(images, offsets, base):
        def step(n, carry):
            row_band = band(rows_apart, offsets[n, 0] - 3, table, offsets[n, 2])
            lane_band = band(lanes_apart, LEAD + offsets[n, 1] - 3, table, offsets[n, 3])
            value = filtered(images[n], row_band, lane_band)
            z[base + n] = value.astype(BF)
            turned[base + n] = crossed(value).astype(BF)
            value = z[base + n]
            powers[base + n] = looks_of(row_sum(value, value), looks)
            return carry

        lax.fori_loop(0, images.shape[0], step, 0)

    resample(images, offsets, 0)
    resample(later, later_offsets, dates)
    count = rows // LOOK_R

    def step(n, carry):
        first = z[n]
        sums = []
        for s in range(SPAN):
            sums.append(row_sum(first, z[n + s + 1]))
            sums.append(row_sum(first, turned[n + s + 1]))
        maps = looks_of(jnp.concatenate(sums, axis=0), looks)
        total = jnp.zeros((count, 128), F32)
        for i in range(2 * SPAN):
            total = total + pltpu.roll(maps[i * count : (i + 1) * count], SLOT * (2 + i), 1)
        for i in range(SPAN + 1):
            total = total + pltpu.roll(powers[n + i], SLOT * (2 + 2 * SPAN + i), 1)
        out[n] = total
        return carry

    lax.fori_loop(0, dates, step, 0)


def reference_kernel(part, z, q, out, first, second):
    dates, count, _ = part.shape
    rows = z.shape[1]
    looks = look_matrix()
    value = jnp.concatenate(
        [q[t * rows : (t + 1) * rows].astype(F32) for t in range(LANES // 128)], axis=1
    )
    first[...] = value.astype(BF)
    second[...] = crossed(value).astype(BF)

    def step(n, carry):
        image = z[n]
        sums = [row_sum(image, first[...]), row_sum(image, second[...])]
        maps = looks_of(jnp.concatenate(sums, axis=0), looks)
        out[n] = part[n] + maps[:count] + pltpu.roll(maps[count:], SLOT, 1)
        return carry

    lax.fori_loop(0, dates, step, 0)


def finish_kernel(on, got, ref_ifg, pair_ifg, coherence):
    slabs, count, _ = got.shape
    date, dates = lax.axis_index(DATE), lax.axis_size(DATE)
    slab = iota((count, 128), 1) // SLOT

    def gathered(m):
        total = jnp.zeros((count, 128), F32)
        for j in range(slabs):
            moved = pltpu.roll(got[j], SLOT * ((j - m) % slabs), 1)
            total = jnp.where(slab == j, moved, total)
        return total * (1.0 / (LOOK_R * LOOK_C))

    ref_ifg[0, 0] = gathered(0)
    ref_ifg[0, 1] = gathered(1)
    own = jnp.sqrt(gathered(2 + 2 * SPAN) + EPS)
    for s in range(SPAN):
        usable = (on[0, s] == 1) & (date + s + 1 < dates)
        re, im = gathered(2 + 2 * s), gathered(3 + 2 * s)
        other = jnp.sqrt(gathered(3 + 2 * SPAN + s) + EPS)
        coh = jnp.sqrt(re * re + im * im) / (own * other)
        pair_ifg[0, s, 0] = jnp.where(usable, re, 0.0)
        pair_ifg[0, s, 1] = jnp.where(usable, im, 0.0)
        coherence[0, s] = jnp.where(usable, coh, 0.0)


SMEM = pl.BlockSpec(memory_space=pltpu.SMEM)
VMEM = pl.BlockSpec(memory_space=pltpu.VMEM)


def call(kernel, scalars, arrays, outs, flops, scratch=()):
    moved = sum(a.size * a.dtype.itemsize for a in arrays)
    out_shape = [jax.ShapeDtypeStruct(s, d) for s, d in outs]
    single = len(out_shape) == 1
    return pl.pallas_call(
        kernel,
        out_shape=out_shape[0] if single else out_shape,
        in_specs=[SMEM] * len(scalars) + [VMEM] * len(arrays),
        out_specs=VMEM if single else [VMEM] * len(out_shape),
        scratch_shapes=list(scratch),
        compiler_params=pltpu.CompilerParams(vmem_limit_bytes=40 * 2**20),
        cost_estimate=pl.CostEstimate(flops=flops, bytes_accessed=moved, transcendentals=0),
    )(*scalars, *arrays)


def on_device(table, slc, coarse, fraction, pair_on, ref_date):
    x = slc[0]
    _, rows, cols = x.shape
    members = lax.axis_size("y") * lax.axis_size("core")
    halves = lax.axis_size("row")
    slabs = members * halves
    groups = lax.axis_size(FAR)
    all_rows = rows * halves
    count = all_rows // LOOK_R
    ref = ref_date[0]

    packed = call(
        pack_kernel, [coarse, fraction], [x], [((slabs, rows, LANES), BF)], 10**8,
        [pltpu.VMEM((2, rows, cols + 256), BF)],
    )
    images = lax.all_to_all(packed, NEAR, 0, 0).reshape(members, all_rows, LANES)

    later = lax.ppermute(images[:SPAN], FAR, [(i + 1, i) for i in range(groups - 1)])

    tiles = LANES // 128 * all_rows
    piece = -(-tiles // (16 * groups)) * 16
    cand = lax.dynamic_index_in_dim(images, ref % members, 0, keepdims=False)
    cand = call(candidate_kernel, [], [cand], [((groups * piece, 128), BF)], 10**8)
    got = lax.all_to_all(cand.reshape(groups, piece, 128), FAR, 0, 0)
    got = lax.dynamic_index_in_dim(got, ref // members, 0)
    q = lax.all_to_all(jnp.broadcast_to(got, (groups, piece, 128)), FAR, 0, 0)
    q = q.reshape(groups * piece, 128)

    offsets = images[:, :4, SPARE].astype(jnp.int32)
    later_offsets = later[:, :4, SPARE].astype(jnp.int32)
    held = (members + SPAN, all_rows, LANES)
    z, part = call(
        pair_kernel, [offsets, later_offsets, table], [images, later],
        [(held, BF), ((members, count, 128), F32)], 4 * 10**9,
        [pltpu.VMEM(held, BF), pltpu.VMEM((members + SPAN, count, 128), F32)],
    )
    maps = call(
        reference_kernel, [], [part, z, q], [((members, count, 128), F32)], 10**9,
        [pltpu.VMEM((all_rows, LANES), BF)] * 2,
    )
    got = lax.all_to_all(maps.reshape(slabs, count // halves, 128), NEAR, 0, 0)
    small = (count // halves, 128)
    return call(
        finish_kernel, [pair_on], [got],
        [((1, 2) + small, F32), ((1, SPAN, 2) + small, F32), ((1, SPAN) + small, F32)], 10**7,
    )


def solution(mesh):
    shape = GRID + (mesh.shape["row"],)
    grid = Mesh(mesh.devices.reshape(shape), DATE + ("row",))
    table = tap_table()

    def program(slc, coarse, fraction, pair_on, ref_date):
        return tuple(
            jax.shard_map(
                on_device,
                mesh=grid,
                in_specs=(
                    P(),
                    P(DATE, None, "row", None),
                    P(DATE, None),
                    P(DATE, None),
                    P(DATE, None),
                    P(),
                ),
                out_specs=(
                    P(DATE, None, "row", None),
                    P(DATE, None, None, "row", None),
                    P(DATE, None, "row", None),
                ),
                check_vma=False,
            )(jnp.asarray(table), slc, coarse, fraction, pair_on, ref_date)
        )

    return program
```

time: 1210 us -> 82.6 us (0.07)
  waiting for transfers between devices: 1020 us -> 21.5 us
  local copies, waits for them, and re-layouts: 95.9 us -> 3.37 us
  other arithmetic: 54.5 us -> 0.3 us
  between operations: 19.6 us -> 1.43 us
  Pallas kernels: 0 us -> 16.7 us
  blocking collectives: 0 us -> 14.1 us
    psum x1 -> x0, waiting for transfers between devices: 1020 us -> none  [broadcast(): return lax.psum(kept, axis)]
    add x8 -> x0, local copies, waits for them, and re-layouts: 62.6 us -> none  [the longest x3 23.8 us: pair_terms(): power_two = multilook(v_real * v_real + v_imag * v_imag)]
    reduce_sum x16 -> x0, other arithmetic: 40.3 us -> none  [the longest x12 35.1 us: multilook(): return jnp.mean(shaped, axis=(-3, -1))]
    sub x4 -> x0, local copies, waits for them, and re-layouts: 31.5 us -> none  [the longest x3 23.4 us: pair_terms(): imag_part = multilook(z_imag * v_real - z_real * v_imag)]
    all_to_all x0 -> x3, starting transfers between devices: none -> 23.4 us  [the longest x1 9.19 us: on_device(): got = lax.all_to_all(cand.reshape(groups, piece, 128), FAR, 0, 0)]
    all_to_all x0 -> x3, waiting for transfers between devices: none -> 21.5 us  [the longest x1 14.2 us: on_device(): lax.all_to_all(packed, NEAR, 0, 0).reshape(members, all_rows, LANES)]
    pallas_call x0 -> x5, Pallas kernels: none -> 16.7 us  [call(): pl.pallas_call(kernel, out_shape=out_shape[0] if single else out_shape, i...]
    all_to_all x0 -> x1, blocking collectives: none -> 14.1 us  [on_device(): got = lax.all_to_all(maps.reshape(slabs, count // halves, 128), NEAR, 0, 0)]
  transfers between devices with their start and end apart: 6 -> 4, of which waited for: 1 -> 2; matrix products, arithmetic and copies ran while one was open for 7% -> 1% of each run, Pallas kernels for 0% -> 13%
where the time goes in v3:
time: 82.6 us; the launch traced here: 82.1 us
  starting transfers between devices  24.7 us (30%)
  waiting for transfers between devices  21.5 us (26%)
  Pallas kernels  16.7 us (20%)
  blocking collectives  14.1 us (17%)
  local copies, waits for them, and re-layouts  3.37 us (4%)
  between operations  1.43 us (2%)
    pallas_call x5, Pallas kernels, call(): pl.pallas_call(kernel, out_shape=out_shape[0] if single else out_shape, i...  16.7 us
    all_to_all x1, waiting for transfers between devices, on_device(): lax.all_to_all(packed, NEAR, 0, 0).reshape(members, all_rows, LANES)  14.2 us
    all_to_all x1, blocking collectives, on_device(): got = lax.all_to_all(maps.reshape(slabs, count // halves, 128), NEAR, 0, 0)  14.1 us
    all_to_all x1, starting transfers between devices, on_device(): got = lax.all_to_all(cand.reshape(groups, piece, 128), FAR, 0, 0)  9.19 us
    all_to_all x1, starting transfers between devices, on_device(): lax.all_to_all(packed, NEAR, 0, 0).reshape(members, all_rows, LANES)  8.45 us
    all_to_all x1, waiting for transfers between devices, on_device(): got = lax.all_to_all(cand.reshape(groups, piece, 128), FAR, 0, 0)  7.32 us
    all_to_all x1, starting transfers between devices, on_device(): q = lax.all_to_all(jnp.broadcast_to(got, (groups, piece, 128)), FAR, 0, 0)  5.75 us
    unnamed x10, local copies, waits for them, and re-layouts  2.46 us
  transfers between devices with their start and end apart: 4, of which 2 were waited for; matrix products, arithmetic and copies ran while one was open for 1% of the time, Pallas kernels for 13%

profile of v3, /device:TPU:1, one launch (start us, length us, event | category | flops | bytes accessed | tf_op | source)
XLA Modules:
  0.0 82.1 jit_solution(14129435106734966020)
XLA Ops:
  0.6 0.0 copy-start
  0.6 1.1 %copy-done = bf16[1,2,80,2560]{3,2,1,0:T(8,128)(2,1)S(1)} copy-done((bf16[1,2,80,2560]{3,2,1,0:T(8,128)(2,1)S(1)}, bf16[1,2,80,2560]{3,2,1,0:T(8,128)(2,1)}, u32[]{:S(2)}) %copy-start) | copy-done | bytes 819224
  1.8 0.0 copy-start.1
  1.8 0.7 copy-done.1
  2.4 0.0 copy-start.2
  2.4 0.7 copy-done.2
  3.1 2.1 %shard_map.85 = bf16[16,80,384]{2,1,0:T(8,128)(2,1)} custom-call(s32[1,2]{1,0:T(1,128)S(1)} %copy-done.1, s32[1,2]{1,0:T(1,128)S(1)} %copy-done.2, bf16[2,80,2560]{2,1,0:T(8,128)(2,1)S(1)} %bitcast.19), custom_call_target="tpu_custom_call" | custom-call | flops 100000000 | bytes 819200 | tf_op jit(solution)/shard_map/pallas_call | solution.py:227
  5.2 8.4 %all-to-all-start = ((bf16[16,80,384]{2,1,0:T(8,128)(2,1)}), bf16[16,80,384]{2,1,0:T(8,128)(2,1)S(1)}, u32[]{:S(2)}, u32[]{:S(2)}) async-start(bf16[16,80,384]{2,1,0:T(8,128)(2,1)} %shard_map.85), calls=%async_computation | async-start | bytes 1966080 | tf_op jit(solution)/shard_map/all_to_all | solution.py:253
  13.7 0.0 copy-start.4
  14.4 14.2 %all-to-all-done = bf16[16,80,384]{2,1,0:T(8,128)(2,1)S(1)} async-done(((bf16[16,80,384]{2,1,0:T(8,128)(2,1)}), bf16[16,80,384]{2,1,0:T(8,128)(2,1)S(1)}, u32[]{:S(2)}, u32[]{:S(2)}) %all-to-all-start) | async-done | bytes 983072 | tf_op jit(solution)/shard_map/all_to_all | solution.py:253
  28.6 1.3 %collective-permute-start = (bf16[3,160,384]{2,1,0:T(8,128)(2,1)S(1)}, bf16[3,160,384]{2,1,0:T(8,128)(2,1)S(1)}, u32[]{:S(2)}, u32[]{:S(2)}) collective-permute-start(bf16[3,160,384]{2,1,0:T(8,128)(2,1)S(1)} %bitcast.22), channel_id=1, source_target_pairs={{16,0},{32,16},{48,32},{64,48},{80,64},{96,80},{112,96},{128,112},... | collective-permute-start | bytes 1105928 | tf_op jit(solution)/shard_map/ppermute | solution.py:255
  29.9 1.0 %shard_map.87 = bf16[512,128]{1,0:T(8,128)(2,1)} custom-call(bf16[160,384]{1,0:T(8,128)(2,1)S(1)} %dynamic-slice_bitcast_fusion.image), custom_call_target="tpu_custom_call" | custom-call | flops 100000000 | bytes 122880 | tf_op jit(solution)/shard_map/pallas_call | solution.py:227
  30.9 9.2 %all-to-all-start.1 = ((bf16[16,32,128]{2,1,0:T(8,128)(2,1)}), bf16[16,32,128]{2,1,0:T(8,128)(2,1)S(1)}, u32[]{:S(2)}, u32[]{:S(2)}) async-start(bf16[16,32,128]{2,1,0:T(8,128)(2,1)} %bitcast.6), calls=%async_computation.1 | async-start | bytes 262144 | tf_op jit(solution)/shard_map/all_to_all | solution.py:261
  40.1 0.1 slice_convert_fusion
  40.2 0.1 copy.13
  40.3 0.1 copy.14.offsets
  40.4 7.3 %all-to-all-done.1 = bf16[16,32,128]{2,1,0:T(8,128)(2,1)S(1)} async-done(((bf16[16,32,128]{2,1,0:T(8,128)(2,1)}), bf16[16,32,128]{2,1,0:T(8,128)(2,1)S(1)}, u32[]{:S(2)}, u32[]{:S(2)}) %all-to-all-start.1) | async-done | bytes 131104 | tf_op jit(solution)/shard_map/all_to_all | solution.py:261
  47.7 0.7 broadcast_in_dim.8
  48.4 5.7 %all-to-all-start.2 = ((bf16[16,32,128]{2,1,0:T(8,128)(2,1)}), bf16[16,32,128]{2,1,0:T(8,128)(2,1)S(1)}, u32[]{:S(2)}, u32[]{:S(2)}) async-start(bf16[16,32,128]{2,1,0:T(8,128)(2,1)} %broadcast_in_dim.8), calls=%async_computation.2 | async-start | bytes 262144 | tf_op jit(solution)/shard_map/all_to_all | solution.py:263
  54.1 0.0 collective-permute-done.later
  54.1 0.2 convert_reduce_fusion.later_offsets
  54.4 0.0 copy-done.4
  54.4 9.8 %shard_map.86 = (bf16[11,160,384]{2,1,0:T(8,128)(2,1)S(1)}, f32[8,32,128]{2,1,0:T(8,128)S(1)}) custom-call(s32[8,4]{1,0:T(8,128)S(1)} %copy.14.offsets, s32[3,4]{1,0:T(4,128)S(1)} %convert_reduce_fusion.later_offsets, f32[64,8]{1,0:T(8,128)S(1)} %copy-done.4, bf16[8,160,384]{2,1,0:T(8,128)(2,1)S(1)} %bitcast.18, ...), custom_call_target="tpu_custom_call" | custom-call | flops 4000000000 | bytes 1351680 | tf_op jit(solution)/shard_map/pallas_call | solution.py:227
  64.2 0.0 all-to-all-done.2
  64.2 0.0 copy-start.3
  64.2 2.2 %shard_map.88 = f32[8,32,128]{2,1,0:T(8,128)S(1)} custom-call(f32[8,32,128]{2,1,0:T(8,128)S(1)} %get-tuple-element.5.part, bf16[11,160,384]{2,1,0:T(8,128)(2,1)S(1)} %get-tuple-element.6.z, bf16[512,128]{1,0:T(8,128)(2,1)S(1)} %bitcast.20), custom_call_target="tpu_custom_call" | custom-call | flops 1000000000 | bytes 1613824 | tf_op jit(solution)/shard_map/pallas_call | solution.py:227
  66.4 14.1 %all_to_all.20.got = f32[16,16,128]{2,1,0:T(8,128)S(1)} all-to-all(f32[16,16,128]{2,1,0:T(8,128)S(1)} %bitcast.21), channel_id=1, replica_groups=mesh['xl'=2,'z'=8,'y'=4,'core'=2,'row'=2] {'y','core','row'}, dimensions={0} | all-to-all | bytes 262144 | tf_op jit(solution)/shard_map/all_to_all | solution.py:278
  80.5 0.0 copy-done.3
  80.5 1.6 %shard_map.89 = (f32[1,2,16,128]{3,2,1,0:T(8,128)}, f32[1,3,2,16,128]{4,3,2,1,0:T(8,128)}, f32[1,3,16,128]{3,2,1,0:T(8,128)}) custom-call(s32[1,3]{1,0:T(1,128)S(1)} %copy-done.3, f32[16,16,128]{2,1,0:T(8,128)S(1)} %all_to_all.20.got), custom_call_target="tpu_custom_call" | custom-call | flops 10000000 | bytes 131072 | tf_op jit(solution)/shard_map/pallas_call | solution.py:227
  (3 shorter events, 0.1 us)
Async XLA Ops:
  0.6 1.1 %copy-start = (bf16[1,2,80,2560]{3,2,1,0:T(8,128)(2,1)S(1)}, bf16[1,2,80,2560]{3,2,1,0:T(8,128)(2,1)}, u32[]{:S(2)}) copy-start(bf16[1,2,80,2560]{3,2,1,0:T(8,128)(2,1)} %param.6) | copy-start | bytes 2457604
  1.8 0.7 copy-start.1
  2.4 0.7 copy-start.2
  5.2 23.3 %all-to-all-start = ((bf16[16,80,384]{2,1,0:T(8,128)(2,1)}), bf16[16,80,384]{2,1,0:T(8,128)(2,1)S(1)}, u32[]{:S(2)}, u32[]{:S(2)}) async-start(bf16[16,80,384]{2,1,0:T(8,128)(2,1)} %shard_map.85), calls=%async_computation | async-start | bytes 1966080 | tf_op jit(solution)/shard_map/all_to_all | solution.py:253
  13.7 40.7 %copy-start.4 = (f32[64,8]{1,0:T(8,128)S(1)}, f32[64,8]{1,0:T(8,128)}, u32[]{:S(2)}) copy-start(f32[64,8]{1,0:T(8,128)} %constant.37.clone.table) | copy-start | bytes 6148
  28.6 25.5 %collective-permute-start = (bf16[3,160,384]{2,1,0:T(8,128)(2,1)S(1)}, bf16[3,160,384]{2,1,0:T(8,128)(2,1)S(1)}, u32[]{:S(2)}, u32[]{:S(2)}) collective-permute-start(bf16[3,160,384]{2,1,0:T(8,128)(2,1)S(1)} %bitcast.22), channel_id=1, source_target_pairs={{16,0},{32,16},{48,32},{64,48},{80,64},{96,80},{112,96},{128,112},... | collective-permute-start | bytes 1105928 | tf_op jit(solution)/shard_map/ppermute | solution.py:255
  30.9 16.8 %all-to-all-start.1 = ((bf16[16,32,128]{2,1,0:T(8,128)(2,1)}), bf16[16,32,128]{2,1,0:T(8,128)(2,1)S(1)}, u32[]{:S(2)}, u32[]{:S(2)}) async-start(bf16[16,32,128]{2,1,0:T(8,128)(2,1)} %bitcast.6), calls=%async_computation.1 | async-start | bytes 262144 | tf_op jit(solution)/shard_map/all_to_all | solution.py:261
  48.4 15.8 %all-to-all-start.2 = ((bf16[16,32,128]{2,1,0:T(8,128)(2,1)}), bf16[16,32,128]{2,1,0:T(8,128)(2,1)S(1)}, u32[]{:S(2)}, u32[]{:S(2)}) async-start(bf16[16,32,128]{2,1,0:T(8,128)(2,1)} %broadcast_in_dim.8), calls=%async_computation.2 | async-start | bytes 262144 | tf_op jit(solution)/shard_map/all_to_all | solution.py:263
  64.2 16.3 %copy-start.3 = (s32[1,3]{1,0:T(1,128)S(1)}, s32[1,3]{1,0:T(1,128)}, u32[]{:S(2)}) copy-start(s32[1,3]{1,0:T(1,128)} %on.1) | copy-start | bytes 40

commit v4 on v3

--- a/solution.py
+++ b/solution.py
@@ -100,16 +100,25 @@
     return total
 
 
-def pack_kernel(coarse, fraction, x, out, wide):
-    _, rows, cols = x.shape
+def pack_kernel(coarse, fraction, x, out, wide, shifts, taps, image_sem, small_sem):
+    _, _, rows, cols = x.shape
+    copies = [
+        pltpu.make_async_copy(x.at[0, p], wide.at[p, :, pl.ds(128, cols)], image_sem.at[p])
+        for p in range(2)
+    ]
+    copies.append(pltpu.make_async_copy(coarse, shifts, small_sem.at[0]))
+    copies.append(pltpu.make_async_copy(fraction, taps, small_sem.at[1]))
+    for copy in copies:
+        copy.start()
     for p in range(2):
         wide[p, :, :128] = jnp.zeros((rows, 128), BF)
         wide[p, :, 128 + cols :] = jnp.zeros((rows, 128), BF)
-        wide[p, :, 128 : 128 + cols] = x[p]
     lane = iota((rows, LANES), 1)
     row = iota((rows, LANES), 0)
-    own = jnp.where(row == 0, coarse[0, 0], jnp.where(row == 1, coarse[0, 1], 0))
-    own = jnp.where(row == 2, fraction[0, 0], jnp.where(row == 3, fraction[0, 1], own))
+    for copy in copies:
+        copy.wait()
+    own = jnp.where(row == 0, shifts[0, 0], jnp.where(row == 1, shifts[0, 1], 0))
+    own = jnp.where(row == 2, taps[0, 0], jnp.where(row == 3, taps[0, 1], own))
     own = own.astype(F32)
     for j in range(out.shape[0]):
         start = 128 + SLAB * j - LEAD
@@ -131,64 +140,77 @@
     out[used:] = jnp.zeros((out.shape[0] - used, 128), BF)
 
 
-def pair_kernel(offsets, later_offsets, table, images, later, z, out, turned, powers):
+def resampled(image, offsets, n, table, rows_apart, lanes_apart):
+    row_band = band(rows_apart, offsets[n, 0] - 3, table, offsets[n, 2])
+    lane_band = band(lanes_apart, LEAD + offsets[n, 1] - 3, table, offsets[n, 3])
+    return filtered(image, row_band, lane_band)
+
+
+def pair_looks(first, partners, looks):
+    sums = []
+    for _, image, turned, _ in partners:
+        sums.append(row_sum(first, image))
+        sums.append(row_sum(first, turned))
+    maps = looks_of(jnp.concatenate(sums, axis=0), looks)
+    count = sums[0].shape[0]
+    total = jnp.zeros((count, 128), F32)
+    for i, (s, _, _, power) in enumerate(partners):
+        for c in range(2):
+            one = maps[(2 * i + c) * count : (2 * i + c + 1) * count]
+            total = total + pltpu.roll(one, SLOT * (2 + 2 * s + c), 1)
+        total = total + pltpu.roll(power, SLOT * (3 + 2 * SPAN + s), 1)
+    return total
+
+
+def own_kernel(offsets, table, images, z, out, turned, powers):
     dates, rows, _ = images.shape
     looks = look_matrix()
     rows_apart, lanes_apart = row_distance(rows), lane_distance()
-
-    def resample(images, offsets, base):
-        def step(n, carry):
-            row_band = band(rows_apart, offsets[n, 0] - 3, table, offsets[n, 2])
-            lane_band = band(lanes_apart, LEAD + offsets[n, 1] - 3, table, offsets[n, 3])
-            value = filtered(images[n], row_band, lane_band)
-            z[base + n] = value.astype(BF)
-            turned[base + n] = crossed(value).astype(BF)
-            value = z[base + n]
-            powers[base + n] = looks_of(row_sum(value, value), looks)
-            return carry
-
-        lax.fori_loop(0, images.shape[0], step, 0)
-
-    resample(images, offsets, 0)
-    resample(later, later_offsets, dates)
-    count = rows // LOOK_R
-
-    def step(n, carry):
-        first = z[n]
-        sums = []
-        for s in range(SPAN):
-            sums.append(row_sum(first, z[n + s + 1]))
-            sums.append(row_sum(first, turned[n + s + 1]))
-        maps = looks_of(jnp.concatenate(sums, axis=0), looks)
-        total = jnp.zeros((count, 128), F32)
-        for i in range(2 * SPAN):
-            total = total + pltpu.roll(maps[i * count : (i + 1) * count], SLOT * (2 + i), 1)
-        for i in range(SPAN + 1):
-            total = total + pltpu.roll(powers[n + i], SLOT * (2 + 2 * SPAN + i), 1)
+    for n in range(dates):
+        value = resampled(images[n], offsets, n, table, rows_apart, lanes_apart)
+        z[n] = value.astype(BF)
+        turned[n] = crossed(value).astype(BF)
+        powers[n] = looks_of(row_sum(z[n], z[n]), looks)
+    for n in range(dates):
+        total = pltpu.roll(powers[n], SLOT * (2 + 2 * SPAN), 1)
+        spans = [s for s in range(SPAN) if n + s + 1 < dates]
+        if spans:
+            partners = [(s, z[n + s + 1], turned[n + s + 1], powers[n + s + 1]) for s in spans]
+            total = total + pair_looks(z[n], partners, looks)
         out[n] = total
-        return carry
-
-    lax.fori_loop(0, dates, step, 0)
-
-
-def reference_kernel(part, z, q, out, first, second):
-    dates, count, _ = part.shape
+
+
+def later_kernel(offsets, table, later, z, out):
+    dates, rows, _ = later.shape
+    looks = look_matrix()
+    rows_apart, lanes_apart = row_distance(rows), lane_distance()
+    found = []
+    for n in range(dates):
+        value = resampled(later[n], offsets, n, table, rows_apart, lanes_apart)
+        image = value.astype(BF)
+        power = looks_of(row_sum(image, image), looks)
+        found.append((image, crossed(value).astype(BF), power))
+    for n in range(dates):
+        partners = [(m - n + dates - 1,) + found[m] for m in range(n + 1)]
+        out[n] = pair_looks(z[n], partners, looks)
+
+
+def reference_kernel(part, later_part, z, q, out):
+    dates = part.shape[0]
     rows = z.shape[1]
     looks = look_matrix()
     value = jnp.concatenate(
         [q[t * rows : (t + 1) * rows].astype(F32) for t in range(LANES // 128)], axis=1
     )
-    first[...] = value.astype(BF)
-    second[...] = crossed(value).astype(BF)
-
-    def step(n, carry):
-        image = z[n]
-        sums = [row_sum(image, first[...]), row_sum(image, second[...])]
-        maps = looks_of(jnp.concatenate(sums, axis=0), looks)
-        out[n] = part[n] + maps[:count] + pltpu.roll(maps[count:], SLOT, 1)
-        return carry
-
-    lax.fori_loop(0, dates, step, 0)
+    turned = crossed(value).astype(BF)
+    value = value.astype(BF)
+    for n in range(dates):
+        maps = looks_of(jnp.concatenate([row_sum(z[n], value), row_sum(z[n], turned)], axis=0), looks)
+        count = maps.shape[0] // 2
+        total = part[n] + maps[:count] + pltpu.roll(maps[count:], SLOT, 1)
+        if n >= dates - SPAN:
+            total = total + later_part[n - dates + SPAN]
+        out[n] = total
 
 
 def finish_kernel(on, got, ref_ifg, pair_ifg, coherence):
@@ -236,8 +258,7 @@
 
 
 def on_device(table, slc, coarse, fraction, pair_on, ref_date):
-    x = slc[0]
-    _, rows, cols = x.shape
+    _, _, rows, cols = slc.shape
     members = lax.axis_size("y") * lax.axis_size("core")
     halves = lax.axis_size("row")
     slabs = members * halves
@@ -246,34 +267,49 @@
     count = all_rows // LOOK_R
     ref = ref_date[0]
 
-    packed = call(
-        pack_kernel, [coarse, fraction], [x], [((slabs, rows, LANES), BF)], 10**8,
-        [pltpu.VMEM((2, rows, cols + 256), BF)],
-    )
+    anywhere = pl.BlockSpec(memory_space=pl.ANY)
+    packed = pl.pallas_call(
+        pack_kernel,
+        out_shape=jax.ShapeDtypeStruct((slabs, rows, LANES), BF),
+        in_specs=[anywhere] * 3,
+        out_specs=VMEM,
+        scratch_shapes=[
+            pltpu.VMEM((2, rows, cols + 256), BF),
+            pltpu.SMEM((1, 2), jnp.int32),
+            pltpu.SMEM((1, 2), jnp.int32),
+            pltpu.SemaphoreType.DMA((2,)),
+            pltpu.SemaphoreType.DMA((2,)),
+        ],
+        compiler_params=pltpu.CompilerParams(vmem_limit_bytes=60 * 2**20),
+        cost_estimate=pl.CostEstimate(flops=10**8, bytes_accessed=2 * 10**6, transcendentals=0),
+    )(coarse, fraction, slc)
     images = lax.all_to_all(packed, NEAR, 0, 0).reshape(members, all_rows, LANES)
-
-    later = lax.ppermute(images[:SPAN], FAR, [(i + 1, i) for i in range(groups - 1)])
 
     tiles = LANES // 128 * all_rows
     piece = -(-tiles // (16 * groups)) * 16
     cand = lax.dynamic_index_in_dim(images, ref % members, 0, keepdims=False)
     cand = call(candidate_kernel, [], [cand], [((groups * piece, 128), BF)], 10**8)
     got = lax.all_to_all(cand.reshape(groups, piece, 128), FAR, 0, 0)
+    offsets = images[:, :4, SPARE].astype(jnp.int32)
+    z, part = call(
+        own_kernel, [offsets, table], [images],
+        [(images.shape, BF), ((members, count, 128), F32)], 4 * 10**9,
+        [pltpu.VMEM(images.shape, BF), pltpu.VMEM((members, count, 128), F32)],
+    )
+    got, z = lax.optimization_barrier((got, z))
+    later = lax.ppermute(images[:SPAN], FAR, [(i + 1, i) for i in range(groups - 1)])
+
     got = lax.dynamic_index_in_dim(got, ref // members, 0)
     q = lax.all_to_all(jnp.broadcast_to(got, (groups, piece, 128)), FAR, 0, 0)
     q = q.reshape(groups * piece, 128)
 
-    offsets = images[:, :4, SPARE].astype(jnp.int32)
     later_offsets = later[:, :4, SPARE].astype(jnp.int32)
-    held = (members + SPAN, all_rows, LANES)
-    z, part = call(
-        pair_kernel, [offsets, later_offsets, table], [images, later],
-        [(held, BF), ((members, count, 128), F32)], 4 * 10**9,
-        [pltpu.VMEM(held, BF), pltpu.VMEM((members + SPAN, count, 128), F32)],
+    later_part = call(
+        later_kernel, [later_offsets, table], [later, z[members - SPAN :]],
+        [((SPAN, count, 128), F32)], 2 * 10**9,
     )
     maps = call(
-        reference_kernel, [], [part, z, q], [((members, count, 128), F32)], 10**9,
-        [pltpu.VMEM((all_rows, LANES), BF)] * 2,
+        reference_kernel, [], [part, later_part, z, q], [((members, count, 128), F32)], 10**9
     )
     got = lax.all_to_all(maps.reshape(slabs, count // halves, 128), NEAR, 0, 0)
     small = (count // halves, 128)

time: 82.6 us -> 77.4 us (0.937)
  Pallas kernels: 16.7 us -> 14.1 us
  local copies, waits for them, and re-layouts: 3.37 us -> 0.97 us
  waiting for transfers between devices: 21.5 us -> 19.4 us
  blocking collectives: 14.1 us -> 15.1 us
  starting transfers between devices: 24.7 us -> 25.6 us
    all_to_all x1, waiting for transfers between devices: 7.32 us -> 0.87 us  [on_device(): got = lax.all_to_all(cand.reshape(groups, piece, 128), FAR, 0, 0)]
    pallas_call x5, Pallas kernels: 16.7 us -> 11.4 us  [call(): pl.pallas_call(kernel, out_shape=out_shape[0] if single else out_shape, i...]
    all_to_all x1, waiting for transfers between devices: 0.01 us -> 4.33 us  [on_device(): q = lax.all_to_all(jnp.broadcast_to(got, (groups, piece, 128)), FAR, 0, 0)]
    pallas_call x0 -> x1, Pallas kernels: none -> 2.72 us  [on_device(): pl.pallas_call(pack_kernel, out_shape=jax.ShapeDtypeStruct((slabs, rows,...]
    unnamed x10 -> x4, local copies, waits for them, and re-layouts: 2.46 us -> 0.01 us
    all_to_all x1, starting transfers between devices: 5.75 us -> 7.6 us  [on_device(): q = lax.all_to_all(jnp.broadcast_to(got, (groups, piece, 128)), FAR, 0, 0)]
    all_to_all x1, blocking collectives: 14.1 us -> 15.1 us  [on_device(): got = lax.all_to_all(maps.reshape(slabs, count // halves, 128), NEAR, 0, 0)]
    all_to_all x1, starting transfers between devices: 9.19 us -> 8.29 us  [on_device(): got = lax.all_to_all(cand.reshape(groups, piece, 128), FAR, 0, 0)]
  transfers between devices with their start and end apart: 4 -> 4, of which waited for: 2 -> 3; matrix products, arithmetic and copies ran while one was open for 1% -> 1% of each run, Pallas kernels for 13% -> 10%
where the time goes in v4:
time: 77.4 us; the launch traced here: 76.9 us
  starting transfers between devices  25.6 us (33%)
  waiting for transfers between devices  19.4 us (25%)
  blocking collectives  15.1 us (20%)
  Pallas kernels  14.1 us (18%)
  between operations  1.42 us (2%)
  local copies, waits for them, and re-layouts  0.97 us (1%)
    all_to_all x1, blocking collectives, on_device(): got = lax.all_to_all(maps.reshape(slabs, count // halves, 128), NEAR, 0, 0)  15.1 us
    all_to_all x1, waiting for transfers between devices, on_device(): lax.all_to_all(packed, NEAR, 0, 0).reshape(members, all_rows, LANES)  14.2 us
    pallas_call x5, Pallas kernels, call(): pl.pallas_call(kernel, out_shape=out_shape[0] if single else out_shape, i...  11.4 us
    all_to_all x1, starting transfers between devices, on_device(): lax.all_to_all(packed, NEAR, 0, 0).reshape(members, all_rows, LANES)  8.46 us
    all_to_all x1, starting transfers between devices, on_device(): got = lax.all_to_all(cand.reshape(groups, piece, 128), FAR, 0, 0)  8.29 us
    all_to_all x1, starting transfers between devices, on_device(): q = lax.all_to_all(jnp.broadcast_to(got, (groups, piece, 128)), FAR, 0, 0)  7.6 us
    all_to_all x1, waiting for transfers between devices, on_device(): q = lax.all_to_all(jnp.broadcast_to(got, (groups, piece, 128)), FAR, 0, 0)  4.33 us
    pallas_call x1, Pallas kernels, on_device(): pl.pallas_call(pack_kernel, out_shape=jax.ShapeDtypeStruct((slabs, rows,...  2.72 us
  transfers between devices with their start and end apart: 4, of which 3 were waited for; matrix products, arithmetic and copies ran while one was open for 1% of the time, Pallas kernels for 10%

profile of v4, /device:TPU:1, one launch (start us, length us, event | category | flops | bytes accessed | tf_op | source)
XLA Modules:
  0.0 76.9 jit_solution(6173740651927201965)
XLA Ops:
  0.6 2.7 %shard_map.85 = bf16[16,80,384]{2,1,0:T(8,128)(2,1)} custom-call(s32[1,2]{1,0:T(1,128)} %coarse.1, s32[1,2]{1,0:T(1,128)} %fraction.1, bf16[1,2,80,2560]{3,2,1,0:T(8,128)(2,1)} %x.1), custom_call_target="tpu_custom_call" | custom-call | flops 100000000 | bytes 2000000 | tf_op jit(solution)/shard_map/pallas_call | solution.py:271
  3.4 8.5 %all-to-all-start = ((bf16[16,80,384]{2,1,0:T(8,128)(2,1)}), bf16[16,80,384]{2,1,0:T(8,128)(2,1)S(1)}, u32[]{:S(2)}, u32[]{:S(2)}) async-start(bf16[16,80,384]{2,1,0:T(8,128)(2,1)} %shard_map.85), calls=%async_computation | async-start | bytes 1966080 | tf_op jit(solution)/shard_map/all_to_all | solution.py:286
  12.5 14.2 %all-to-all-done = bf16[16,80,384]{2,1,0:T(8,128)(2,1)S(1)} async-done(((bf16[16,80,384]{2,1,0:T(8,128)(2,1)}), bf16[16,80,384]{2,1,0:T(8,128)(2,1)S(1)}, u32[]{:S(2)}, u32[]{:S(2)}) %all-to-all-start) | async-done | bytes 983072 | tf_op jit(solution)/shard_map/all_to_all | solution.py:286
  26.7 0.1 slice_convert_fusion
  26.8 0.1 copy.13
  26.9 0.1 copy.14.offsets
  27.0 1.0 %shard_map.87 = bf16[512,128]{1,0:T(8,128)(2,1)} custom-call(bf16[160,384]{1,0:T(8,128)(2,1)S(1)} %dynamic-slice_bitcast_fusion.image), custom_call_target="tpu_custom_call" | custom-call | flops 100000000 | bytes 122880 | tf_op jit(solution)/shard_map/pallas_call | solution.py:249
  28.0 8.3 %all-to-all-start.1 = ((bf16[16,32,128]{2,1,0:T(8,128)(2,1)}), bf16[16,32,128]{2,1,0:T(8,128)(2,1)S(1)}, u32[]{:S(2)}, u32[]{:S(2)}) async-start(bf16[16,32,128]{2,1,0:T(8,128)(2,1)} %bitcast.5), calls=%async_computation.1 | async-start | bytes 262144 | tf_op jit(solution)/shard_map/all_to_all | solution.py:292
  36.3 0.0 copy-start.1
  36.3 1.3 %collective-permute-start = (bf16[3,160,384]{2,1,0:T(8,128)(2,1)S(1)}, bf16[3,160,384]{2,1,0:T(8,128)(2,1)S(1)}, u32[]{:S(2)}, u32[]{:S(2)}) collective-permute-start(bf16[3,160,384]{2,1,0:T(8,128)(2,1)S(1)} %bitcast.20), channel_id=1, source_target_pairs={{16,0},{32,16},{48,32},{64,48},{80,64},{96,80},{112,96},{128,112},... | collective-permute-start | bytes 1105928 | tf_op jit(solution)/shard_map/ppermute | solution.py:300
  37.6 0.0 copy-done.1
  37.6 5.2 %shard_map.86 = (bf16[8,160,384]{2,1,0:T(8,128)(2,1)S(1)}, f32[8,32,128]{2,1,0:T(8,128)S(1)}) custom-call(s32[8,4]{1,0:T(8,128)S(1)} %copy.14.offsets, f32[64,8]{1,0:T(8,128)S(1)} %copy-done.1, bf16[8,160,384]{2,1,0:T(8,128)(2,1)S(1)} %bitcast.17), custom_call_target="tpu_custom_call" | custom-call | flops 4000000000 | bytes 983040 | tf_op jit(solution)/shard_map/pallas_call | solution.py:249
  42.8 0.9 %all-to-all-done.1 = bf16[16,32,128]{2,1,0:T(8,128)(2,1)S(1)} async-done(((bf16[16,32,128]{2,1,0:T(8,128)(2,1)}), bf16[16,32,128]{2,1,0:T(8,128)(2,1)S(1)}, u32[]{:S(2)}, u32[]{:S(2)}) %all-to-all-start.1) | async-done | bytes 131104 | tf_op jit(solution)/shard_map/all_to_all | solution.py:292
  43.7 0.7 broadcast_in_dim.8
  44.4 7.6 %all-to-all-start.2 = ((bf16[16,32,128]{2,1,0:T(8,128)(2,1)}), bf16[16,32,128]{2,1,0:T(8,128)(2,1)S(1)}, u32[]{:S(2)}, u32[]{:S(2)}) async-start(bf16[16,32,128]{2,1,0:T(8,128)(2,1)} %broadcast_in_dim.8), calls=%async_computation.2 | async-start | bytes 262144 | tf_op jit(solution)/shard_map/all_to_all | solution.py:303
  52.0 0.0 collective-permute-done.later
  52.0 0.2 convert_reduce_fusion.offsets
  52.3 2.8 %shard_map.88.later_part = f32[3,32,128]{2,1,0:T(8,128)S(1)} custom-call(s32[3,4]{1,0:T(4,128)S(1)} %convert_reduce_fusion.offsets, f32[64,8]{1,0:T(8,128)S(1)} %copy-done.1, bf16[3,160,384]{2,1,0:T(8,128)(2,1)S(1)} %collective-permute-done.later, bf16[3,160,384]{2,1,0:T(8,128)(2,1)S(1)} %slice.19.z), custom_call_target="tpu_custom_call" | custom-call | flops 2000000000 | bytes 737280 | tf_op jit(solution)/shard_map/pallas_call | solution.py:249
  55.1 4.3 %all-to-all-done.2 = bf16[16,32,128]{2,1,0:T(8,128)(2,1)S(1)} async-done(((bf16[16,32,128]{2,1,0:T(8,128)(2,1)}), bf16[16,32,128]{2,1,0:T(8,128)(2,1)S(1)}, u32[]{:S(2)}, u32[]{:S(2)}) %all-to-all-start.2) | async-done | bytes 131104 | tf_op jit(solution)/shard_map/all_to_all | solution.py:303
  59.4 0.8 %shard_map.89 = f32[8,32,128]{2,1,0:T(8,128)S(1)} custom-call(f32[8,32,128]{2,1,0:T(8,128)S(1)} %get-tuple-element.7.part, f32[3,32,128]{2,1,0:T(8,128)S(1)} %shard_map.88.later_part, bf16[8,160,384]{2,1,0:T(8,128)(2,1)S(1)} %get-tuple-element.9.z, bf16[512,128]{1,0:T(8,128)(2,1)S(1)} %bitcast.18), custom_call_target="tpu_custom_call" | custom-call | flops 1000000000 | bytes 1294336 | tf_op jit(solution)/shard_map/pallas_call | solution.py:249
  60.2 0.0 copy-start
  60.2 15.1 %all_to_all.20.got = f32[16,16,128]{2,1,0:T(8,128)S(1)} all-to-all(f32[16,16,128]{2,1,0:T(8,128)S(1)} %bitcast.19), channel_id=1, replica_groups=mesh['xl'=2,'z'=8,'y'=4,'core'=2,'row'=2] {'y','core','row'}, dimensions={0} | all-to-all | bytes 262144 | tf_op jit(solution)/shard_map/all_to_all | solution.py:314
  75.3 0.0 copy-done
  75.3 1.6 %shard_map.90 = (f32[1,2,16,128]{3,2,1,0:T(8,128)}, f32[1,3,2,16,128]{4,3,2,1,0:T(8,128)}, f32[1,3,16,128]{3,2,1,0:T(8,128)}) custom-call(s32[1,3]{1,0:T(1,128)S(1)} %copy-done, f32[16,16,128]{2,1,0:T(8,128)S(1)} %all_to_all.20.got), custom_call_target="tpu_custom_call" | custom-call | flops 10000000 | bytes 131072 | tf_op jit(solution)/shard_map/pallas_call | solution.py:249
  (4 shorter events, 0.1 us)
Async XLA Ops:
  3.4 23.3 %all-to-all-start = ((bf16[16,80,384]{2,1,0:T(8,128)(2,1)}), bf16[16,80,384]{2,1,0:T(8,128)(2,1)S(1)}, u32[]{:S(2)}, u32[]{:S(2)}) async-start(bf16[16,80,384]{2,1,0:T(8,128)(2,1)} %shard_map.85), calls=%async_computation | async-start | bytes 1966080 | tf_op jit(solution)/shard_map/all_to_all | solution.py:286
  28.0 15.7 %all-to-all-start.1 = ((bf16[16,32,128]{2,1,0:T(8,128)(2,1)}), bf16[16,32,128]{2,1,0:T(8,128)(2,1)S(1)}, u32[]{:S(2)}, u32[]{:S(2)}) async-start(bf16[16,32,128]{2,1,0:T(8,128)(2,1)} %bitcast.5), calls=%async_computation.1 | async-start | bytes 262144 | tf_op jit(solution)/shard_map/all_to_all | solution.py:292
  36.3 1.4 %copy-start.1 = (f32[64,8]{1,0:T(8,128)S(1)}, f32[64,8]{1,0:T(8,128)}, u32[]{:S(2)}) copy-start(f32[64,8]{1,0:T(8,128)} %constant.37.clone.table) | copy-start | bytes 6148
  36.3 15.7 %collective-permute-start = (bf16[3,160,384]{2,1,0:T(8,128)(2,1)S(1)}, bf16[3,160,384]{2,1,0:T(8,128)(2,1)S(1)}, u32[]{:S(2)}, u32[]{:S(2)}) collective-permute-start(bf16[3,160,384]{2,1,0:T(8,128)(2,1)S(1)} %bitcast.20), channel_id=1, source_target_pairs={{16,0},{32,16},{48,32},{64,48},{80,64},{96,80},{112,96},{128,112},... | collective-permute-start | bytes 1105928 | tf_op jit(solution)/shard_map/ppermute | solution.py:300
  44.4 15.0 %all-to-all-start.2 = ((bf16[16,32,128]{2,1,0:T(8,128)(2,1)}), bf16[16,32,128]{2,1,0:T(8,128)(2,1)S(1)}, u32[]{:S(2)}, u32[]{:S(2)}) async-start(bf16[16,32,128]{2,1,0:T(8,128)(2,1)} %broadcast_in_dim.8), calls=%async_computation.2 | async-start | bytes 262144 | tf_op jit(solution)/shard_map/all_to_all | solution.py:303
  60.2 15.1 %copy-start = (s32[1,3]{1,0:T(1,128)S(1)}, s32[1,3]{1,0:T(1,128)}, u32[]{:S(2)}) copy-start(s32[1,3]{1,0:T(1,128)} %on.1) | copy-start | bytes 40

commit v5 on v4

--- a/solution.py
+++ b/solution.py
@@ -131,13 +131,17 @@
 
 def candidate_kernel(image, out):
     rows = image.shape[0]
+    half = rows // 2
     order = jnp.where(row_distance(rows) == 0, 1.0, 0.0).astype(BF)
     shift = jnp.where(lane_distance() == LEAD, 1.0, 0.0).astype(BF)
-    value = filtered(image[...], order, shift).astype(BF)
-    for t in range(LANES // 128):
-        out[t * rows : (t + 1) * rows] = value[:, t * 128 : (t + 1) * 128]
-    used = LANES // 128 * rows
-    out[used:] = jnp.zeros((out.shape[0] - used, 128), BF)
+    value = filtered(image[...], order, shift)
+    lane = iota((rows, 128), 1)
+    last = value[:, 256:]
+    middle = jnp.where((lane >= 32) & (lane < 64), pltpu.roll(last, 96, 1), value[:, 128:256])
+    last = jnp.where(lane[:half] < 64, last[:half], pltpu.roll(last[half:], 64, 1))
+    out[:rows] = value[:, :128].astype(BF)
+    out[rows : 2 * rows] = middle.astype(BF)
+    out[2 * rows :] = last.astype(BF)
 
 
 def resampled(image, offsets, n, table, rows_apart, lanes_apart):
@@ -162,7 +166,7 @@
     return total
 
 
-def own_kernel(offsets, table, images, z, out, turned, powers):
+def resample_kernel(offsets, table, images, z, turned, powers):
     dates, rows, _ = images.shape
     looks = look_matrix()
     rows_apart, lanes_apart = row_distance(rows), lane_distance()
@@ -171,6 +175,11 @@
         z[n] = value.astype(BF)
         turned[n] = crossed(value).astype(BF)
         powers[n] = looks_of(row_sum(z[n], z[n]), looks)
+
+
+def own_kernel(z, turned, powers, out):
+    dates = z.shape[0]
+    looks = look_matrix()
     for n in range(dates):
         total = pltpu.roll(powers[n], SLOT * (2 + 2 * SPAN), 1)
         spans = [s for s in range(SPAN) if n + s + 1 < dates]
@@ -195,13 +204,25 @@
         out[n] = pair_looks(z[n], partners, looks)
 
 
-def reference_kernel(part, later_part, z, q, out):
+def reference_kernel(ref, part, later_part, z, near, below, above, out):
     dates = part.shape[0]
     rows = z.shape[1]
     looks = look_matrix()
-    value = jnp.concatenate(
-        [q[t * rows : (t + 1) * rows].astype(F32) for t in range(LANES // 128)], axis=1
-    )
+    size, members = lax.axis_size("z"), part.shape[0]
+    apart = (lax.axis_index("z") - ref[0] // members) % size
+    from_below = (apart >= 2) & (apart <= 4)
+    from_above = (apart >= 5) & (apart <= 6)
+
+    def chosen(start, count):
+        at = slice(start, start + count)
+        value = jnp.where(from_below, below[at].astype(F32), near[at].astype(F32))
+        return jnp.where(from_above, above[at].astype(F32), value)
+
+    middle = chosen(rows, rows)
+    last = chosen(2 * rows, rows // 2)
+    last = jnp.concatenate([last, pltpu.roll(last, 64, 1)], axis=0)
+    last = jnp.where(iota((rows, 128), 1) < 64, last, pltpu.roll(middle, 32, 1))
+    value = jnp.concatenate([chosen(0, rows), middle, last], axis=1)
     turned = crossed(value).astype(BF)
     value = value.astype(BF)
     for n in range(dates):
@@ -285,23 +306,30 @@
     )(coarse, fraction, slc)
     images = lax.all_to_all(packed, NEAR, 0, 0).reshape(members, all_rows, LANES)
 
-    tiles = LANES // 128 * all_rows
-    piece = -(-tiles // (16 * groups)) * 16
     cand = lax.dynamic_index_in_dim(images, ref % members, 0, keepdims=False)
-    cand = call(candidate_kernel, [], [cand], [((groups * piece, 128), BF)], 10**8)
-    got = lax.all_to_all(cand.reshape(groups, piece, 128), FAR, 0, 0)
+    cand = call(candidate_kernel, [], [cand], [((all_rows * 5 // 2, 128), BF)], 10**8)
+    size = lax.axis_size("z")
+
+    def around(value, by):
+        return lax.ppermute(value, "z", [(i, (i + by) % size) for i in range(size)])
+
+    got = lax.ppermute(cand, "xl", [(0, 1), (1, 0)])
     offsets = images[:, :4, SPARE].astype(jnp.int32)
-    z, part = call(
-        own_kernel, [offsets, table], [images],
-        [(images.shape, BF), ((members, count, 128), F32)], 4 * 10**9,
-        [pltpu.VMEM(images.shape, BF), pltpu.VMEM((members, count, 128), F32)],
+    sums = (members, count, 128)
+    z, turned, powers = call(
+        resample_kernel, [offsets, table], [images],
+        [(images.shape, BF), (images.shape, BF), (sums, F32)], 4 * 10**9,
     )
     got, z = lax.optimization_barrier((got, z))
+    q = jnp.where(lax.axis_index("xl") == ref // (members * size), cand, got)
+    apart = (lax.axis_index("z") - ref // members) % size
+    below, above = around(q, 1), around(q, -1)
+    part = call(own_kernel, [], [z, turned, powers], [(sums, F32)], 2 * 10**9)
+    below, part = lax.optimization_barrier((below, part))
+    q = jnp.where(apart == 1, below, jnp.where(apart == size - 1, above, q))
+    below, above = around(q, 3), around(q, -3)
+
     later = lax.ppermute(images[:SPAN], FAR, [(i + 1, i) for i in range(groups - 1)])
-
-    got = lax.dynamic_index_in_dim(got, ref // members, 0)
-    q = lax.all_to_all(jnp.broadcast_to(got, (groups, piece, 128)), FAR, 0, 0)
-    q = q.reshape(groups * piece, 128)
 
     later_offsets = later[:, :4, SPARE].astype(jnp.int32)
     later_part = call(
@@ -309,7 +337,7 @@
         [((SPAN, count, 128), F32)], 2 * 10**9,
     )
     maps = call(
-        reference_kernel, [], [part, later_part, z, q], [((members, count, 128), F32)], 10**9
+        reference_kernel, [ref_date], [part, later_part, z, q, below, above], [(sums, F32)], 10**9
     )
     got = lax.all_to_all(maps.reshape(slabs, count // halves, 128), NEAR, 0, 0)
     small = (count // halves, 128)

time: 77.4 us -> 75.2 us (0.972)
  the two profiles are of different devices: /device:TPU:1 before, /device:TPU:33 now
where the time goes in v5:
time: 75.2 us; the launch traced here: 74.9 us
  waiting for transfers between devices  24 us (32%)
  blocking collectives  18.1 us (24%)
  starting transfers between devices  16.8 us (22%)
  Pallas kernels  14 us (19%)
  between operations  1.43 us (2%)
    all_to_all x1, blocking collectives, on_device(): got = lax.all_to_all(maps.reshape(slabs, count // halves, 128), NEAR, 0, 0)  18.1 us
    all_to_all x1, waiting for transfers between devices, on_device(): lax.all_to_all(packed, NEAR, 0, 0).reshape(members, all_rows, LANES)  14.2 us
    pallas_call x6, Pallas kernels, call(): pl.pallas_call(kernel, out_shape=out_shape[0] if single else out_shape, i...  11.2 us
    ppermute x4, waiting for transfers between devices, around(): return lax.ppermute(value, 'z', [(i, (i + by) % size) for i in range(size)])  9.89 us
    all_to_all x1, starting transfers between devices, on_device(): lax.all_to_all(packed, NEAR, 0, 0).reshape(members, all_rows, LANES)  7.63 us
    ppermute x4, starting transfers between devices, around(): return lax.ppermute(value, 'z', [(i, (i + by) % size) for i in range(size)])  7.05 us
    pallas_call x1, Pallas kernels, on_device(): pl.pallas_call(pack_kernel, out_shape=jax.ShapeDtypeStruct((slabs, rows,...  2.72 us
    ppermute x1, starting transfers between devices, on_device(): lax.ppermute(images[:SPAN], FAR, [(i + 1, i) for i in range(groups - 1)])  1.92 us
  transfers between devices with their start and end apart: 7, of which 5 were waited for; matrix products, arithmetic and copies ran while one was open for 1% of the time, Pallas kernels for 11%

profile of v5, /device:TPU:33, one launch (start us, length us, event | category | flops | bytes accessed | tf_op | source)
XLA Modules:
  0.0 74.9 jit_solution(12018943367229348774)
XLA Ops:
  0.6 2.7 %shard_map.85 = bf16[16,80,384]{2,1,0:T(8,128)(2,1)} custom-call(s32[1,2]{1,0:T(1,128)} %coarse.1, s32[1,2]{1,0:T(1,128)} %fraction.1, bf16[1,2,80,2560]{3,2,1,0:T(8,128)(2,1)} %x.1), custom_call_target="tpu_custom_call" | custom-call | flops 100000000 | bytes 2000000 | tf_op jit(solution)/shard_map/pallas_call | solution.py:292
  3.4 7.6 %all-to-all-start = ((bf16[16,80,384]{2,1,0:T(8,128)(2,1)}), bf16[16,80,384]{2,1,0:T(8,128)(2,1)S(1)}, u32[]{:S(2)}, u32[]{:S(2)}) async-start(bf16[16,80,384]{2,1,0:T(8,128)(2,1)} %shard_map.85), calls=%async_computation | async-start | bytes 1966080 | tf_op jit(solution)/shard_map/all_to_all | solution.py:307
  11.7 14.2 %all-to-all-done = bf16[16,80,384]{2,1,0:T(8,128)(2,1)S(1)} async-done(((bf16[16,80,384]{2,1,0:T(8,128)(2,1)}), bf16[16,80,384]{2,1,0:T(8,128)(2,1)S(1)}, u32[]{:S(2)}, u32[]{:S(2)}) %all-to-all-start) | async-done | bytes 983072 | tf_op jit(solution)/shard_map/all_to_all | solution.py:307
  25.9 0.1 slice_convert_fusion
  26.0 0.4 shard_map.86
  26.4 0.2 collective-permute-start
  26.5 0.1 copy.13
  26.6 0.1 copy.14.offsets
  26.7 0.0 copy-start.1
  26.8 1.9 %collective-permute-start.2 = (bf16[3,160,384]{2,1,0:T(8,128)(2,1)S(1)}, bf16[3,160,384]{2,1,0:T(8,128)(2,1)S(1)}, u32[]{:S(2)}, u32[]{:S(2)}) collective-permute-start(bf16[3,160,384]{2,1,0:T(8,128)(2,1)S(1)} %bitcast.15), channel_id=1, source_target_pairs={{16,0},{32,16},{48,32},{64,48},{80,64},{96,80},{112,96},{128,112},... | collective-permute-start | bytes 1105928 | tf_op jit(solution)/shard_map/ppermute | solution.py:332
  28.7 0.0 copy-done.1
  28.7 4.4 %shard_map.87 = (bf16[8,160,384]{2,1,0:T(8,128)(2,1)S(1)}, bf16[8,160,384]{2,1,0:T(8,128)(2,1)S(1)}, f32[8,32,128]{2,1,0:T(8,128)S(1)}) custom-call(s32[8,4]{1,0:T(8,128)S(1)} %copy.14.offsets, f32[64,8]{1,0:T(8,128)S(1)} %copy-done.1, bf16[8,160,384]{2,1,0:T(8,128)(2,1)S(1)} %bitcast.13), custom_call_target="tpu_custom_call" | custom-call | flops 4000000000 | bytes 983040 | tf_op jit(solution)/shard_map/pallas_call | solution.py:270
  33.1 0.0 collective-permute-done
  33.2 1.7 %collective-permute-start.1 = (bf16[400,128]{1,0:T(8,128)(2,1)S(1)}, bf16[400,128]{1,0:T(8,128)(2,1)S(1)}, u32[]{:S(2)}, u32[]{:S(2)}) collective-permute-start(bf16[400,128]{1,0:T(8,128)(2,1)S(1)} %broadcast_select_fusion), channel_id=1, source_target_pairs={{0,16},{16,32},{32,48},{48,64},{64,80},{80,96},{96,112},{112,0},{1... | collective-permute-start | bytes 307208 | tf_op jit(solution)/shard_map/ppermute | solution.py:314
  34.9 0.0 collective-permute-start.3
  34.9 1.1 %shard_map.88.part = f32[8,32,128]{2,1,0:T(8,128)S(1)} custom-call(bf16[8,160,384]{2,1,0:T(8,128)(2,1)S(1)} %get-tuple-element.12.z, bf16[8,160,384]{2,1,0:T(8,128)(2,1)S(1)} %get-tuple-element.13.turned, f32[8,32,128]{2,1,0:T(8,128)S(1)} %get-tuple-element.14.powers), custom_call_target="tpu_custom_call" | custom-call | flops 2000000000 | bytes 2097152 | tf_op jit(solution)/shard_map/pallas_call | solution.py:270
  36.1 1.0 %collective-permute-done.1 = bf16[400,128]{1,0:T(8,128)(2,1)S(1)} collective-permute-done((bf16[400,128]{1,0:T(8,128)(2,1)S(1)}, bf16[400,128]{1,0:T(8,128)(2,1)S(1)}, u32[]{:S(2)}, u32[]{:S(2)}) %collective-permute-start.1) | collective-permute-done | bytes 102432 | tf_op jit(solution)/shard_map/ppermute | solution.py:314
  37.0 3.4 %collective-permute-done.3 = bf16[400,128]{1,0:T(8,128)(2,1)S(1)} collective-permute-done((bf16[400,128]{1,0:T(8,128)(2,1)S(1)}, bf16[400,128]{1,0:T(8,128)(2,1)S(1)}, u32[]{:S(2)}, u32[]{:S(2)}) %collective-permute-start.3) | collective-permute-done | bytes 102432 | tf_op jit(solution)/shard_map/ppermute | solution.py:314
  40.5 5.2 %collective-permute-start.4 = (bf16[400,128]{1,0:T(8,128)(2,1)S(1)}, bf16[400,128]{1,0:T(8,128)(2,1)S(1)}, u32[]{:S(2)}, u32[]{:S(2)}) collective-permute-start(bf16[400,128]{1,0:T(8,128)(2,1)S(1)} %select_select_fusion.near), channel_id=1, source_target_pairs={{0,48},{16,64},{32,80},{48,96},{64,112},{80,0},{96,16},{112,32},{1... | collective-permute-start | bytes 307208 | tf_op jit(solution)/shard_map/ppermute | solution.py:314
  45.7 0.1 collective-permute-start.5
  45.8 0.0 collective-permute-done.2.later
  45.8 0.2 convert_reduce_fusion.offsets
  46.0 2.8 %shard_map.89.later_part = f32[3,32,128]{2,1,0:T(8,128)S(1)} custom-call(s32[3,4]{1,0:T(4,128)S(1)} %convert_reduce_fusion.offsets, f32[64,8]{1,0:T(8,128)S(1)} %copy-done.1, bf16[3,160,384]{2,1,0:T(8,128)(2,1)S(1)} %collective-permute-done.2.later, bf16[3,160,384]{2,1,0:T(8,128)(2,1)S(1)} %slice.19.z), custom_call_target="tpu_custom_call" | custom-call | flops 2000000000 | bytes 737280 | tf_op jit(solution)/shard_map/pallas_call | solution.py:270
  48.8 3.3 %collective-permute-done.4.below = bf16[400,128]{1,0:T(8,128)(2,1)S(1)} collective-permute-done((bf16[400,128]{1,0:T(8,128)(2,1)S(1)}, bf16[400,128]{1,0:T(8,128)(2,1)S(1)}, u32[]{:S(2)}, u32[]{:S(2)}) %collective-permute-start.4) | collective-permute-done | bytes 102432 | tf_op jit(solution)/shard_map/ppermute | solution.py:314
  52.1 2.3 %collective-permute-done.5.above = bf16[400,128]{1,0:T(8,128)(2,1)S(1)} collective-permute-done((bf16[400,128]{1,0:T(8,128)(2,1)S(1)}, bf16[400,128]{1,0:T(8,128)(2,1)S(1)}, u32[]{:S(2)}, u32[]{:S(2)}) %collective-permute-start.5) | collective-permute-done | bytes 102432 | tf_op jit(solution)/shard_map/ppermute | solution.py:314
  54.4 0.8 %shard_map.90 = f32[8,32,128]{2,1,0:T(8,128)S(1)} custom-call(s32[1]{0:T(128)} %copy.15.ref, f32[8,32,128]{2,1,0:T(8,128)S(1)} %shard_map.88.part, f32[3,32,128]{2,1,0:T(8,128)S(1)} %shard_map.89.later_part, bf16[8,160,384]{2,1,0:T(8,128)(2,1)S(1)} %get-tuple-element.12.z, bf16[400,128]{1,0:T(8,128)(2,1)S(1)} %select_select_fusion.near, ...), custom_call_target="tpu_custom_call" | custom-call | flops 1000000000 | bytes 1470464 | tf_op jit(solution)/shard_map/pallas_call | solution.py:270
  55.2 0.0 copy-start
  55.2 18.1 %all_to_all.10.got = f32[16,16,128]{2,1,0:T(8,128)S(1)} all-to-all(f32[16,16,128]{2,1,0:T(8,128)S(1)} %bitcast.14), channel_id=1, replica_groups=mesh['xl'=2,'z'=8,'y'=4,'core'=2,'row'=2] {'y','core','row'}, dimensions={0} | all-to-all | bytes 262144 | tf_op jit(solution)/shard_map/all_to_all | solution.py:342
  73.3 0.0 copy-done
  73.3 1.6 %shard_map.91 = (f32[1,2,16,128]{3,2,1,0:T(8,128)}, f32[1,3,2,16,128]{4,3,2,1,0:T(8,128)}, f32[1,3,16,128]{3,2,1,0:T(8,128)}) custom-call(s32[1,3]{1,0:T(1,128)S(1)} %copy-done, f32[16,16,128]{2,1,0:T(8,128)S(1)} %all_to_all.10.got), custom_call_target="tpu_custom_call" | custom-call | flops 10000000 | bytes 131072 | tf_op jit(solution)/shard_map/pallas_call | solution.py:270
  (5 shorter events, 0.1 us)
Async XLA Ops:
  3.4 22.5 %all-to-all-start = ((bf16[16,80,384]{2,1,0:T(8,128)(2,1)}), bf16[16,80,384]{2,1,0:T(8,128)(2,1)S(1)}, u32[]{:S(2)}, u32[]{:S(2)}) async-start(bf16[16,80,384]{2,1,0:T(8,128)(2,1)} %shard_map.85), calls=%async_computation | async-start | bytes 1966080 | tf_op jit(solution)/shard_map/all_to_all | solution.py:307
  26.4 6.8 %collective-permute-start = (bf16[400,128]{1,0:T(8,128)(2,1)S(1)}, bf16[400,128]{1,0:T(8,128)(2,1)S(1)}, u32[]{:S(2)}, u32[]{:S(2)}) collective-permute-start(bf16[400,128]{1,0:T(8,128)(2,1)S(1)} %shard_map.86), channel_id=1, source_target_pairs={{0,128},{128,0},{1,129},{129,1},{2,130},{130,2},{3,131},{131,3},{4... | collective-permute-start | bytes 307208 | tf_op jit(solution)/shard_map/ppermute | solution.py:316
  26.7 2.0 %copy-start.1 = (f32[64,8]{1,0:T(8,128)S(1)}, f32[64,8]{1,0:T(8,128)}, u32[]{:S(2)}) copy-start(f32[64,8]{1,0:T(8,128)} %constant.60.clone.table) | copy-start | bytes 6148
  26.8 19.0 %collective-permute-start.2 = (bf16[3,160,384]{2,1,0:T(8,128)(2,1)S(1)}, bf16[3,160,384]{2,1,0:T(8,128)(2,1)S(1)}, u32[]{:S(2)}, u32[]{:S(2)}) collective-permute-start(bf16[3,160,384]{2,1,0:T(8,128)(2,1)S(1)} %bitcast.15), channel_id=1, source_target_pairs={{16,0},{32,16},{48,32},{64,48},{80,64},{96,80},{112,96},{128,112},... | collective-permute-start | bytes 1105928 | tf_op jit(solution)/shard_map/ppermute | solution.py:332
  33.2 3.9 %collective-permute-start.1 = (bf16[400,128]{1,0:T(8,128)(2,1)S(1)}, bf16[400,128]{1,0:T(8,128)(2,1)S(1)}, u32[]{:S(2)}, u32[]{:S(2)}) collective-permute-start(bf16[400,128]{1,0:T(8,128)(2,1)S(1)} %broadcast_select_fusion), channel_id=1, source_target_pairs={{0,16},{16,32},{32,48},{48,64},{64,80},{80,96},{96,112},{112,0},{1... | collective-permute-start | bytes 307208 | tf_op jit(solution)/shard_map/ppermute | solution.py:314
  34.9 5.6 %collective-permute-start.3 = (bf16[400,128]{1,0:T(8,128)(2,1)S(1)}, bf16[400,128]{1,0:T(8,128)(2,1)S(1)}, u32[]{:S(2)}, u32[]{:S(2)}) collective-permute-start(bf16[400,128]{1,0:T(8,128)(2,1)S(1)} %broadcast_select_fusion), channel_id=1, source_target_pairs={{0,112},{16,0},{32,16},{48,32},{64,48},{80,64},{96,80},{112,96},{1... | collective-permute-start | bytes 307208 | tf_op jit(solution)/shard_map/ppermute | solution.py:314
  40.5 11.6 %collective-permute-start.4 = (bf16[400,128]{1,0:T(8,128)(2,1)S(1)}, bf16[400,128]{1,0:T(8,128)(2,1)S(1)}, u32[]{:S(2)}, u32[]{:S(2)}) collective-permute-start(bf16[400,128]{1,0:T(8,128)(2,1)S(1)} %select_select_fusion.near), channel_id=1, source_target_pairs={{0,48},{16,64},{32,80},{48,96},{64,112},{80,0},{96,16},{112,32},{1... | collective-permute-start | bytes 307208 | tf_op jit(solution)/shard_map/ppermute | solution.py:314
  45.7 8.7 %collective-permute-start.5 = (bf16[400,128]{1,0:T(8,128)(2,1)S(1)}, bf16[400,128]{1,0:T(8,128)(2,1)S(1)}, u32[]{:S(2)}, u32[]{:S(2)}) collective-permute-start(bf16[400,128]{1,0:T(8,128)(2,1)S(1)} %select_select_fusion.near), channel_id=1, source_target_pairs={{0,80},{16,96},{32,112},{48,0},{64,16},{80,32},{96,48},{112,64},{1... | collective-permute-start | bytes 307208 | tf_op jit(solution)/shard_map/ppermute | solution.py:314
  55.2 18.1 %copy-start = (s32[1,3]{1,0:T(1,128)S(1)}, s32[1,3]{1,0:T(1,128)}, u32[]{:S(2)}) copy-start(s32[1,3]{1,0:T(1,128)} %on.1) | copy-start | bytes 40

commit v6 on v5

--- a/solution.py
+++ b/solution.py
@@ -17,8 +17,9 @@
 
 GRID = (2, 8, 4, 2)
 DATE = ("xl", "z", "y", "core")
-FAR = ("xl", "z")
-NEAR = ("y", "core", "row")
+NEAR = ("xl", "y", "core")
+RUNS = 2
+HALO = 16
 
 SLAB = 160
 WIN = 192
@@ -43,33 +44,42 @@
     return jnp.dot(a, b, preferred_element_type=F32)
 
 
+def row_order(rows, columns):
+    looks = rows // LOOK_R
+    out = iota((rows, columns), 0)
+    return (out % looks) * LOOK_R + out // looks
+
+
 def row_distance(rows):
-    looks = rows // LOOK_R
-    out = iota((rows, rows), 0)
-    return iota((rows, rows), 1) - (out % looks) * LOOK_R - out // looks
-
-
-def lane_distance():
-    return iota((256, 128), 0) - iota((256, 128), 1)
-
-
-def band(distance, shift, table, index):
+    source = iota((rows, rows + HALO), 1)
+    first = lax.axis_index("row") == 0
+    source = jnp.where((source < rows) | first, source, source - rows - HALO)
+    return source - row_order(rows, rows + HALO)
+
+
+def placed(distance, shift, table, index):
     total = jnp.zeros(distance.shape, F32)
     for k in range(8):
         total = jnp.where(distance == shift + k, table[index, k], total)
-    return total.astype(BF)
+    return total
+
+
+def lane_band_of(shift, table, index):
+    lane = iota((8, 128), 1)
+    base = placed(jnp.where(lane == 0, 0, 128 - lane), shift, table, index)
+    turned = pltpu.roll(jnp.broadcast_to(base[:1], (128, 128)), 0, 1, stride=1, stride_axis=0)
+    upper = iota((128, 128), 1) <= iota((128, 128), 0)
+    return jnp.concatenate(
+        [jnp.where(upper, turned, 0.0), jnp.where(upper, 0.0, turned)], axis=0
+    ).astype(BF)
 
 
 def filtered(image, row_band, lane_band):
+    rows = row_band.shape[0]
     fit = dot(row_band, image).astype(BF)
-    return jnp.concatenate(
-        [
-            dot(fit[:, :256], lane_band),
-            dot(fit[:, 128:], lane_band),
-            dot(fit[:, 256:], lane_band[:128]),
-        ],
-        axis=1,
-    )
+    last = jnp.concatenate([fit[:, 256:], jnp.zeros((rows, 128), BF)], axis=1)
+    found = dot(jnp.concatenate([fit[:, :256], fit[:, 128:], last], axis=0), lane_band)
+    return jnp.concatenate([found[:rows], found[rows : 2 * rows], found[2 * rows :]], axis=1)
 
 
 def crossed(value):
@@ -131,106 +141,116 @@
 
 def candidate_kernel(image, out):
     rows = image.shape[0]
-    half = rows // 2
-    order = jnp.where(row_distance(rows) == 0, 1.0, 0.0).astype(BF)
-    shift = jnp.where(lane_distance() == LEAD, 1.0, 0.0).astype(BF)
-    value = filtered(image[...], order, shift)
-    lane = iota((rows, 128), 1)
-    last = value[:, 256:]
-    middle = jnp.where((lane >= 32) & (lane < 64), pltpu.roll(last, 96, 1), value[:, 128:256])
-    last = jnp.where(lane[:half] < 64, last[:half], pltpu.roll(last[half:], 64, 1))
-    out[:rows] = value[:, :128].astype(BF)
-    out[rows : 2 * rows] = middle.astype(BF)
-    out[2 * rows :] = last.astype(BF)
-
-
-def resampled(image, offsets, n, table, rows_apart, lanes_apart):
-    row_band = band(rows_apart, offsets[n, 0] - 3, table, offsets[n, 2])
-    lane_band = band(lanes_apart, LEAD + offsets[n, 1] - 3, table, offsets[n, 3])
-    return filtered(image, row_band, lane_band)
-
-
-def pair_looks(first, partners, looks):
+    order = jnp.where(row_order(rows, rows) == iota((rows, rows), 1), 1.0, 0.0).astype(BF)
+    shift = jnp.where(iota((256, 128), 0) - iota((256, 128), 1) == LEAD, 1.0, 0.0).astype(BF)
+    value = filtered(image[...], order, shift).astype(BF)
+    for t in range(LANES // 128):
+        out[t * rows : (t + 1) * rows] = value[:, t * 128 : (t + 1) * 128]
+
+
+def resampled(image, edge, offsets, n, table, rows_apart):
+    row_band = placed(rows_apart, offsets[n, 0] - 3, table, offsets[n, 2]).astype(BF)
+    lane_band = lane_band_of(LEAD + offsets[n, 1] - 3, table, offsets[n, 3])
+    return filtered(jnp.concatenate([image, edge], axis=0), row_band, lane_band)
+
+
+def add_pairs(out, start, pairs, looks):
     sums = []
-    for _, image, turned, _ in partners:
-        sums.append(row_sum(first, image))
+    for _, _, first, second, turned, _ in pairs:
+        sums.append(row_sum(first, second))
         sums.append(row_sum(first, turned))
+    count = sums[0].shape[0]
     maps = looks_of(jnp.concatenate(sums, axis=0), looks)
-    count = sums[0].shape[0]
-    total = jnp.zeros((count, 128), F32)
-    for i, (s, _, _, power) in enumerate(partners):
+    totals = dict(start)
+    for i, (n, s, _, _, _, power) in enumerate(pairs):
         for c in range(2):
             one = maps[(2 * i + c) * count : (2 * i + c + 1) * count]
-            total = total + pltpu.roll(one, SLOT * (2 + 2 * s + c), 1)
-        total = total + pltpu.roll(power, SLOT * (3 + 2 * SPAN + s), 1)
-    return total
-
-
-def resample_kernel(offsets, table, images, z, turned, powers):
+            one = pltpu.roll(one, SLOT * (2 + 2 * s + c), 1)
+            totals[n] = totals[n] + one if n in totals else one
+        totals[n] = totals[n] + pltpu.roll(power, SLOT * (3 + 2 * SPAN + s), 1)
+    for n, total in totals.items():
+        out[n] = total
+
+
+def resample_kernel(offsets, table, images, edges, z, turned, powers):
     dates, rows, _ = images.shape
-    looks = look_matrix()
-    rows_apart, lanes_apart = row_distance(rows), lane_distance()
+    rows_apart = row_distance(rows)
+    sums = []
     for n in range(dates):
-        value = resampled(images[n], offsets, n, table, rows_apart, lanes_apart)
+        value = resampled(images[n], edges[n], offsets, n, table, rows_apart)
         z[n] = value.astype(BF)
         turned[n] = crossed(value).astype(BF)
-        powers[n] = looks_of(row_sum(z[n], z[n]), looks)
+        sums.append(row_sum(z[n], z[n]))
+    powers[...] = looks_of(jnp.concatenate(sums, axis=0), look_matrix()).reshape(powers.shape)
 
 
 def own_kernel(z, turned, powers, out):
-    dates = z.shape[0]
+    dates = z.shape[0] // RUNS
     looks = look_matrix()
-    for n in range(dates):
-        total = pltpu.roll(powers[n], SLOT * (2 + 2 * SPAN), 1)
-        spans = [s for s in range(SPAN) if n + s + 1 < dates]
-        if spans:
-            partners = [(s, z[n + s + 1], turned[n + s + 1], powers[n + s + 1]) for s in spans]
-            total = total + pair_looks(z[n], partners, looks)
-        out[n] = total
-
-
-def later_kernel(offsets, table, later, z, out):
-    dates, rows, _ = later.shape
+    for run in range(0, z.shape[0], dates):
+        start = {n: pltpu.roll(powers[n], SLOT * (2 + 2 * SPAN), 1) for n in range(run, run + dates)}
+        pairs = [
+            (n, s, z[n], z[n + s + 1], turned[n + s + 1], powers[n + s + 1])
+            for n in range(run, run + dates)
+            for s in range(SPAN)
+            if n + s + 1 < run + dates
+        ]
+        add_pairs(out, start, pairs, looks)
+
+
+def later_kernel(offsets, table, later, edges, z, out):
+    rows = later.shape[1]
+    members = z.shape[0] // RUNS
     looks = look_matrix()
-    rows_apart, lanes_apart = row_distance(rows), lane_distance()
-    found = []
-    for n in range(dates):
-        value = resampled(later[n], offsets, n, table, rows_apart, lanes_apart)
-        image = value.astype(BF)
-        power = looks_of(row_sum(image, image), looks)
-        found.append((image, crossed(value).astype(BF), power))
-    for n in range(dates):
-        partners = [(m - n + dates - 1,) + found[m] for m in range(n + 1)]
-        out[n] = pair_looks(z[n], partners, looks)
+    rows_apart = row_distance(rows)
+    last = lax.axis_index("z") == lax.axis_size("z") - 1
+    found, sums = [], []
+    for run in range(RUNS):
+        base = jnp.where(last, SPAN * (RUNS - 1), SPAN * run)
+        for n in range(SPAN):
+            value = resampled(later[base + n], edges[base + n], offsets, base + n, table, rows_apart)
+            image = value.astype(BF)
+            sums.append(row_sum(image, image))
+            found.append((image, crossed(value).astype(BF)))
+    powers = looks_of(jnp.concatenate(sums, axis=0), looks)
+    count = sums[0].shape[0]
+    pairs = []
+    for run in range(RUNS):
+        for n in range(SPAN):
+            first = z[(run + 1) * members - SPAN + n]
+            for m in range(n + 1):
+                at = run * SPAN + m
+                power = powers[at * count : (at + 1) * count]
+                pairs.append((run * SPAN + n, m - n + SPAN - 1, first) + found[at] + (power,))
+    add_pairs(out, {}, pairs, looks)
 
 
 def reference_kernel(ref, part, later_part, z, near, below, above, out):
     dates = part.shape[0]
     rows = z.shape[1]
-    looks = look_matrix()
-    size, members = lax.axis_size("z"), part.shape[0]
+    size, members = lax.axis_size("z"), dates // RUNS
     apart = (lax.axis_index("z") - ref[0] // members) % size
     from_below = (apart >= 2) & (apart <= 4)
     from_above = (apart >= 5) & (apart <= 6)
-
-    def chosen(start, count):
-        at = slice(start, start + count)
+    tiles = []
+    for t in range(LANES // 128):
+        at = slice(t * rows, (t + 1) * rows)
         value = jnp.where(from_below, below[at].astype(F32), near[at].astype(F32))
-        return jnp.where(from_above, above[at].astype(F32), value)
-
-    middle = chosen(rows, rows)
-    last = chosen(2 * rows, rows // 2)
-    last = jnp.concatenate([last, pltpu.roll(last, 64, 1)], axis=0)
-    last = jnp.where(iota((rows, 128), 1) < 64, last, pltpu.roll(middle, 32, 1))
-    value = jnp.concatenate([chosen(0, rows), middle, last], axis=1)
+        tiles.append(jnp.where(from_above, above[at].astype(F32), value))
+    value = jnp.concatenate(tiles, axis=1)
     turned = crossed(value).astype(BF)
     value = value.astype(BF)
+    sums = []
     for n in range(dates):
-        maps = looks_of(jnp.concatenate([row_sum(z[n], value), row_sum(z[n], turned)], axis=0), looks)
-        count = maps.shape[0] // 2
-        total = part[n] + maps[:count] + pltpu.roll(maps[count:], SLOT, 1)
-        if n >= dates - SPAN:
-            total = total + later_part[n - dates + SPAN]
+        sums.append(row_sum(z[n], value))
+        sums.append(row_sum(z[n], turned))
+    maps = looks_of(jnp.concatenate(sums, axis=0), look_matrix())
+    count = sums[0].shape[0]
+    for n in range(dates):
+        at = 2 * n * count
+        total = part[n] + maps[at : at + count] + pltpu.roll(maps[at + count : at + 2 * count], SLOT, 1)
+        if n % members >= members - SPAN:
+            total = total + later_part[n // members * SPAN + n % members - members + SPAN]
         out[n] = total
 
 
@@ -280,12 +300,11 @@
 
 def on_device(table, slc, coarse, fraction, pair_on, ref_date):
     _, _, rows, cols = slc.shape
-    members = lax.axis_size("y") * lax.axis_size("core")
-    halves = lax.axis_size("row")
-    slabs = members * halves
-    groups = lax.axis_size(FAR)
-    all_rows = rows * halves
-    count = all_rows // LOOK_R
+    slabs = lax.axis_size(NEAR)
+    members = slabs // RUNS
+    size = lax.axis_size("z")
+    count = rows // LOOK_R
+    row = lax.axis_index("row")
     ref = ref_date[0]
 
     anywhere = pl.BlockSpec(memory_space=pl.ANY)
@@ -304,43 +323,51 @@
         compiler_params=pltpu.CompilerParams(vmem_limit_bytes=60 * 2**20),
         cost_estimate=pl.CostEstimate(flops=10**8, bytes_accessed=2 * 10**6, transcendentals=0),
     )(coarse, fraction, slc)
-    images = lax.all_to_all(packed, NEAR, 0, 0).reshape(members, all_rows, LANES)
-
-    cand = lax.dynamic_index_in_dim(images, ref % members, 0, keepdims=False)
-    cand = call(candidate_kernel, [], [cand], [((all_rows * 5 // 2, 128), BF)], 10**8)
-    size = lax.axis_size("z")
+    images = lax.all_to_all(packed, NEAR, 0, 0)
+
+    edge = jnp.where(row == 0, images[:, rows - HALO :], images[:, :HALO])
+    edges = lax.ppermute(edge, "row", [(0, 1), (1, 0)])
+
+    def first_dates(value):
+        return jnp.concatenate([value[n : n + SPAN] for n in range(0, slabs, members)], axis=0)
+
+    later = lax.ppermute(first_dates(images), "z", [((i + 1) % size, i) for i in range(size)])
+    later_edges = lax.ppermute(
+        first_dates(edge), ("z", "row"),
+        [((i + 1) % size * 2 + 1 - r, i * 2 + r) for i in range(size) for r in range(2)],
+    )
+
+    cand = lax.dynamic_index_in_dim(
+        images, ref // (members * size) * members + ref % members, 0, keepdims=False
+    )
+    q = call(candidate_kernel, [], [cand], [((LANES // 128 * rows, 128), BF)], 10**8)
 
     def around(value, by):
         return lax.ppermute(value, "z", [(i, (i + by) % size) for i in range(size)])
 
-    got = lax.ppermute(cand, "xl", [(0, 1), (1, 0)])
-    offsets = images[:, :4, SPARE].astype(jnp.int32)
-    sums = (members, count, 128)
-    z, turned, powers = call(
-        resample_kernel, [offsets, table], [images],
-        [(images.shape, BF), (images.shape, BF), (sums, F32)], 4 * 10**9,
-    )
-    got, z = lax.optimization_barrier((got, z))
-    q = jnp.where(lax.axis_index("xl") == ref // (members * size), cand, got)
     apart = (lax.axis_index("z") - ref // members) % size
     below, above = around(q, 1), around(q, -1)
+    near = jnp.where(apart == 1, below, jnp.where(apart == size - 1, above, q))
+    below, above = around(near, 3), around(near, -3)
+
+    sums = (slabs, count, 128)
+    offsets = images[:, :4, SPARE].astype(jnp.int32)
+    z, turned, powers = call(
+        resample_kernel, [offsets, table], [images, edges],
+        [(images.shape, BF), (images.shape, BF), (sums, F32)], 4 * 10**9,
+    )
     part = call(own_kernel, [], [z, turned, powers], [(sums, F32)], 2 * 10**9)
-    below, part = lax.optimization_barrier((below, part))
-    q = jnp.where(apart == 1, below, jnp.where(apart == size - 1, above, q))
-    below, above = around(q, 3), around(q, -3)
-
-    later = lax.ppermute(images[:SPAN], FAR, [(i + 1, i) for i in range(groups - 1)])
-
     later_offsets = later[:, :4, SPARE].astype(jnp.int32)
     later_part = call(
-        later_kernel, [later_offsets, table], [later, z[members - SPAN :]],
-        [((SPAN, count, 128), F32)], 2 * 10**9,
+        later_kernel, [later_offsets, table], [later, later_edges, z],
+        [((RUNS * SPAN, count, 128), F32)], 2 * 10**9,
     )
     maps = call(
-        reference_kernel, [ref_date], [part, later_part, z, q, below, above], [(sums, F32)], 10**9
-    )
-    got = lax.all_to_all(maps.reshape(slabs, count // halves, 128), NEAR, 0, 0)
-    small = (count // halves, 128)
+        reference_kernel, [ref_date], [part, later_part, z, near, below, above],
+        [(sums, F32)], 10**9,
+    )
+    got = lax.all_to_all(maps, NEAR, 0, 0)
+    small = (count, 128)
     return call(
         finish_kernel, [pair_on], [got],
         [((1, 2) + small, F32), ((1, SPAN, 2) + small, F32), ((1, SPAN) + small, F32)], 10**7,

time: 75.2 us -> 64.9 us (0.86)
  the two profiles are of different devices: /device:TPU:33 before, /device:TPU:1 now
where the time goes in v6:
time: 64.9 us; the launch traced here: 64.7 us
  starting transfers between devices  22.3 us (34%)
  waiting for transfers between devices  14.4 us (22%)
  blocking collectives  13.8 us (21%)
  Pallas kernels  12 us (18%)
  between operations  1.47 us (2%)
    all_to_all x1, waiting for transfers between devices, on_device(): images = lax.all_to_all(packed, NEAR, 0, 0)  14.4 us
    all_to_all x1, blocking collectives, on_device(): got = lax.all_to_all(maps, NEAR, 0, 0)  13.8 us
    ppermute x4, starting transfers between devices, around(): return lax.ppermute(value, 'z', [(i, (i + by) % size) for i in range(size)])  10.3 us
    pallas_call x6, Pallas kernels, call(): pl.pallas_call(kernel, out_shape=out_shape[0] if single else out_shape, i...  9.29 us
    all_to_all x1, starting transfers between devices, on_device(): images = lax.all_to_all(packed, NEAR, 0, 0)  6.93 us
    pallas_call x1, Pallas kernels, on_device(): pl.pallas_call(pack_kernel, out_shape=jax.ShapeDtypeStruct((slabs, rows,...  2.72 us
    ppermute x1, starting transfers between devices, on_device(): edges = lax.ppermute(edge, 'row', [(0, 1), (1, 0)])  2.54 us
    ppermute x1, starting transfers between devices, on_device(): lax.ppermute(first_dates(images), 'z', [((i + 1) % size, i) for i in rang...  1.45 us
  transfers between devices with their start and end apart: 8, of which 1 were waited for; matrix products, arithmetic and copies ran while one was open for 1% of the time, Pallas kernels for 11%

profile of v6, /device:TPU:1, one launch (start us, length us, event | category | flops | bytes accessed | tf_op | source)
XLA Modules:
  0.0 64.7 jit_solution(375861862845012595)
XLA Ops:
  0.6 2.7 %shard_map.85 = bf16[16,80,384]{2,1,0:T(8,128)(2,1)} custom-call(s32[1,2]{1,0:T(1,128)} %coarse.1, s32[1,2]{1,0:T(1,128)} %fraction.1, bf16[1,2,80,2560]{3,2,1,0:T(8,128)(2,1)} %x.1), custom_call_target="tpu_custom_call" | custom-call | flops 100000000 | bytes 2000000 | tf_op jit(solution)/shard_map/pallas_call | solution.py:311
  3.4 6.9 %all-to-all-start = ((bf16[16,80,384]{2,1,0:T(8,128)(2,1)}), bf16[16,80,384]{2,1,0:T(8,128)(2,1)S(1)}, u32[]{:S(2)}, u32[]{:S(2)}) async-start(bf16[16,80,384]{2,1,0:T(8,128)(2,1)} %shard_map.85), calls=%async_computation | async-start | bytes 1966080 | tf_op jit(solution)/shard_map/all_to_all | solution.py:326
  11.0 14.4 %all-to-all-done.images = bf16[16,80,384]{2,1,0:T(8,128)(2,1)S(1)} async-done(((bf16[16,80,384]{2,1,0:T(8,128)(2,1)}), bf16[16,80,384]{2,1,0:T(8,128)(2,1)S(1)}, u32[]{:S(2)}, u32[]{:S(2)}) %all-to-all-start) | async-done | bytes 983072 | tf_op jit(solution)/shard_map/all_to_all | solution.py:326
  25.4 2.5 %collective-permute-start = (bf16[16,16,384]{2,1,0:T(8,128)(2,1)S(1)}, bf16[16,16,384]{2,1,0:T(8,128)(2,1)S(1)}, u32[]{:S(2)}, u32[]{:S(2)}) collective-permute-start(bf16[16,16,384]{2,1,0:T(8,128)(2,1)S(1)} %slice_select_fusion), channel_id=1, source_target_pairs={{0,1},{1,0},{2,3},{3,2},{4,5},{5,4},{6,7},{7,6},{8,9},{9,8},{10,11... | collective-permute-start | bytes 589832 | tf_op jit(solution)/shard_map/ppermute | solution.py:329
  28.0 0.3 shard_map.89
  28.3 1.7 %collective-permute-start.3 = (bf16[240,128]{1,0:T(8,128)(2,1)S(1)}, bf16[240,128]{1,0:T(8,128)(2,1)S(1)}, u32[]{:S(2)}, u32[]{:S(2)}) collective-permute-start(bf16[240,128]{1,0:T(8,128)(2,1)S(1)} %shard_map.89), channel_id=1, source_target_pairs={{0,16},{16,32},{32,48},{48,64},{64,80},{80,96},{96,112},{112,0},{1... | collective-permute-start | bytes 184328 | tf_op jit(solution)/shard_map/ppermute | solution.py:346
  30.0 4.0 %collective-permute-start.4 = (bf16[240,128]{1,0:T(8,128)(2,1)S(1)}, bf16[240,128]{1,0:T(8,128)(2,1)S(1)}, u32[]{:S(2)}, u32[]{:S(2)}) collective-permute-start(bf16[240,128]{1,0:T(8,128)(2,1)S(1)} %shard_map.89), channel_id=1, source_target_pairs={{0,112},{16,0},{32,16},{48,32},{64,48},{80,64},{96,80},{112,96},{1... | collective-permute-start | bytes 184328 | tf_op jit(solution)/shard_map/ppermute | solution.py:346
  34.0 0.1 slice_convert_fusion
  34.1 0.1 copy.13
  34.2 0.1 copy.14.offsets
  34.4 1.5 %collective-permute-start.1 = (bf16[6,80,384]{2,1,0:T(8,128)(2,1)S(1)}, bf16[6,80,384]{2,1,0:T(8,128)(2,1)S(1)}, u32[]{:S(2)}, u32[]{:S(2)}) collective-permute-start(bf16[6,80,384]{2,1,0:T(8,128)(2,1)S(1)} %pad_maximum_fusion), channel_id=1, source_target_pairs={{16,0},{32,16},{48,32},{64,48},{80,64},{96,80},{112,96},{0,112},{1... | collective-permute-start | bytes 1105928 | tf_op jit(solution)/shard_map/ppermute | solution.py:334
  35.9 0.0 copy-start.1
  35.9 1.0 %collective-permute-start.2 = (bf16[6,16,384]{2,1,0:T(8,128)(2,1)S(1)}, bf16[6,16,384]{2,1,0:T(8,128)(2,1)S(1)}, u32[]{:S(2)}, u32[]{:S(2)}) collective-permute-start(bf16[6,16,384]{2,1,0:T(8,128)(2,1)S(1)} %pad_maximum_fusion.1), channel_id=1, source_target_pairs={{17,0},{16,1},{33,16},{32,17},{49,32},{48,33},{65,48},{64,49},{81,... | collective-permute-start | bytes 221192 | tf_op jit(solution)/shard_map/ppermute | solution.py:335
  36.9 0.0 collective-permute-done.3
  36.9 0.0 collective-permute-done.4
  36.9 3.0 %collective-permute-start.5 = (bf16[240,128]{1,0:T(8,128)(2,1)S(1)}, bf16[240,128]{1,0:T(8,128)(2,1)S(1)}, u32[]{:S(2)}, u32[]{:S(2)}) collective-permute-start(bf16[240,128]{1,0:T(8,128)(2,1)S(1)} %select_select_fusion.near), channel_id=1, source_target_pairs={{0,48},{16,64},{32,80},{48,96},{64,112},{80,0},{96,16},{112,32},{1... | collective-permute-start | bytes 184328 | tf_op jit(solution)/shard_map/ppermute | solution.py:346
  39.9 1.6 %collective-permute-start.6 = (bf16[240,128]{1,0:T(8,128)(2,1)S(1)}, bf16[240,128]{1,0:T(8,128)(2,1)S(1)}, u32[]{:S(2)}, u32[]{:S(2)}) collective-permute-start(bf16[240,128]{1,0:T(8,128)(2,1)S(1)} %select_select_fusion.near), channel_id=1, source_target_pairs={{0,80},{16,96},{32,112},{48,0},{64,16},{80,32},{96,48},{112,64},{1... | collective-permute-start | bytes 184328 | tf_op jit(solution)/shard_map/ppermute | solution.py:346
  41.5 0.0 collective-permute-done.edges
  41.5 0.0 copy-done.1
  41.5 3.2 %shard_map.86 = (bf16[16,80,384]{2,1,0:T(8,128)(2,1)S(1)}, bf16[16,80,384]{2,1,0:T(8,128)(2,1)S(1)}, f32[16,16,128]{2,1,0:T(8,128)S(1)}) custom-call(s32[16,4]{1,0:T(8,128)S(1)} %copy.14.offsets, f32[64,8]{1,0:T(8,128)S(1)} %copy-done.1, bf16[16,80,384]{2,1,0:T(8,128)(2,1)S(1)} %all-to-all-done.images, bf16[16,16,384]{2,1,0:T(8,128)(2,1)S(1)} %collective-permute-done.edges), custom_call_target="tpu_custom_call" | custom-call | flops 4000000000 | bytes 1179648 | tf_op jit(solution)/shard_map/pallas_call | solution.py:290
  44.7 1.0 %shard_map.87.part = f32[16,16,128]{2,1,0:T(8,128)S(1)} custom-call(bf16[16,80,384]{2,1,0:T(8,128)(2,1)S(1)} %get-tuple-element.6.z, bf16[16,80,384]{2,1,0:T(8,128)(2,1)S(1)} %get-tuple-element.7.turned, f32[16,16,128]{2,1,0:T(8,128)S(1)} %get-tuple-element.8.powers), custom_call_target="tpu_custom_call" | custom-call | flops 2000000000 | bytes 2097152 | tf_op jit(solution)/shard_map/pallas_call | solution.py:290
  45.8 0.0 collective-permute-done.1.later
  45.8 0.1 slice_convert_fusion.1
  45.9 0.1 copy.15
  46.0 0.1 copy.16.offsets
  46.1 0.0 collective-permute-done.2.edges
  46.1 2.3 %shard_map.88.later_part = f32[6,16,128]{2,1,0:T(8,128)S(1)} custom-call(s32[6,4]{1,0:T(8,128)S(1)} %copy.16.offsets, f32[64,8]{1,0:T(8,128)S(1)} %copy-done.1, bf16[6,80,384]{2,1,0:T(8,128)(2,1)S(1)} %collective-permute-done.1.later, bf16[6,16,384]{2,1,0:T(8,128)(2,1)S(1)} %collective-permute-done.2.edges, bf16[16,80,384]{2,1,0:T(8,128)(2,1)S(1)} %get-tuple-element.6.z), custom_call_target="tpu_custom_call" | custom-call | flops 2000000000 | bytes 1425408 | tf_op jit(solution)/shard_map/pallas_call | solution.py:290
  48.4 0.0 collective-permute-done.5.below
  48.4 0.0 collective-permute-done.6.above
  48.4 0.8 %shard_map.90 = f32[16,16,128]{2,1,0:T(8,128)S(1)} custom-call(s32[1]{0:T(128)} %copy.17.ref, f32[16,16,128]{2,1,0:T(8,128)S(1)} %shard_map.87.part, f32[6,16,128]{2,1,0:T(8,128)S(1)} %shard_map.88.later_part, bf16[16,80,384]{2,1,0:T(8,128)(2,1)S(1)} %get-tuple-element.6.z, bf16[240,128]{1,0:T(8,128)(2,1)S(1)} %select_select_fusion.near, ...), custom_call_target="tpu_custom_call" | custom-call | flops 1000000000 | bytes 1347584 | tf_op jit(solution)/shard_map/pallas_call | solution.py:290
  49.2 0.0 copy-start
  49.2 13.8 %all_to_all.10.got = f32[16,16,128]{2,1,0:T(8,128)S(1)} all-to-all(f32[16,16,128]{2,1,0:T(8,128)S(1)} %shard_map.90), channel_id=1, replica_groups=mesh['xl'=2,'z'=8,'y'=4,'core'=2,'row'=2] {'xl','y','core'}, dimensions={0} | all-to-all | bytes 262144 | tf_op jit(solution)/shard_map/all_to_all | solution.py:369
  63.0 0.0 copy-done
  63.0 1.6 %shard_map.91 = (f32[1,2,16,128]{3,2,1,0:T(8,128)}, f32[1,3,2,16,128]{4,3,2,1,0:T(8,128)}, f32[1,3,16,128]{3,2,1,0:T(8,128)}) custom-call(s32[1,3]{1,0:T(1,128)S(1)} %copy-done, f32[16,16,128]{2,1,0:T(8,128)S(1)} %all_to_all.10.got), custom_call_target="tpu_custom_call" | custom-call | flops 10000000 | bytes 131072 | tf_op jit(solution)/shard_map/pallas_call | solution.py:290
  (7 shorter events, 0.2 us)
Async XLA Ops:
  3.4 22.0 %all-to-all-start = ((bf16[16,80,384]{2,1,0:T(8,128)(2,1)}), bf16[16,80,384]{2,1,0:T(8,128)(2,1)S(1)}, u32[]{:S(2)}, u32[]{:S(2)}) async-start(bf16[16,80,384]{2,1,0:T(8,128)(2,1)} %shard_map.85), calls=%async_computation | async-start | bytes 1966080 | tf_op jit(solution)/shard_map/all_to_all | solution.py:326
  25.4 16.1 %collective-permute-start = (bf16[16,16,384]{2,1,0:T(8,128)(2,1)S(1)}, bf16[16,16,384]{2,1,0:T(8,128)(2,1)S(1)}, u32[]{:S(2)}, u32[]{:S(2)}) collective-permute-start(bf16[16,16,384]{2,1,0:T(8,128)(2,1)S(1)} %slice_select_fusion), channel_id=1, source_target_pairs={{0,1},{1,0},{2,3},{3,2},{4,5},{5,4},{6,7},{7,6},{8,9},{9,8},{10,11... | collective-permute-start | bytes 589832 | tf_op jit(solution)/shard_map/ppermute | solution.py:329
  28.3 8.6 %collective-permute-start.3 = (bf16[240,128]{1,0:T(8,128)(2,1)S(1)}, bf16[240,128]{1,0:T(8,128)(2,1)S(1)}, u32[]{:S(2)}, u32[]{:S(2)}) collective-permute-start(bf16[240,128]{1,0:T(8,128)(2,1)S(1)} %shard_map.89), channel_id=1, source_target_pairs={{0,16},{16,32},{32,48},{48,64},{64,80},{80,96},{96,112},{112,0},{1... | collective-permute-start | bytes 184328 | tf_op jit(solution)/shard_map/ppermute | solution.py:346
  30.0 6.9 %collective-permute-start.4 = (bf16[240,128]{1,0:T(8,128)(2,1)S(1)}, bf16[240,128]{1,0:T(8,128)(2,1)S(1)}, u32[]{:S(2)}, u32[]{:S(2)}) collective-permute-start(bf16[240,128]{1,0:T(8,128)(2,1)S(1)} %shard_map.89), channel_id=1, source_target_pairs={{0,112},{16,0},{32,16},{48,32},{64,48},{80,64},{96,80},{112,96},{1... | collective-permute-start | bytes 184328 | tf_op jit(solution)/shard_map/ppermute | solution.py:346
  34.4 11.4 %collective-permute-start.1 = (bf16[6,80,384]{2,1,0:T(8,128)(2,1)S(1)}, bf16[6,80,384]{2,1,0:T(8,128)(2,1)S(1)}, u32[]{:S(2)}, u32[]{:S(2)}) collective-permute-start(bf16[6,80,384]{2,1,0:T(8,128)(2,1)S(1)} %pad_maximum_fusion), channel_id=1, source_target_pairs={{16,0},{32,16},{48,32},{64,48},{80,64},{96,80},{112,96},{0,112},{1... | collective-permute-start | bytes 1105928 | tf_op jit(solution)/shard_map/ppermute | solution.py:334
  35.9 5.6 %copy-start.1 = (f32[64,8]{1,0:T(8,128)S(1)}, f32[64,8]{1,0:T(8,128)}, u32[]{:S(2)}) copy-start(f32[64,8]{1,0:T(8,128)} %constant.61.clone.table) | copy-start | bytes 6148
  35.9 10.2 %collective-permute-start.2 = (bf16[6,16,384]{2,1,0:T(8,128)(2,1)S(1)}, bf16[6,16,384]{2,1,0:T(8,128)(2,1)S(1)}, u32[]{:S(2)}, u32[]{:S(2)}) collective-permute-start(bf16[6,16,384]{2,1,0:T(8,128)(2,1)S(1)} %pad_maximum_fusion.1), channel_id=1, source_target_pairs={{17,0},{16,1},{33,16},{32,17},{49,32},{48,33},{65,48},{64,49},{81,... | collective-permute-start | bytes 221192 | tf_op jit(solution)/shard_map/ppermute | solution.py:335
  36.9 11.5 %collective-permute-start.5 = (bf16[240,128]{1,0:T(8,128)(2,1)S(1)}, bf16[240,128]{1,0:T(8,128)(2,1)S(1)}, u32[]{:S(2)}, u32[]{:S(2)}) collective-permute-start(bf16[240,128]{1,0:T(8,128)(2,1)S(1)} %select_select_fusion.near), channel_id=1, source_target_pairs={{0,48},{16,64},{32,80},{48,96},{64,112},{80,0},{96,16},{112,32},{1... | collective-permute-start | bytes 184328 | tf_op jit(solution)/shard_map/ppermute | solution.py:346
  39.9 8.5 %collective-permute-start.6 = (bf16[240,128]{1,0:T(8,128)(2,1)S(1)}, bf16[240,128]{1,0:T(8,128)(2,1)S(1)}, u32[]{:S(2)}, u32[]{:S(2)}) collective-permute-start(bf16[240,128]{1,0:T(8,128)(2,1)S(1)} %select_select_fusion.near), channel_id=1, source_target_pairs={{0,80},{16,96},{32,112},{48,0},{64,16},{80,32},{96,48},{112,64},{1... | collective-permute-start | bytes 184328 | tf_op jit(solution)/shard_map/ppermute | solution.py:346
  49.2 13.8 %copy-start = (s32[1,3]{1,0:T(1,128)S(1)}, s32[1,3]{1,0:T(1,128)}, u32[]{:S(2)}) copy-start(s32[1,3]{1,0:T(1,128)} %on.1) | copy-start | bytes 40

commit v7 on v6

--- a/solution.py
+++ b/solution.py
@@ -110,33 +110,52 @@
     return total
 
 
-def pack_kernel(coarse, fraction, x, out, wide, shifts, taps, image_sem, small_sem):
+def pack_kernel(coarse, fraction, x, out, wide, packed, shifts, taps, in_sem, out_sem, small_sem):
     _, _, rows, cols = x.shape
-    copies = [
-        pltpu.make_async_copy(x.at[0, p], wide.at[p, :, pl.ds(128, cols)], image_sem.at[p])
+    pieces = in_sem.shape[0] // 2
+    width = cols // pieces
+    small = [
+        pltpu.make_async_copy(coarse, shifts, small_sem.at[0]),
+        pltpu.make_async_copy(fraction, taps, small_sem.at[1]),
+    ]
+    incoming = [
+        pltpu.make_async_copy(
+            x.at[0, p, :, pl.ds(c * width, width)],
+            wide.at[p, :, pl.ds(128 + c * width, width)],
+            in_sem.at[2 * c + p],
+        )
+        for c in range(pieces)
         for p in range(2)
     ]
-    copies.append(pltpu.make_async_copy(coarse, shifts, small_sem.at[0]))
-    copies.append(pltpu.make_async_copy(fraction, taps, small_sem.at[1]))
-    for copy in copies:
+    for copy in small + incoming:
         copy.start()
     for p in range(2):
         wide[p, :, :128] = jnp.zeros((rows, 128), BF)
         wide[p, :, 128 + cols :] = jnp.zeros((rows, 128), BF)
     lane = iota((rows, LANES), 1)
     row = iota((rows, LANES), 0)
-    for copy in copies:
+    for copy in small:
         copy.wait()
     own = jnp.where(row == 0, shifts[0, 0], jnp.where(row == 1, shifts[0, 1], 0))
     own = jnp.where(row == 2, taps[0, 0], jnp.where(row == 3, taps[0, 1], own))
     own = own.astype(F32)
+    here = 0
+    outgoing = []
     for j in range(out.shape[0]):
         start = 128 + SLAB * j - LEAD
         base, off = start // 128 * 128, start % 128
+        while here < pieces and 128 + here * width < base + LANES:
+            incoming[2 * here].wait()
+            incoming[2 * here + 1].wait()
+            here += 1
         first = pltpu.roll(wide[0, :, base : base + LANES].astype(F32), (LANES - off) % LANES, 1)
         second = pltpu.roll(wide[1, :, base : base + LANES].astype(F32), WIN - off, 1)
         value = jnp.where(lane < WIN, first, second)
-        out[j] = jnp.where(lane == SPARE, own, value).astype(BF)
+        packed[j] = jnp.where(lane == SPARE, own, value).astype(BF)
+        outgoing.append(pltpu.make_async_copy(packed.at[j], out.at[j], out_sem.at[j]))
+        outgoing[-1].start()
+    for copy in outgoing:
+        copy.wait()
 
 
 def candidate_kernel(image, out):
@@ -148,10 +167,10 @@
         out[t * rows : (t + 1) * rows] = value[:, t * 128 : (t + 1) * 128]
 
 
-def resampled(image, edge, offsets, n, table, rows_apart):
+def resampled(image, offsets, n, table, rows_apart):
     row_band = placed(rows_apart, offsets[n, 0] - 3, table, offsets[n, 2]).astype(BF)
     lane_band = lane_band_of(LEAD + offsets[n, 1] - 3, table, offsets[n, 3])
-    return filtered(jnp.concatenate([image, edge], axis=0), row_band, lane_band)
+    return filtered(image, row_band, lane_band)
 
 
 def add_pairs(out, start, pairs, looks):
@@ -177,7 +196,8 @@
     rows_apart = row_distance(rows)
     sums = []
     for n in range(dates):
-        value = resampled(images[n], edges[n], offsets, n, table, rows_apart)
+        image = jnp.concatenate([images[n], edges[n]], axis=0)
+        value = resampled(image, offsets, n, table, rows_apart)
         z[n] = value.astype(BF)
         turned[n] = crossed(value).astype(BF)
         sums.append(row_sum(z[n], z[n]))
@@ -198,8 +218,8 @@
         add_pairs(out, start, pairs, looks)
 
 
-def later_kernel(offsets, table, later, edges, z, out):
-    rows = later.shape[1]
+def later_kernel(offsets, table, later, z, out):
+    rows = z.shape[1]
     members = z.shape[0] // RUNS
     looks = look_matrix()
     rows_apart = row_distance(rows)
@@ -208,7 +228,7 @@
     for run in range(RUNS):
         base = jnp.where(last, SPAN * (RUNS - 1), SPAN * run)
         for n in range(SPAN):
-            value = resampled(later[base + n], edges[base + n], offsets, base + n, table, rows_apart)
+            value = resampled(later[base + n], offsets, base + n, table, rows_apart)
             image = value.astype(BF)
             sums.append(row_sum(image, image))
             found.append((image, crossed(value).astype(BF)))
@@ -312,12 +332,14 @@
         pack_kernel,
         out_shape=jax.ShapeDtypeStruct((slabs, rows, LANES), BF),
         in_specs=[anywhere] * 3,
-        out_specs=VMEM,
+        out_specs=anywhere,
         scratch_shapes=[
             pltpu.VMEM((2, rows, cols + 256), BF),
+            pltpu.VMEM((slabs, rows, LANES), BF),
             pltpu.SMEM((1, 2), jnp.int32),
             pltpu.SMEM((1, 2), jnp.int32),
-            pltpu.SemaphoreType.DMA((2,)),
+            pltpu.SemaphoreType.DMA((8,)),
+            pltpu.SemaphoreType.DMA((slabs,)),
             pltpu.SemaphoreType.DMA((2,)),
         ],
         compiler_params=pltpu.CompilerParams(vmem_limit_bytes=60 * 2**20),
@@ -331,10 +353,9 @@
     def first_dates(value):
         return jnp.concatenate([value[n : n + SPAN] for n in range(0, slabs, members)], axis=0)
 
-    later = lax.ppermute(first_dates(images), "z", [((i + 1) % size, i) for i in range(size)])
-    later_edges = lax.ppermute(
-        first_dates(edge), ("z", "row"),
-        [((i + 1) % size * 2 + 1 - r, i * 2 + r) for i in range(size) for r in range(2)],
+    later = lax.ppermute(
+        jnp.concatenate([first_dates(images), first_dates(edges)], axis=1),
+        "z", [((i + 1) % size, i) for i in range(size)],
     )
 
     cand = lax.dynamic_index_in_dim(
@@ -347,8 +368,6 @@
 
     apart = (lax.axis_index("z") - ref // members) % size
     below, above = around(q, 1), around(q, -1)
-    near = jnp.where(apart == 1, below, jnp.where(apart == size - 1, above, q))
-    below, above = around(near, 3), around(near, -3)
 
     sums = (slabs, count, 128)
     offsets = images[:, :4, SPARE].astype(jnp.int32)
@@ -356,10 +375,13 @@
         resample_kernel, [offsets, table], [images, edges],
         [(images.shape, BF), (images.shape, BF), (sums, F32)], 4 * 10**9,
     )
+    below, z = lax.optimization_barrier((below, z))
+    near = jnp.where(apart == 1, below, jnp.where(apart == size - 1, above, q))
+    below, above = around(near, 3), around(near, -3)
     part = call(own_kernel, [], [z, turned, powers], [(sums, F32)], 2 * 10**9)
     later_offsets = later[:, :4, SPARE].astype(jnp.int32)
     later_part = call(
-        later_kernel, [later_offsets, table], [later, later_edges, z],
+        later_kernel, [later_offsets, table], [later, z],
         [((RUNS * SPAN, count, 128), F32)], 2 * 10**9,
     )
     maps = call(

time: 64.9 us -> 69.9 us (1.077)
  waiting for transfers between devices: 14.4 us -> 18.6 us
  blocking collectives: 13.8 us -> 15.9 us
  starting transfers between devices: 22.3 us -> 20.9 us
    ppermute x1, waiting for transfers between devices: 0.01 us -> 4.26 us  [on_device(): edges = lax.ppermute(edge, 'row', [(0, 1), (1, 0)])]
    all_to_all x1, blocking collectives: 13.8 us -> 15.9 us  [on_device(): got = lax.all_to_all(maps, NEAR, 0, 0)]
    ppermute x2 -> x1, starting transfers between devices: 2.5 us -> 1.17 us  [on_device(): lax.ppermute(jnp.concatenate([first_dates(images), first_dates(edges)], a...]
  transfers between devices with their start and end apart: 8 -> 7, of which waited for: 1 -> 2; matrix products, arithmetic and copies ran while one was open for 1% -> 1% of each run, Pallas kernels for 11% -> 9%
where the time goes in v7:
time: 69.9 us; the launch traced here: 69.6 us
  starting transfers between devices  20.9 us (30%)
  waiting for transfers between devices  18.6 us (27%)
  blocking collectives  15.9 us (23%)
  Pallas kernels  11.9 us (17%)
  between operations  1.47 us (2%)
    all_to_all x1, blocking collectives, on_device(): got = lax.all_to_all(maps, NEAR, 0, 0)  15.9 us
    all_to_all x1, waiting for transfers between devices, on_device(): images = lax.all_to_all(packed, NEAR, 0, 0)  14.4 us
    ppermute x4, starting transfers between devices, around(): return lax.ppermute(value, 'z', [(i, (i + by) % size) for i in range(size)])  10.3 us
    pallas_call x6, Pallas kernels, call(): pl.pallas_call(kernel, out_shape=out_shape[0] if single else out_shape, i...  9.29 us
    all_to_all x1, starting transfers between devices, on_device(): images = lax.all_to_all(packed, NEAR, 0, 0)  6.93 us
    ppermute x1, waiting for transfers between devices, on_device(): edges = lax.ppermute(edge, 'row', [(0, 1), (1, 0)])  4.26 us
    pallas_call x1, Pallas kernels, on_device(): pl.pallas_call(pack_kernel, out_shape=jax.ShapeDtypeStruct((slabs, rows,...  2.61 us
    ppermute x1, starting transfers between devices, on_device(): edges = lax.ppermute(edge, 'row', [(0, 1), (1, 0)])  2.54 us
  transfers between devices with their start and end apart: 7, of which 2 were waited for; matrix products, arithmetic and copies ran while one was open for 1% of the time, Pallas kernels for 9%

profile of v7, /device:TPU:1, one launch (start us, length us, event | category | flops | bytes accessed | tf_op | source)
XLA Modules:
  0.0 69.6 jit_solution(15544070278867887285)
XLA Ops:
  0.6 2.6 %shard_map.85 = bf16[16,80,384]{2,1,0:T(8,128)(2,1)} custom-call(s32[1,2]{1,0:T(1,128)} %coarse.1, s32[1,2]{1,0:T(1,128)} %fraction.1, bf16[1,2,80,2560]{3,2,1,0:T(8,128)(2,1)} %x.1), custom_call_target="tpu_custom_call" | custom-call | flops 100000000 | bytes 2000000 | tf_op jit(solution)/shard_map/pallas_call | solution.py:331
  3.3 6.9 %all-to-all-start = ((bf16[16,80,384]{2,1,0:T(8,128)(2,1)}), bf16[16,80,384]{2,1,0:T(8,128)(2,1)S(1)}, u32[]{:S(2)}, u32[]{:S(2)}) async-start(bf16[16,80,384]{2,1,0:T(8,128)(2,1)} %shard_map.85), calls=%async_computation | async-start | bytes 1966080 | tf_op jit(solution)/shard_map/all_to_all | solution.py:348
  10.9 14.4 %all-to-all-done.images = bf16[16,80,384]{2,1,0:T(8,128)(2,1)S(1)} async-done(((bf16[16,80,384]{2,1,0:T(8,128)(2,1)}), bf16[16,80,384]{2,1,0:T(8,128)(2,1)S(1)}, u32[]{:S(2)}, u32[]{:S(2)}) %all-to-all-start) | async-done | bytes 983072 | tf_op jit(solution)/shard_map/all_to_all | solution.py:348
  25.3 0.3 shard_map.86
  25.6 1.7 %collective-permute-start = (bf16[240,128]{1,0:T(8,128)(2,1)S(1)}, bf16[240,128]{1,0:T(8,128)(2,1)S(1)}, u32[]{:S(2)}, u32[]{:S(2)}) collective-permute-start(bf16[240,128]{1,0:T(8,128)(2,1)S(1)} %shard_map.86), channel_id=1, source_target_pairs={{0,16},{16,32},{32,48},{48,64},{64,80},{80,96},{96,112},{112,0},{1... | collective-permute-start | bytes 184328 | tf_op jit(solution)/shard_map/ppermute | solution.py:367
  27.3 4.0 %collective-permute-start.3 = (bf16[240,128]{1,0:T(8,128)(2,1)S(1)}, bf16[240,128]{1,0:T(8,128)(2,1)S(1)}, u32[]{:S(2)}, u32[]{:S(2)}) collective-permute-start(bf16[240,128]{1,0:T(8,128)(2,1)S(1)} %shard_map.86), channel_id=1, source_target_pairs={{0,112},{16,0},{32,16},{48,32},{64,48},{80,64},{96,80},{112,96},{1... | collective-permute-start | bytes 184328 | tf_op jit(solution)/shard_map/ppermute | solution.py:367
  31.3 0.1 slice_convert_fusion
  31.4 0.1 copy.13
  31.5 0.1 copy.14.offsets
  31.6 2.5 %collective-permute-start.1 = (bf16[16,16,384]{2,1,0:T(8,128)(2,1)S(1)}, bf16[16,16,384]{2,1,0:T(8,128)(2,1)S(1)}, u32[]{:S(2)}, u32[]{:S(2)}) collective-permute-start(bf16[16,16,384]{2,1,0:T(8,128)(2,1)S(1)} %slice_select_fusion), channel_id=1, source_target_pairs={{0,1},{1,0},{2,3},{3,2},{4,5},{5,4},{6,7},{7,6},{8,9},{9,8},{10,11... | collective-permute-start | bytes 589832 | tf_op jit(solution)/shard_map/ppermute | solution.py:351
  34.2 4.3 %collective-permute-done.1.edges = bf16[16,16,384]{2,1,0:T(8,128)(2,1)S(1)} collective-permute-done((bf16[16,16,384]{2,1,0:T(8,128)(2,1)S(1)}, bf16[16,16,384]{2,1,0:T(8,128)(2,1)S(1)}, u32[]{:S(2)}, u32[]{:S(2)}) %collective-permute-start.1) | collective-permute-done | bytes 196640 | tf_op jit(solution)/shard_map/ppermute | solution.py:351
  38.5 0.0 copy-start.1
  38.5 1.2 %collective-permute-start.2 = (bf16[6,96,384]{2,1,0:T(8,128)(2,1)S(1)}, bf16[6,96,384]{2,1,0:T(8,128)(2,1)S(1)}, u32[]{:S(2)}, u32[]{:S(2)}) collective-permute-start(bf16[6,96,384]{2,1,0:T(8,128)(2,1)S(1)} %maximum_maximum_fusion), channel_id=1, source_target_pairs={{16,0},{32,16},{48,32},{64,48},{80,64},{96,80},{112,96},{0,112},{1... | collective-permute-start | bytes 1327112 | tf_op jit(solution)/shard_map/ppermute | solution.py:356
  39.7 0.0 copy-done.1
  39.7 3.2 %shard_map.87 = (bf16[16,80,384]{2,1,0:T(8,128)(2,1)S(1)}, bf16[16,80,384]{2,1,0:T(8,128)(2,1)S(1)}, f32[16,16,128]{2,1,0:T(8,128)S(1)}) custom-call(s32[16,4]{1,0:T(8,128)S(1)} %copy.14.offsets, f32[64,8]{1,0:T(8,128)S(1)} %copy-done.1, bf16[16,80,384]{2,1,0:T(8,128)(2,1)S(1)} %all-to-all-done.images, bf16[16,16,384]{2,1,0:T(8,128)(2,1)S(1)} %collective-permute-done.1.edges), custom_call_target="tpu_custom_call" | custom-call | flops 4000000000 | bytes 1179648 | tf_op jit(solution)/shard_map/pallas_call | solution.py:310
  43.0 0.0 collective-permute-done
  43.0 0.0 collective-permute-done.3
  43.0 1.1 %collective-permute-start.4 = (bf16[240,128]{1,0:T(8,128)(2,1)S(1)}, bf16[240,128]{1,0:T(8,128)(2,1)S(1)}, u32[]{:S(2)}, u32[]{:S(2)}) collective-permute-start(bf16[240,128]{1,0:T(8,128)(2,1)S(1)} %select_select_fusion.near), channel_id=1, source_target_pairs={{0,48},{16,64},{32,80},{48,96},{64,112},{80,0},{96,16},{112,32},{1... | collective-permute-start | bytes 184328 | tf_op jit(solution)/shard_map/ppermute | solution.py:367
  44.1 3.4 %collective-permute-start.5 = (bf16[240,128]{1,0:T(8,128)(2,1)S(1)}, bf16[240,128]{1,0:T(8,128)(2,1)S(1)}, u32[]{:S(2)}, u32[]{:S(2)}) collective-permute-start(bf16[240,128]{1,0:T(8,128)(2,1)S(1)} %select_select_fusion.near), channel_id=1, source_target_pairs={{0,80},{16,96},{32,112},{48,0},{64,16},{80,32},{96,48},{112,64},{1... | collective-permute-start | bytes 184328 | tf_op jit(solution)/shard_map/ppermute | solution.py:367
  47.5 1.0 %shard_map.88.part = f32[16,16,128]{2,1,0:T(8,128)S(1)} custom-call(bf16[16,80,384]{2,1,0:T(8,128)(2,1)S(1)} %get-tuple-element.9.z, bf16[16,80,384]{2,1,0:T(8,128)(2,1)S(1)} %get-tuple-element.10.turned, f32[16,16,128]{2,1,0:T(8,128)S(1)} %get-tuple-element.11.powers), custom_call_target="tpu_custom_call" | custom-call | flops 2000000000 | bytes 2097152 | tf_op jit(solution)/shard_map/pallas_call | solution.py:310
  48.6 0.0 collective-permute-done.2.later
  48.6 0.1 slice_convert_fusion.1
  48.7 0.1 copy.15
  48.8 0.1 copy.16.offsets
  48.9 2.3 %shard_map.89.later_part = f32[6,16,128]{2,1,0:T(8,128)S(1)} custom-call(s32[6,4]{1,0:T(8,128)S(1)} %copy.16.offsets, f32[64,8]{1,0:T(8,128)S(1)} %copy-done.1, bf16[6,96,384]{2,1,0:T(8,128)(2,1)S(1)} %collective-permute-done.2.later, bf16[16,80,384]{2,1,0:T(8,128)(2,1)S(1)} %get-tuple-element.9.z), custom_call_target="tpu_custom_call" | custom-call | flops 2000000000 | bytes 1425408 | tf_op jit(solution)/shard_map/pallas_call | solution.py:310
  51.2 0.0 collective-permute-done.4.below
  51.2 0.0 collective-permute-done.5.above
  51.2 0.8 %shard_map.90 = f32[16,16,128]{2,1,0:T(8,128)S(1)} custom-call(s32[1]{0:T(128)} %copy.17.ref, f32[16,16,128]{2,1,0:T(8,128)S(1)} %shard_map.88.part, f32[6,16,128]{2,1,0:T(8,128)S(1)} %shard_map.89.later_part, bf16[16,80,384]{2,1,0:T(8,128)(2,1)S(1)} %get-tuple-element.9.z, bf16[240,128]{1,0:T(8,128)(2,1)S(1)} %select_select_fusion.near, ...), custom_call_target="tpu_custom_call" | custom-call | flops 1000000000 | bytes 1347584 | tf_op jit(solution)/shard_map/pallas_call | solution.py:310
  52.0 0.0 copy-start
  52.1 15.9 %all_to_all.10.got = f32[16,16,128]{2,1,0:T(8,128)S(1)} all-to-all(f32[16,16,128]{2,1,0:T(8,128)S(1)} %shard_map.90), channel_id=1, replica_groups=mesh['xl'=2,'z'=8,'y'=4,'core'=2,'row'=2] {'xl','y','core'}, dimensions={0} | all-to-all | bytes 262144 | tf_op jit(solution)/shard_map/all_to_all | solution.py:391
  68.0 0.0 copy-done
  68.0 1.6 %shard_map.91 = (f32[1,2,16,128]{3,2,1,0:T(8,128)}, f32[1,3,2,16,128]{4,3,2,1,0:T(8,128)}, f32[1,3,16,128]{3,2,1,0:T(8,128)}) custom-call(s32[1,3]{1,0:T(1,128)S(1)} %copy-done, f32[16,16,128]{2,1,0:T(8,128)S(1)} %all_to_all.10.got), custom_call_target="tpu_custom_call" | custom-call | flops 10000000 | bytes 131072 | tf_op jit(solution)/shard_map/pallas_call | solution.py:310
  (6 shorter events, 0.1 us)
Async XLA Ops:
  3.3 22.0 %all-to-all-start = ((bf16[16,80,384]{2,1,0:T(8,128)(2,1)}), bf16[16,80,384]{2,1,0:T(8,128)(2,1)S(1)}, u32[]{:S(2)}, u32[]{:S(2)}) async-start(bf16[16,80,384]{2,1,0:T(8,128)(2,1)} %shard_map.85), calls=%async_computation | async-start | bytes 1966080 | tf_op jit(solution)/shard_map/all_to_all | solution.py:348
  25.6 17.4 %collective-permute-start = (bf16[240,128]{1,0:T(8,128)(2,1)S(1)}, bf16[240,128]{1,0:T(8,128)(2,1)S(1)}, u32[]{:S(2)}, u32[]{:S(2)}) collective-permute-start(bf16[240,128]{1,0:T(8,128)(2,1)S(1)} %shard_map.86), channel_id=1, source_target_pairs={{0,16},{16,32},{32,48},{48,64},{64,80},{80,96},{96,112},{112,0},{1... | collective-permute-start | bytes 184328 | tf_op jit(solution)/shard_map/ppermute | solution.py:367
  27.3 15.7 %collective-permute-start.3 = (bf16[240,128]{1,0:T(8,128)(2,1)S(1)}, bf16[240,128]{1,0:T(8,128)(2,1)S(1)}, u32[]{:S(2)}, u32[]{:S(2)}) collective-permute-start(bf16[240,128]{1,0:T(8,128)(2,1)S(1)} %shard_map.86), channel_id=1, source_target_pairs={{0,112},{16,0},{32,16},{48,32},{64,48},{80,64},{96,80},{112,96},{1... | collective-permute-start | bytes 184328 | tf_op jit(solution)/shard_map/ppermute | solution.py:367
  31.6 6.8 %collective-permute-start.1 = (bf16[16,16,384]{2,1,0:T(8,128)(2,1)S(1)}, bf16[16,16,384]{2,1,0:T(8,128)(2,1)S(1)}, u32[]{:S(2)}, u32[]{:S(2)}) collective-permute-start(bf16[16,16,384]{2,1,0:T(8,128)(2,1)S(1)} %slice_select_fusion), channel_id=1, source_target_pairs={{0,1},{1,0},{2,3},{3,2},{4,5},{5,4},{6,7},{7,6},{8,9},{9,8},{10,11... | collective-permute-start | bytes 589832 | tf_op jit(solution)/shard_map/ppermute | solution.py:351
  38.5 1.2 %copy-start.1 = (f32[64,8]{1,0:T(8,128)S(1)}, f32[64,8]{1,0:T(8,128)}, u32[]{:S(2)}) copy-start(f32[64,8]{1,0:T(8,128)} %constant.61.clone.table) | copy-start | bytes 6148
  38.5 10.0 %collective-permute-start.2 = (bf16[6,96,384]{2,1,0:T(8,128)(2,1)S(1)}, bf16[6,96,384]{2,1,0:T(8,128)(2,1)S(1)}, u32[]{:S(2)}, u32[]{:S(2)}) collective-permute-start(bf16[6,96,384]{2,1,0:T(8,128)(2,1)S(1)} %maximum_maximum_fusion), channel_id=1, source_target_pairs={{16,0},{32,16},{48,32},{64,48},{80,64},{96,80},{112,96},{0,112},{1... | collective-permute-start | bytes 1327112 | tf_op jit(solution)/shard_map/ppermute | solution.py:356
  43.0 8.2 %collective-permute-start.4 = (bf16[240,128]{1,0:T(8,128)(2,1)S(1)}, bf16[240,128]{1,0:T(8,128)(2,1)S(1)}, u32[]{:S(2)}, u32[]{:S(2)}) collective-permute-start(bf16[240,128]{1,0:T(8,128)(2,1)S(1)} %select_select_fusion.near), channel_id=1, source_target_pairs={{0,48},{16,64},{32,80},{48,96},{64,112},{80,0},{96,16},{112,32},{1... | collective-permute-start | bytes 184328 | tf_op jit(solution)/shard_map/ppermute | solution.py:367
  44.1 7.1 %collective-permute-start.5 = (bf16[240,128]{1,0:T(8,128)(2,1)S(1)}, bf16[240,128]{1,0:T(8,128)(2,1)S(1)}, u32[]{:S(2)}, u32[]{:S(2)}) collective-permute-start(bf16[240,128]{1,0:T(8,128)(2,1)S(1)} %select_select_fusion.near), channel_id=1, source_target_pairs={{0,80},{16,96},{32,112},{48,0},{64,16},{80,32},{96,48},{112,64},{1... | collective-permute-start | bytes 184328 | tf_op jit(solution)/shard_map/ppermute | solution.py:367
  52.0 15.9 %copy-start = (s32[1,3]{1,0:T(1,128)S(1)}, s32[1,3]{1,0:T(1,128)}, u32[]{:S(2)}) copy-start(s32[1,3]{1,0:T(1,128)} %on.1) | copy-start | bytes 40

commit v8 on v7

--- a/solution.py
+++ b/solution.py
@@ -218,7 +218,7 @@
         add_pairs(out, start, pairs, looks)
 
 
-def later_kernel(offsets, table, later, z, out):
+def later_kernel(offsets, table, later, edges, z, out):
     rows = z.shape[1]
     members = z.shape[0] // RUNS
     looks = look_matrix()
@@ -228,7 +228,8 @@
     for run in range(RUNS):
         base = jnp.where(last, SPAN * (RUNS - 1), SPAN * run)
         for n in range(SPAN):
-            value = resampled(later[base + n], offsets, base + n, table, rows_apart)
+            image = jnp.concatenate([later[base + n], edges[base + n]], axis=0)
+            value = resampled(image, offsets, base + n, table, rows_apart)
             image = value.astype(BF)
             sums.append(row_sum(image, image))
             found.append((image, crossed(value).astype(BF)))
@@ -353,15 +354,16 @@
     def first_dates(value):
         return jnp.concatenate([value[n : n + SPAN] for n in range(0, slabs, members)], axis=0)
 
-    later = lax.ppermute(
-        jnp.concatenate([first_dates(images), first_dates(edges)], axis=1),
-        "z", [((i + 1) % size, i) for i in range(size)],
+    later = lax.ppermute(first_dates(images), "z", [((i + 1) % size, i) for i in range(size)])
+    later_edges = lax.ppermute(
+        first_dates(edge), ("z", "row"),
+        [((i + 1) % size * 2 + 1 - r, i * 2 + r) for i in range(size) for r in range(2)],
     )
 
     cand = lax.dynamic_index_in_dim(
         images, ref // (members * size) * members + ref % members, 0, keepdims=False
     )
-    q = call(candidate_kernel, [], [cand], [((LANES // 128 * rows, 128), BF)], 10**8)
+    q = call(candidate_kernel, [], [cand], [((LANES // 128 * rows, 128), BF)], 10**10)
 
     def around(value, by):
         return lax.ppermute(value, "z", [(i, (i + by) % size) for i in range(size)])
@@ -381,7 +383,7 @@
     part = call(own_kernel, [], [z, turned, powers], [(sums, F32)], 2 * 10**9)
     later_offsets = later[:, :4, SPARE].astype(jnp.int32)
     later_part = call(
-        later_kernel, [later_offsets, table], [later, z],
+        later_kernel, [later_offsets, table], [later, later_edges, z],
         [((RUNS * SPAN, count, 128), F32)], 2 * 10**9,
     )
     maps = call(

time: 69.9 us -> 63 us (0.901)
  blocking collectives: 15.9 us -> 11.5 us
  waiting for transfers between devices: 18.6 us -> 14.4 us
  starting transfers between devices: 20.9 us -> 22.2 us
    all_to_all x1, blocking collectives: 15.9 us -> 11.5 us  [on_device(): got = lax.all_to_all(maps, NEAR, 0, 0)]
    ppermute x1, waiting for transfers between devices: 4.26 us -> 0.01 us  [on_device(): edges = lax.ppermute(edge, 'row', [(0, 1), (1, 0)])]
    ppermute x1 -> x2, starting transfers between devices: 1.17 us -> 2.49 us  [the longest x1 1.45 us: on_device(): lax.ppermute(first_dates(images), 'z', [((i + 1) % size, i) for i in rang...]
  transfers between devices with their start and end apart: 7 -> 8, of which waited for: 2 -> 1; matrix products, arithmetic and copies ran while one was open for 1% -> 1% of each run, Pallas kernels for 9% -> 11%
where the time goes in v8:
time: 63 us; the launch traced here: 62.2 us
  starting transfers between devices  22.2 us (35%)
  waiting for transfers between devices  14.4 us (23%)
  Pallas kernels  11.9 us (19%)
  blocking collectives  11.5 us (18%)
  between operations  1.48 us (2%)
    all_to_all x1, waiting for transfers between devices, on_device(): images = lax.all_to_all(packed, NEAR, 0, 0)  14.4 us
    all_to_all x1, blocking collectives, on_device(): got = lax.all_to_all(maps, NEAR, 0, 0)  11.5 us
    ppermute x4, starting transfers between devices, around(): return lax.ppermute(value, 'z', [(i, (i + by) % size) for i in range(size)])  10.3 us
    pallas_call x6, Pallas kernels, call(): pl.pallas_call(kernel, out_shape=out_shape[0] if single else out_shape, i...  9.29 us
    all_to_all x1, starting transfers between devices, on_device(): images = lax.all_to_all(packed, NEAR, 0, 0)  6.93 us
    pallas_call x1, Pallas kernels, on_device(): pl.pallas_call(pack_kernel, out_shape=jax.ShapeDtypeStruct((slabs, rows,...  2.61 us
    ppermute x1, starting transfers between devices, on_device(): edges = lax.ppermute(edge, 'row', [(0, 1), (1, 0)])  2.54 us
    ppermute x1, starting transfers between devices, on_device(): lax.ppermute(first_dates(images), 'z', [((i + 1) % size, i) for i in rang...  1.45 us
  transfers between devices with their start and end apart: 8, of which 1 were waited for; matrix products, arithmetic and copies ran while one was open for 1% of the time, Pallas kernels for 11%

profile of v8, /device:TPU:1, one launch (start us, length us, event | category | flops | bytes accessed | tf_op | source)
XLA Modules:
  0.0 62.2 jit_solution(1363897963358203878)
XLA Ops:
  0.6 2.6 %shard_map.85 = bf16[16,80,384]{2,1,0:T(8,128)(2,1)} custom-call(s32[1,2]{1,0:T(1,128)} %coarse.1, s32[1,2]{1,0:T(1,128)} %fraction.1, bf16[1,2,80,2560]{3,2,1,0:T(8,128)(2,1)} %x.1), custom_call_target="tpu_custom_call" | custom-call | flops 100000000 | bytes 2000000 | tf_op jit(solution)/shard_map/pallas_call | solution.py:332
  3.2 6.9 %all-to-all-start = ((bf16[16,80,384]{2,1,0:T(8,128)(2,1)}), bf16[16,80,384]{2,1,0:T(8,128)(2,1)S(1)}, u32[]{:S(2)}, u32[]{:S(2)}) async-start(bf16[16,80,384]{2,1,0:T(8,128)(2,1)} %shard_map.85), calls=%async_computation | async-start | bytes 1966080 | tf_op jit(solution)/shard_map/all_to_all | solution.py:349
  10.9 14.4 %all-to-all-done.images = bf16[16,80,384]{2,1,0:T(8,128)(2,1)S(1)} async-done(((bf16[16,80,384]{2,1,0:T(8,128)(2,1)}), bf16[16,80,384]{2,1,0:T(8,128)(2,1)S(1)}, u32[]{:S(2)}, u32[]{:S(2)}) %all-to-all-start) | async-done | bytes 983072 | tf_op jit(solution)/shard_map/all_to_all | solution.py:349
  25.3 2.5 %collective-permute-start.1 = (bf16[16,16,384]{2,1,0:T(8,128)(2,1)S(1)}, bf16[16,16,384]{2,1,0:T(8,128)(2,1)S(1)}, u32[]{:S(2)}, u32[]{:S(2)}) collective-permute-start(bf16[16,16,384]{2,1,0:T(8,128)(2,1)S(1)} %slice_select_fusion), channel_id=1, source_target_pairs={{0,1},{1,0},{2,3},{3,2},{4,5},{5,4},{6,7},{7,6},{8,9},{9,8},{10,11... | collective-permute-start | bytes 589832 | tf_op jit(solution)/shard_map/ppermute | solution.py:352
  27.9 0.3 shard_map.86
  28.2 1.7 %collective-permute-start = (bf16[240,128]{1,0:T(8,128)(2,1)S(1)}, bf16[240,128]{1,0:T(8,128)(2,1)S(1)}, u32[]{:S(2)}, u32[]{:S(2)}) collective-permute-start(bf16[240,128]{1,0:T(8,128)(2,1)S(1)} %shard_map.86), channel_id=1, source_target_pairs={{0,16},{16,32},{32,48},{48,64},{64,80},{80,96},{96,112},{112,0},{1... | collective-permute-start | bytes 184328 | tf_op jit(solution)/shard_map/ppermute | solution.py:369
  29.9 4.0 %collective-permute-start.4 = (bf16[240,128]{1,0:T(8,128)(2,1)S(1)}, bf16[240,128]{1,0:T(8,128)(2,1)S(1)}, u32[]{:S(2)}, u32[]{:S(2)}) collective-permute-start(bf16[240,128]{1,0:T(8,128)(2,1)S(1)} %shard_map.86), channel_id=1, source_target_pairs={{0,112},{16,0},{32,16},{48,32},{64,48},{80,64},{96,80},{112,96},{1... | collective-permute-start | bytes 184328 | tf_op jit(solution)/shard_map/ppermute | solution.py:369
  33.9 0.1 slice_convert_fusion
  34.0 0.1 copy.13
  34.1 0.1 copy.14.offsets
  34.3 1.5 %collective-permute-start.2 = (bf16[6,80,384]{2,1,0:T(8,128)(2,1)S(1)}, bf16[6,80,384]{2,1,0:T(8,128)(2,1)S(1)}, u32[]{:S(2)}, u32[]{:S(2)}) collective-permute-start(bf16[6,80,384]{2,1,0:T(8,128)(2,1)S(1)} %pad_maximum_fusion), channel_id=1, source_target_pairs={{16,0},{32,16},{48,32},{64,48},{80,64},{96,80},{112,96},{0,112},{1... | collective-permute-start | bytes 1105928 | tf_op jit(solution)/shard_map/ppermute | solution.py:357
  35.7 0.0 copy-start.1
  35.8 1.0 %collective-permute-start.3 = (bf16[6,16,384]{2,1,0:T(8,128)(2,1)S(1)}, bf16[6,16,384]{2,1,0:T(8,128)(2,1)S(1)}, u32[]{:S(2)}, u32[]{:S(2)}) collective-permute-start(bf16[6,16,384]{2,1,0:T(8,128)(2,1)S(1)} %pad_maximum_fusion.1), channel_id=1, source_target_pairs={{17,0},{16,1},{33,16},{32,17},{49,32},{48,33},{65,48},{64,49},{81,... | collective-permute-start | bytes 221192 | tf_op jit(solution)/shard_map/ppermute | solution.py:358
  36.8 0.0 collective-permute-done.1.edges
  36.8 0.0 copy-done.1
  36.8 3.2 %shard_map.87 = (bf16[16,80,384]{2,1,0:T(8,128)(2,1)S(1)}, bf16[16,80,384]{2,1,0:T(8,128)(2,1)S(1)}, f32[16,16,128]{2,1,0:T(8,128)S(1)}) custom-call(s32[16,4]{1,0:T(8,128)S(1)} %copy.14.offsets, f32[64,8]{1,0:T(8,128)S(1)} %copy-done.1, bf16[16,80,384]{2,1,0:T(8,128)(2,1)S(1)} %all-to-all-done.images, bf16[16,16,384]{2,1,0:T(8,128)(2,1)S(1)} %collective-permute-done.1.edges), custom_call_target="tpu_custom_call" | custom-call | flops 4000000000 | bytes 1179648 | tf_op jit(solution)/shard_map/pallas_call | solution.py:311
  40.0 0.0 collective-permute-done
  40.0 0.0 collective-permute-done.4
  40.1 0.1 collective-permute-start.5
  40.2 4.5 %collective-permute-start.6 = (bf16[240,128]{1,0:T(8,128)(2,1)S(1)}, bf16[240,128]{1,0:T(8,128)(2,1)S(1)}, u32[]{:S(2)}, u32[]{:S(2)}) collective-permute-start(bf16[240,128]{1,0:T(8,128)(2,1)S(1)} %select_select_fusion.near), channel_id=1, source_target_pairs={{0,80},{16,96},{32,112},{48,0},{64,16},{80,32},{96,48},{112,64},{1... | collective-permute-start | bytes 184328 | tf_op jit(solution)/shard_map/ppermute | solution.py:369
  44.6 1.0 %shard_map.88.part = f32[16,16,128]{2,1,0:T(8,128)S(1)} custom-call(bf16[16,80,384]{2,1,0:T(8,128)(2,1)S(1)} %get-tuple-element.9.z, bf16[16,80,384]{2,1,0:T(8,128)(2,1)S(1)} %get-tuple-element.10.turned, f32[16,16,128]{2,1,0:T(8,128)S(1)} %get-tuple-element.11.powers), custom_call_target="tpu_custom_call" | custom-call | flops 2000000000 | bytes 2097152 | tf_op jit(solution)/shard_map/pallas_call | solution.py:311
  45.7 0.0 collective-permute-done.2.later
  45.7 0.1 slice_convert_fusion.1
  45.8 0.1 copy.15
  45.9 0.1 copy.16.offsets
  46.0 0.0 collective-permute-done.3.edges
  46.0 2.3 %shard_map.89.later_part = f32[6,16,128]{2,1,0:T(8,128)S(1)} custom-call(s32[6,4]{1,0:T(8,128)S(1)} %copy.16.offsets, f32[64,8]{1,0:T(8,128)S(1)} %copy-done.1, bf16[6,80,384]{2,1,0:T(8,128)(2,1)S(1)} %collective-permute-done.2.later, bf16[6,16,384]{2,1,0:T(8,128)(2,1)S(1)} %collective-permute-done.3.edges, bf16[16,80,384]{2,1,0:T(8,128)(2,1)S(1)} %get-tuple-element.9.z), custom_call_target="tpu_custom_call" | custom-call | flops 2000000000 | bytes 1425408 | tf_op jit(solution)/shard_map/pallas_call | solution.py:311
  48.3 0.0 collective-permute-done.5.below
  48.3 0.0 collective-permute-done.6.above
  48.3 0.8 %shard_map.90 = f32[16,16,128]{2,1,0:T(8,128)S(1)} custom-call(s32[1]{0:T(128)} %copy.17.ref, f32[16,16,128]{2,1,0:T(8,128)S(1)} %shard_map.88.part, f32[6,16,128]{2,1,0:T(8,128)S(1)} %shard_map.89.later_part, bf16[16,80,384]{2,1,0:T(8,128)(2,1)S(1)} %get-tuple-element.9.z, bf16[240,128]{1,0:T(8,128)(2,1)S(1)} %select_select_fusion.near, ...), custom_call_target="tpu_custom_call" | custom-call | flops 1000000000 | bytes 1347584 | tf_op jit(solution)/shard_map/pallas_call | solution.py:311
  49.1 0.0 copy-start
  49.1 11.5 %all_to_all.10.got = f32[16,16,128]{2,1,0:T(8,128)S(1)} all-to-all(f32[16,16,128]{2,1,0:T(8,128)S(1)} %shard_map.90), channel_id=1, replica_groups=mesh['xl'=2,'z'=8,'y'=4,'core'=2,'row'=2] {'xl','y','core'}, dimensions={0} | all-to-all | bytes 262144 | tf_op jit(solution)/shard_map/all_to_all | solution.py:393
  60.6 0.0 copy-done
  60.6 1.6 %shard_map.91 = (f32[1,2,16,128]{3,2,1,0:T(8,128)}, f32[1,3,2,16,128]{4,3,2,1,0:T(8,128)}, f32[1,3,16,128]{3,2,1,0:T(8,128)}) custom-call(s32[1,3]{1,0:T(1,128)S(1)} %copy-done, f32[16,16,128]{2,1,0:T(8,128)S(1)} %all_to_all.10.got), custom_call_target="tpu_custom_call" | custom-call | flops 10000000 | bytes 131072 | tf_op jit(solution)/shard_map/pallas_call | solution.py:311
  (7 shorter events, 0.2 us)
Async XLA Ops:
  3.2 22.0 %all-to-all-start = ((bf16[16,80,384]{2,1,0:T(8,128)(2,1)}), bf16[16,80,384]{2,1,0:T(8,128)(2,1)S(1)}, u32[]{:S(2)}, u32[]{:S(2)}) async-start(bf16[16,80,384]{2,1,0:T(8,128)(2,1)} %shard_map.85), calls=%async_computation | async-start | bytes 1966080 | tf_op jit(solution)/shard_map/all_to_all | solution.py:349
  25.3 11.5 %collective-permute-start.1 = (bf16[16,16,384]{2,1,0:T(8,128)(2,1)S(1)}, bf16[16,16,384]{2,1,0:T(8,128)(2,1)S(1)}, u32[]{:S(2)}, u32[]{:S(2)}) collective-permute-start(bf16[16,16,384]{2,1,0:T(8,128)(2,1)S(1)} %slice_select_fusion), channel_id=1, source_target_pairs={{0,1},{1,0},{2,3},{3,2},{4,5},{5,4},{6,7},{7,6},{8,9},{9,8},{10,11... | collective-permute-start | bytes 589832 | tf_op jit(solution)/shard_map/ppermute | solution.py:352
  28.2 11.9 %collective-permute-start = (bf16[240,128]{1,0:T(8,128)(2,1)S(1)}, bf16[240,128]{1,0:T(8,128)(2,1)S(1)}, u32[]{:S(2)}, u32[]{:S(2)}) collective-permute-start(bf16[240,128]{1,0:T(8,128)(2,1)S(1)} %shard_map.86), channel_id=1, source_target_pairs={{0,16},{16,32},{32,48},{48,64},{64,80},{80,96},{96,112},{112,0},{1... | collective-permute-start | bytes 184328 | tf_op jit(solution)/shard_map/ppermute | solution.py:369
  29.9 10.2 %collective-permute-start.4 = (bf16[240,128]{1,0:T(8,128)(2,1)S(1)}, bf16[240,128]{1,0:T(8,128)(2,1)S(1)}, u32[]{:S(2)}, u32[]{:S(2)}) collective-permute-start(bf16[240,128]{1,0:T(8,128)(2,1)S(1)} %shard_map.86), channel_id=1, source_target_pairs={{0,112},{16,0},{32,16},{48,32},{64,48},{80,64},{96,80},{112,96},{1... | collective-permute-start | bytes 184328 | tf_op jit(solution)/shard_map/ppermute | solution.py:369
  34.3 11.4 %collective-permute-start.2 = (bf16[6,80,384]{2,1,0:T(8,128)(2,1)S(1)}, bf16[6,80,384]{2,1,0:T(8,128)(2,1)S(1)}, u32[]{:S(2)}, u32[]{:S(2)}) collective-permute-start(bf16[6,80,384]{2,1,0:T(8,128)(2,1)S(1)} %pad_maximum_fusion), channel_id=1, source_target_pairs={{16,0},{32,16},{48,32},{64,48},{80,64},{96,80},{112,96},{0,112},{1... | collective-permute-start | bytes 1105928 | tf_op jit(solution)/shard_map/ppermute | solution.py:357
  35.7 1.1 %copy-start.1 = (f32[64,8]{1,0:T(8,128)S(1)}, f32[64,8]{1,0:T(8,128)}, u32[]{:S(2)}) copy-start(f32[64,8]{1,0:T(8,128)} %constant.61.clone.table) | copy-start | bytes 6148
  35.8 10.2 %collective-permute-start.3 = (bf16[6,16,384]{2,1,0:T(8,128)(2,1)S(1)}, bf16[6,16,384]{2,1,0:T(8,128)(2,1)S(1)}, u32[]{:S(2)}, u32[]{:S(2)}) collective-permute-start(bf16[6,16,384]{2,1,0:T(8,128)(2,1)S(1)} %pad_maximum_fusion.1), channel_id=1, source_target_pairs={{17,0},{16,1},{33,16},{32,17},{49,32},{48,33},{65,48},{64,49},{81,... | collective-permute-start | bytes 221192 | tf_op jit(solution)/shard_map/ppermute | solution.py:358
  40.1 8.2 %collective-permute-start.5 = (bf16[240,128]{1,0:T(8,128)(2,1)S(1)}, bf16[240,128]{1,0:T(8,128)(2,1)S(1)}, u32[]{:S(2)}, u32[]{:S(2)}) collective-permute-start(bf16[240,128]{1,0:T(8,128)(2,1)S(1)} %select_select_fusion.near), channel_id=1, source_target_pairs={{0,48},{16,64},{32,80},{48,96},{64,112},{80,0},{96,16},{112,32},{1... | collective-permute-start | bytes 184328 | tf_op jit(solution)/shard_map/ppermute | solution.py:369
  40.2 8.2 %collective-permute-start.6 = (bf16[240,128]{1,0:T(8,128)(2,1)S(1)}, bf16[240,128]{1,0:T(8,128)(2,1)S(1)}, u32[]{:S(2)}, u32[]{:S(2)}) collective-permute-start(bf16[240,128]{1,0:T(8,128)(2,1)S(1)} %select_select_fusion.near), channel_id=1, source_target_pairs={{0,80},{16,96},{32,112},{48,0},{64,16},{80,32},{96,48},{112,64},{1... | collective-permute-start | bytes 184328 | tf_op jit(solution)/shard_map/ppermute | solution.py:369
  49.1 11.5 %copy-start = (s32[1,3]{1,0:T(1,128)S(1)}, s32[1,3]{1,0:T(1,128)}, u32[]{:S(2)}) copy-start(s32[1,3]{1,0:T(1,128)} %on.1) | copy-start | bytes 40

commit v9 on v8

--- a/solution.py
+++ b/solution.py
@@ -60,7 +60,7 @@
 def placed(distance, shift, table, index):
     total = jnp.zeros(distance.shape, F32)
     for k in range(8):
-        total = jnp.where(distance == shift + k, table[index, k], total)
+        total = jnp.where(distance == shift + k, table[8 * index + k], total)
     return total
 
 
@@ -138,7 +138,7 @@
         copy.wait()
     own = jnp.where(row == 0, shifts[0, 0], jnp.where(row == 1, shifts[0, 1], 0))
     own = jnp.where(row == 2, taps[0, 0], jnp.where(row == 3, taps[0, 1], own))
-    own = own.astype(F32)
+    own = own.astype(F32).astype(BF)
     here = 0
     outgoing = []
     for j in range(out.shape[0]):
@@ -148,10 +148,10 @@
             incoming[2 * here].wait()
             incoming[2 * here + 1].wait()
             here += 1
-        first = pltpu.roll(wide[0, :, base : base + LANES].astype(F32), (LANES - off) % LANES, 1)
-        second = pltpu.roll(wide[1, :, base : base + LANES].astype(F32), WIN - off, 1)
+        first = pltpu.roll(wide[0, :, base : base + LANES], (LANES - off) % LANES, 1)
+        second = pltpu.roll(wide[1, :, base : base + LANES], WIN - off, 1)
         value = jnp.where(lane < WIN, first, second)
-        packed[j] = jnp.where(lane == SPARE, own, value).astype(BF)
+        packed[j] = jnp.where(lane == SPARE, own, value)
         outgoing.append(pltpu.make_async_copy(packed.at[j], out.at[j], out_sem.at[j]))
         outgoing[-1].start()
     for copy in outgoing:
@@ -276,16 +276,24 @@
 
 
 def finish_kernel(on, got, ref_ifg, pair_ifg, coherence):
-    slabs, count, _ = got.shape
+    slabs, count, lanes = got.shape
     date, dates = lax.axis_index(DATE), lax.axis_size(DATE)
-    slab = iota((count, 128), 1) // SLOT
+    slab = iota((count, lanes), 1) // SLOT
+    maps = [got[j] for j in range(slabs)]
+    step = 1
+    while step < slabs:
+        low = slab // step % 2 == 0
+        moved = []
+        for j in range(slabs):
+            if j // step % 2 == 0:
+                moved.append(jnp.where(low, maps[j], pltpu.roll(maps[j + step], SLOT * step, 1)))
+            else:
+                moved.append(jnp.where(low, pltpu.roll(maps[j - step], lanes - SLOT * step, 1), maps[j]))
+        maps = moved
+        step *= 2
 
     def gathered(m):
-        total = jnp.zeros((count, 128), F32)
-        for j in range(slabs):
-            moved = pltpu.roll(got[j], SLOT * ((j - m) % slabs), 1)
-            total = jnp.where(slab == j, moved, total)
-        return total * (1.0 / (LOOK_R * LOOK_C))
+        return maps[m] * (1.0 / (LOOK_R * LOOK_C))
 
     ref_ifg[0, 0] = gathered(0)
     ref_ifg[0, 1] = gathered(1)
@@ -422,7 +430,7 @@
                     P(DATE, None, "row", None),
                 ),
                 check_vma=False,
-            )(jnp.asarray(table), slc, coarse, fraction, pair_on, ref_date)
+            )(jnp.asarray(table.reshape(-1)), slc, coarse, fraction, pair_on, ref_date)
         )
 
     return program

time: 63 us -> 62.8 us (level)
  Pallas kernels: 11.9 us -> 10.7 us
    pallas_call x6, Pallas kernels: 9.29 us -> 8.14 us  [call(): pl.pallas_call(kernel, out_shape=out_shape[0] if single else out_shape, i...]
  transfers between devices with their start and end apart: 8 -> 8, of which waited for: 1 -> 1; matrix products, arithmetic and copies ran while one was open for 1% -> 1% of each run, Pallas kernels for 11% -> 10%
where the time goes in v9:
time: 62.8 us; the launch traced here: 61.7 us
  starting transfers between devices  22.3 us (36%)
  waiting for transfers between devices  14.4 us (23%)
  blocking collectives  12.1 us (19%)
  Pallas kernels  10.7 us (17%)
  between operations  1.48 us (2%)
    all_to_all x1, waiting for transfers between devices, on_device(): images = lax.all_to_all(packed, NEAR, 0, 0)  14.4 us
    all_to_all x1, blocking collectives, on_device(): got = lax.all_to_all(maps, NEAR, 0, 0)  12.1 us
    ppermute x4, starting transfers between devices, around(): return lax.ppermute(value, 'z', [(i, (i + by) % size) for i in range(size)])  10.3 us
    pallas_call x6, Pallas kernels, call(): pl.pallas_call(kernel, out_shape=out_shape[0] if single else out_shape, i...  8.14 us
    all_to_all x1, starting transfers between devices, on_device(): images = lax.all_to_all(packed, NEAR, 0, 0)  6.93 us
    pallas_call x1, Pallas kernels, on_device(): pl.pallas_call(pack_kernel, out_shape=jax.ShapeDtypeStruct((slabs, rows,...  2.59 us
    ppermute x1, starting transfers between devices, on_device(): edges = lax.ppermute(edge, 'row', [(0, 1), (1, 0)])  2.54 us
    ppermute x1, starting transfers between devices, on_device(): lax.ppermute(first_dates(images), 'z', [((i + 1) % size, i) for i in rang...  1.45 us
  transfers between devices with their start and end apart: 8, of which 1 were waited for; matrix products, arithmetic and copies ran while one was open for 1% of the time, Pallas kernels for 10%

profile of v9, /device:TPU:1, one launch (start us, length us, event | category | flops | bytes accessed | tf_op | source)
XLA Modules:
  0.0 61.7 jit_solution(161767248105321773)
XLA Ops:
  0.6 2.6 %shard_map.85 = bf16[16,80,384]{2,1,0:T(8,128)(2,1)} custom-call(s32[1,2]{1,0:T(1,128)} %coarse.1, s32[1,2]{1,0:T(1,128)} %fraction.1, bf16[1,2,80,2560]{3,2,1,0:T(8,128)(2,1)} %x.1), custom_call_target="tpu_custom_call" | custom-call | flops 100000000 | bytes 2000000 | tf_op jit(solution)/shard_map/pallas_call | solution.py:340
  3.2 6.9 %all-to-all-start = ((bf16[16,80,384]{2,1,0:T(8,128)(2,1)}), bf16[16,80,384]{2,1,0:T(8,128)(2,1)S(1)}, u32[]{:S(2)}, u32[]{:S(2)}) async-start(bf16[16,80,384]{2,1,0:T(8,128)(2,1)} %shard_map.85), calls=%async_computation | async-start | bytes 1966080 | tf_op jit(solution)/shard_map/all_to_all | solution.py:357
  10.9 14.4 %all-to-all-done.images = bf16[16,80,384]{2,1,0:T(8,128)(2,1)S(1)} async-done(((bf16[16,80,384]{2,1,0:T(8,128)(2,1)}), bf16[16,80,384]{2,1,0:T(8,128)(2,1)S(1)}, u32[]{:S(2)}, u32[]{:S(2)}) %all-to-all-start) | async-done | bytes 983072 | tf_op jit(solution)/shard_map/all_to_all | solution.py:357
  25.3 2.5 %collective-permute-start.1 = (bf16[16,16,384]{2,1,0:T(8,128)(2,1)S(1)}, bf16[16,16,384]{2,1,0:T(8,128)(2,1)S(1)}, u32[]{:S(2)}, u32[]{:S(2)}) collective-permute-start(bf16[16,16,384]{2,1,0:T(8,128)(2,1)S(1)} %slice_select_fusion), channel_id=1, source_target_pairs={{0,1},{1,0},{2,3},{3,2},{4,5},{5,4},{6,7},{7,6},{8,9},{9,8},{10,11... | collective-permute-start | bytes 589832 | tf_op jit(solution)/shard_map/ppermute | solution.py:360
  27.9 0.3 shard_map.86
  28.1 1.7 %collective-permute-start = (bf16[240,128]{1,0:T(8,128)(2,1)S(1)}, bf16[240,128]{1,0:T(8,128)(2,1)S(1)}, u32[]{:S(2)}, u32[]{:S(2)}) collective-permute-start(bf16[240,128]{1,0:T(8,128)(2,1)S(1)} %shard_map.86), channel_id=1, source_target_pairs={{0,16},{16,32},{32,48},{48,64},{64,80},{80,96},{96,112},{112,0},{1... | collective-permute-start | bytes 184328 | tf_op jit(solution)/shard_map/ppermute | solution.py:377
  29.9 4.0 %collective-permute-start.4 = (bf16[240,128]{1,0:T(8,128)(2,1)S(1)}, bf16[240,128]{1,0:T(8,128)(2,1)S(1)}, u32[]{:S(2)}, u32[]{:S(2)}) collective-permute-start(bf16[240,128]{1,0:T(8,128)(2,1)S(1)} %shard_map.86), channel_id=1, source_target_pairs={{0,112},{16,0},{32,16},{48,32},{64,48},{80,64},{96,80},{112,96},{1... | collective-permute-start | bytes 184328 | tf_op jit(solution)/shard_map/ppermute | solution.py:377
  33.9 0.1 slice_convert_fusion
  34.0 0.1 copy.13
  34.1 0.1 copy.14.offsets
  34.3 1.5 %collective-permute-start.2 = (bf16[6,80,384]{2,1,0:T(8,128)(2,1)S(1)}, bf16[6,80,384]{2,1,0:T(8,128)(2,1)S(1)}, u32[]{:S(2)}, u32[]{:S(2)}) collective-permute-start(bf16[6,80,384]{2,1,0:T(8,128)(2,1)S(1)} %pad_maximum_fusion), channel_id=1, source_target_pairs={{16,0},{32,16},{48,32},{64,48},{80,64},{96,80},{112,96},{0,112},{1... | collective-permute-start | bytes 1105928 | tf_op jit(solution)/shard_map/ppermute | solution.py:365
  35.7 0.0 copy-start.1
  35.7 1.0 %collective-permute-start.3 = (bf16[6,16,384]{2,1,0:T(8,128)(2,1)S(1)}, bf16[6,16,384]{2,1,0:T(8,128)(2,1)S(1)}, u32[]{:S(2)}, u32[]{:S(2)}) collective-permute-start(bf16[6,16,384]{2,1,0:T(8,128)(2,1)S(1)} %pad_maximum_fusion.1), channel_id=1, source_target_pairs={{17,0},{16,1},{33,16},{32,17},{49,32},{48,33},{65,48},{64,49},{81,... | collective-permute-start | bytes 221192 | tf_op jit(solution)/shard_map/ppermute | solution.py:366
  36.8 0.0 collective-permute-done.1.edges
  36.8 0.0 copy-done.1
  36.8 2.7 %shard_map.87 = (bf16[16,80,384]{2,1,0:T(8,128)(2,1)S(1)}, bf16[16,80,384]{2,1,0:T(8,128)(2,1)S(1)}, f32[16,16,128]{2,1,0:T(8,128)S(1)}) custom-call(s32[16,4]{1,0:T(8,128)S(1)} %copy.14.offsets, f32[512]{0:T(512)S(1)} %copy-done.1, bf16[16,80,384]{2,1,0:T(8,128)(2,1)S(1)} %all-to-all-done.images, bf16[16,16,384]{2,1,0:T(8,128)(2,1)S(1)} %collective-permute-done.1.edges), custom_call_target="tpu_custom_call" | custom-call | flops 4000000000 | bytes 1179648 | tf_op jit(solution)/shard_map/pallas_call | solution.py:319
  39.5 0.0 collective-permute-done
  39.5 0.0 collective-permute-done.4
  39.6 0.2 collective-permute-start.5
  39.8 4.3 %collective-permute-start.6 = (bf16[240,128]{1,0:T(8,128)(2,1)S(1)}, bf16[240,128]{1,0:T(8,128)(2,1)S(1)}, u32[]{:S(2)}, u32[]{:S(2)}) collective-permute-start(bf16[240,128]{1,0:T(8,128)(2,1)S(1)} %select_select_fusion.near), channel_id=1, source_target_pairs={{0,80},{16,96},{32,112},{48,0},{64,16},{80,32},{96,48},{112,64},{1... | collective-permute-start | bytes 184328 | tf_op jit(solution)/shard_map/ppermute | solution.py:377
  44.1 1.0 %shard_map.88.part = f32[16,16,128]{2,1,0:T(8,128)S(1)} custom-call(bf16[16,80,384]{2,1,0:T(8,128)(2,1)S(1)} %get-tuple-element.9.z, bf16[16,80,384]{2,1,0:T(8,128)(2,1)S(1)} %get-tuple-element.10.turned, f32[16,16,128]{2,1,0:T(8,128)S(1)} %get-tuple-element.11.powers), custom_call_target="tpu_custom_call" | custom-call | flops 2000000000 | bytes 2097152 | tf_op jit(solution)/shard_map/pallas_call | solution.py:319
  45.1 0.0 collective-permute-done.2.later
  45.1 0.1 slice_convert_fusion.1
  45.2 0.1 copy.15
  45.3 0.1 copy.16.offsets
  45.4 0.0 collective-permute-done.3.edges
  45.4 1.8 %shard_map.89.later_part = f32[6,16,128]{2,1,0:T(8,128)S(1)} custom-call(s32[6,4]{1,0:T(8,128)S(1)} %copy.16.offsets, f32[512]{0:T(512)S(1)} %copy-done.1, bf16[6,80,384]{2,1,0:T(8,128)(2,1)S(1)} %collective-permute-done.2.later, bf16[6,16,384]{2,1,0:T(8,128)(2,1)S(1)} %collective-permute-done.3.edges, bf16[16,80,384]{2,1,0:T(8,128)(2,1)S(1)} %get-tuple-element.9.z), custom_call_target="tpu_custom_call" | custom-call | flops 2000000000 | bytes 1425408 | tf_op jit(solution)/shard_map/pallas_call | solution.py:319
  47.3 0.0 collective-permute-done.5.below
  47.3 0.0 collective-permute-done.6.above
  47.3 0.8 %shard_map.90 = f32[16,16,128]{2,1,0:T(8,128)S(1)} custom-call(s32[1]{0:T(128)} %copy.17.ref, f32[16,16,128]{2,1,0:T(8,128)S(1)} %shard_map.88.part, f32[6,16,128]{2,1,0:T(8,128)S(1)} %shard_map.89.later_part, bf16[16,80,384]{2,1,0:T(8,128)(2,1)S(1)} %get-tuple-element.9.z, bf16[240,128]{1,0:T(8,128)(2,1)S(1)} %select_select_fusion.near, ...), custom_call_target="tpu_custom_call" | custom-call | flops 1000000000 | bytes 1347584 | tf_op jit(solution)/shard_map/pallas_call | solution.py:319
  48.1 0.0 copy-start
  48.1 12.1 %all_to_all.10.got = f32[16,16,128]{2,1,0:T(8,128)S(1)} all-to-all(f32[16,16,128]{2,1,0:T(8,128)S(1)} %shard_map.90), channel_id=1, replica_groups=mesh['xl'=2,'z'=8,'y'=4,'core'=2,'row'=2] {'xl','y','core'}, dimensions={0} | all-to-all | bytes 262144 | tf_op jit(solution)/shard_map/all_to_all | solution.py:401
  60.2 0.0 copy-done
  60.2 1.5 %shard_map.91 = (f32[1,2,16,128]{3,2,1,0:T(8,128)}, f32[1,3,2,16,128]{4,3,2,1,0:T(8,128)}, f32[1,3,16,128]{3,2,1,0:T(8,128)}) custom-call(s32[1,3]{1,0:T(1,128)S(1)} %copy-done, f32[16,16,128]{2,1,0:T(8,128)S(1)} %all_to_all.10.got), custom_call_target="tpu_custom_call" | custom-call | flops 10000000 | bytes 131072 | tf_op jit(solution)/shard_map/pallas_call | solution.py:319
  (7 shorter events, 0.2 us)
Async XLA Ops:
  3.2 22.0 %all-to-all-start = ((bf16[16,80,384]{2,1,0:T(8,128)(2,1)}), bf16[16,80,384]{2,1,0:T(8,128)(2,1)S(1)}, u32[]{:S(2)}, u32[]{:S(2)}) async-start(bf16[16,80,384]{2,1,0:T(8,128)(2,1)} %shard_map.85), calls=%async_computation | async-start | bytes 1966080 | tf_op jit(solution)/shard_map/all_to_all | solution.py:357
  25.3 11.5 %collective-permute-start.1 = (bf16[16,16,384]{2,1,0:T(8,128)(2,1)S(1)}, bf16[16,16,384]{2,1,0:T(8,128)(2,1)S(1)}, u32[]{:S(2)}, u32[]{:S(2)}) collective-permute-start(bf16[16,16,384]{2,1,0:T(8,128)(2,1)S(1)} %slice_select_fusion), channel_id=1, source_target_pairs={{0,1},{1,0},{2,3},{3,2},{4,5},{5,4},{6,7},{7,6},{8,9},{9,8},{10,11... | collective-permute-start | bytes 589832 | tf_op jit(solution)/shard_map/ppermute | solution.py:360
  28.1 11.4 %collective-permute-start = (bf16[240,128]{1,0:T(8,128)(2,1)S(1)}, bf16[240,128]{1,0:T(8,128)(2,1)S(1)}, u32[]{:S(2)}, u32[]{:S(2)}) collective-permute-start(bf16[240,128]{1,0:T(8,128)(2,1)S(1)} %shard_map.86), channel_id=1, source_target_pairs={{0,16},{16,32},{32,48},{48,64},{64,80},{80,96},{96,112},{112,0},{1... | collective-permute-start | bytes 184328 | tf_op jit(solution)/shard_map/ppermute | solution.py:377
  29.9 9.7 %collective-permute-start.4 = (bf16[240,128]{1,0:T(8,128)(2,1)S(1)}, bf16[240,128]{1,0:T(8,128)(2,1)S(1)}, u32[]{:S(2)}, u32[]{:S(2)}) collective-permute-start(bf16[240,128]{1,0:T(8,128)(2,1)S(1)} %shard_map.86), channel_id=1, source_target_pairs={{0,112},{16,0},{32,16},{48,32},{64,48},{80,64},{96,80},{112,96},{1... | collective-permute-start | bytes 184328 | tf_op jit(solution)/shard_map/ppermute | solution.py:377
  34.3 10.9 %collective-permute-start.2 = (bf16[6,80,384]{2,1,0:T(8,128)(2,1)S(1)}, bf16[6,80,384]{2,1,0:T(8,128)(2,1)S(1)}, u32[]{:S(2)}, u32[]{:S(2)}) collective-permute-start(bf16[6,80,384]{2,1,0:T(8,128)(2,1)S(1)} %pad_maximum_fusion), channel_id=1, source_target_pairs={{16,0},{32,16},{48,32},{64,48},{80,64},{96,80},{112,96},{0,112},{1... | collective-permute-start | bytes 1105928 | tf_op jit(solution)/shard_map/ppermute | solution.py:365
  35.7 1.1 %copy-start.1 = (f32[512]{0:T(512)S(1)}, f32[512]{0:T(512)}, u32[]{:S(2)}) copy-start(f32[512]{0:T(512)} %constant.61.clone.table) | copy-start | bytes 6148
  35.7 9.7 %collective-permute-start.3 = (bf16[6,16,384]{2,1,0:T(8,128)(2,1)S(1)}, bf16[6,16,384]{2,1,0:T(8,128)(2,1)S(1)}, u32[]{:S(2)}, u32[]{:S(2)}) collective-permute-start(bf16[6,16,384]{2,1,0:T(8,128)(2,1)S(1)} %pad_maximum_fusion.1), channel_id=1, source_target_pairs={{17,0},{16,1},{33,16},{32,17},{49,32},{48,33},{65,48},{64,49},{81,... | collective-permute-start | bytes 221192 | tf_op jit(solution)/shard_map/ppermute | solution.py:366
  39.6 7.7 %collective-permute-start.5 = (bf16[240,128]{1,0:T(8,128)(2,1)S(1)}, bf16[240,128]{1,0:T(8,128)(2,1)S(1)}, u32[]{:S(2)}, u32[]{:S(2)}) collective-permute-start(bf16[240,128]{1,0:T(8,128)(2,1)S(1)} %select_select_fusion.near), channel_id=1, source_target_pairs={{0,48},{16,64},{32,80},{48,96},{64,112},{80,0},{96,16},{112,32},{1... | collective-permute-start | bytes 184328 | tf_op jit(solution)/shard_map/ppermute | solution.py:377
  39.8 7.5 %collective-permute-start.6 = (bf16[240,128]{1,0:T(8,128)(2,1)S(1)}, bf16[240,128]{1,0:T(8,128)(2,1)S(1)}, u32[]{:S(2)}, u32[]{:S(2)}) collective-permute-start(bf16[240,128]{1,0:T(8,128)(2,1)S(1)} %select_select_fusion.near), channel_id=1, source_target_pairs={{0,80},{16,96},{32,112},{48,0},{64,16},{80,32},{96,48},{112,64},{1... | collective-permute-start | bytes 184328 | tf_op jit(solution)/shard_map/ppermute | solution.py:377
  48.1 12.1 %copy-start = (s32[1,3]{1,0:T(1,128)S(1)}, s32[1,3]{1,0:T(1,128)}, u32[]{:S(2)}) copy-start(s32[1,3]{1,0:T(1,128)} %on.1) | copy-start | bytes 40
